TPU v7x, 512 devices: a whole 4x4x16 slice. The times are simulated.
512 devices in a mesh: wide: 128 (over z, x, y_lo), narrow: 4 (over y_hi, core).
Axes of the slice: x: 4, y: 4 (y_hi: 2, y_lo: 2; y = y_hi * 2 + y_lo), z: 16, core: 2. Of those that a mesh axis runs over, the one named last changes fastest.
Arguments:
- rhs: float32 [64, 1024, 1024], P(None, 'wide', 'narrow'), may hold values from -6 to 6
- areas: float32 [1024, 1024], P('wide', 'narrow'), may hold values from 0.5 to 2
- stiffness: float32 [64], replicated, may hold values from 1e-07 to 1
Outputs:
- pressure: float32 [64, 1024, 1024], P(None, 'wide', 'narrow')
- residual: float32 [64, 1024, 1024], P(None, 'wide', 'narrow')
All inputs are finite; a program needn't handle non-finite values.
Results may differ from a plain program's by a relative error of at most 0.0003.
Values sent between devices are 32-bit elements; how exact they have to be, the bound alone decides.
No kernel may reach another device: no remote copies, remote signals or barrier semaphores. Data moves between devices by JAX's collectives and lax.ppermute only.
A program may use at most 64 MiB of HBM per device.

v0:
```python
import jax
import jax.numpy as jnp
from jax import lax
from jax.sharding import PartitionSpec as P

coupling = 2.0
relaxation = 0.4


def extended(cells, sides, width):
    for axis, dim in sides:
        count = lax.axis_size(axis)
        ends = count - 1
        head = lax.slice_in_dim(cells, 0, width, axis=dim)
        tail = lax.slice_in_dim(cells, cells.shape[dim] - width, cells.shape[dim], axis=dim)
        cells = jnp.concatenate(
            [
                lax.ppermute(tail, axis, [(i, (i + 1) % count) for i in range(ends)]),
                cells,
                lax.ppermute(head, axis, [((i + 1) % count, i) for i in range(ends)]),
            ],
            axis=dim,
        )
    return cells


def entering_2(array, axis, combine, identity, reverse):
    peers, here = (lax.axis_size(axis), lax.axis_index(axis))
    everything = jax.tree.map(lambda part: lax.all_gather(part, axis), array)
    start = jax.tree.map(
        lambda part, zero: jnp.broadcast_to(jnp.asarray(zero, part.dtype), part.shape),
        array,
        identity,
    )

    def turn(k, before):
        at = peers - 1 - k if reverse else k
        reached = at > here if reverse else at < here
        new = combine(before, jax.tree.map(lambda part: part[at], everything))
        return jax.tree.map(lambda a, b: jnp.where(reached, a, b), new, before)

    return lax.fori_loop(0, peers, turn, start)


def column_inverse(stiffness):
    levels = stiffness.shape[0]
    identity_k = jnp.eye(levels, dtype=stiffness.dtype)
    neighbours = jnp.eye(levels, k=1, dtype=stiffness.dtype) + jnp.eye(
        levels, k=-1, dtype=stiffness.dtype
    )
    matrix = jnp.diag(stiffness + 2.0 * coupling + 4.0) - coupling * neighbours
    lower = jnp.linalg.cholesky(matrix)
    lower_inv = lax.linalg.triangular_solve(lower, identity_k, left_side=True, lower=True)
    return jnp.dot(lower_inv.T, lower_inv, precision=lax.Precision.HIGHEST)


def apply_columns(inverse, field):
    return jnp.einsum("kl,lxy->kxy", inverse, field, precision=lax.Precision.HIGHEST)


def vertical(field, stiffness):
    empty = jnp.zeros_like(field[:1])
    above = jnp.concatenate([field[1:], empty], axis=0)
    below = jnp.concatenate([empty, field[:-1]], axis=0)
    return stiffness[:, None, None] * field + coupling * (2.0 * field - above - below)


def operate(padded, coef, stiffness):
    center = padded[:, 1:-1, 1:-1]
    beside = padded[:, 2:, 1:-1] + padded[:, :-2, 1:-1] + padded[:, 1:-1, 2:] + padded[:, 1:-1, :-2]
    return vertical(center, stiffness) + coef[None] * (4.0 * center - beside)


def coarsen(field):
    return 0.25 * (
        field[..., 0::2, 0::2]
        + field[..., 1::2, 0::2]
        + field[..., 0::2, 1::2]
        + field[..., 1::2, 1::2]
    )


def line_factors(stiffness):
    gain_in = jnp.sqrt(stiffness + 0.25 * stiffness * stiffness) - 0.5 * stiffness
    return (gain_in, 1.0 - gain_in)


def compose(earlier, later):
    return (earlier[0] * later[0], later[0][:, None] * earlier[1] + later[1])


def local(rhs, areas, stiffness):
    inverse = column_inverse(stiffness)

    def fine_residual(field):
        padded = extended(field, (("wide", 1), ("narrow", 2)), 1)
        return rhs - operate(padded, areas, stiffness)

    field = relaxation * apply_columns(inverse, rhs)
    field = field + relaxation * apply_columns(inverse, fine_residual(field))
    fine_res = fine_residual(field)
    coarse_rhs = coarsen(fine_res)
    coarse_coef = 0.25 * coarsen(areas)
    gain_in, retain = line_factors(stiffness)
    columns_x = coarse_rhs.shape[1]
    running = jnp.zeros_like(coarse_rhs[:, 0])
    forward_local = []
    for step in range(columns_x):
        running = gain_in[:, None] * coarse_rhs[:, step] + retain[:, None] * running
        forward_local.append(running)
    carried = retain**columns_x
    neutral = (jnp.ones_like(carried), jnp.zeros_like(running))
    _, entering = entering_2((carried, running), "wide", compose, neutral, False)
    forward = [
        forward_local[step] + (retain ** (step + 1))[:, None] * entering
        for step in range(columns_x)
    ]
    running = jnp.zeros_like(running)
    backward_local = [running] * columns_x
    for step in reversed(range(columns_x)):
        running = gain_in[:, None] * forward[step] + retain[:, None] * running
        backward_local[step] = running
    _, leaving = entering_2((carried, running), "wide", compose, neutral, True)
    backward = [
        backward_local[step] + (retain ** (columns_x - step))[:, None] * leaving
        for step in range(columns_x)
    ]
    line_corr = jnp.stack(backward, axis=1)
    coarse_pad = extended(line_corr, (("wide", 1), ("narrow", 2)), 1)
    coarse_corr = line_corr + relaxation * apply_columns(
        inverse, coarse_rhs - operate(coarse_pad, coarse_coef, stiffness)
    )
    field = field + jnp.repeat(jnp.repeat(coarse_corr, 2, axis=1), 2, axis=2)
    field = field + relaxation * apply_columns(inverse, fine_residual(field))
    field = field + relaxation * apply_columns(inverse, fine_residual(field))
    return (field, fine_residual(field))


def solution(mesh):
    placed = (P(None, "wide", "narrow"), P("wide", "narrow"), P())
    return jax.shard_map(
        local,
        mesh=mesh,
        in_specs=placed,
        out_specs=(P(None, "wide", "narrow"), P(None, "wide", "narrow")),
        check_vma=False,
    )
```

profile of v0, /device:TPU:144, one launch (start us, length us, event | category | flops | bytes accessed | tf_op | source)
XLA Modules:
  0.0 1636.5 jit_solution(18187768366698665735)
XLA Ops:
  8.1 5.8 cholesky.17
  15.2 4.9 custom-call.6
  22.4 4.9 collective-permute-start
  29.3 8.4 collective-permute-done.1
  40.5 3.1 collective-permute-start.3
  45.6 6.3 collective-permute-done.3
  56.1 3.9 collective-permute-start.5
  60.3 6.1 collective-permute-done.5
  68.6 2.4 collective-permute-start.7
  73.1 5.3 collective-permute-done.7
  79.1 4.6 slice.260
  83.8 4.7 slice.261
  88.5 4.6 slice.262
  93.2 4.7 slice.263
  98.7 604.6 %all-reduce.12 = f32[8192]{0:T(1024)S(1)} all-reduce(f32[8192]{0:T(1024)S(1)} %get-tuple-element.338), channel_id=2, replica_groups=mesh['wide'=128,'narrow'=4] {'wide'}, use_global_device_ids=true, to_apply=%add.12 | all-reduce | flops 8192 | bytes 65536
  703.4 109.9 %while.30 = (s32[]{:T(128)}, f32[64,128]{1,0:T(8,128)S(1)}, s32[]{:T(128)}, f32[128,64]{1,0:T(8,128)S(1)}, f32[128,64,128]{2,1,0:T(8,128)}, /*index=5*/s32[]{:T(128)}, s32[]{:T(128)}) while((s32[]{:T(128)}, f32[64,128]{1,0:T(8,128)S(1)}, s32[]{:T(128)}, f32[128,64]{1,0:T(8,128)S(1)}, f32[128,64,128]{2,1,0:T(8,128)}, ...), condition=%wide.region_3.4_spmd.clone, body=%wide.region_2.3_spmd.clone.sunk | while | flops 32772 | bytes 99177 | solution.py:42
  815.0 591.1 %all-gather.7.cloned.1.call-done = f32[8192,128]{1,0:T(8,128)} async-done(((f32[64,128]{1,0:T(8,128)}), f32[8192,128]{1,0:T(8,128)}) %all-gather.7.cloned.1.call-update) | async-done | bytes 4194320 | tf_op jit(solution)/shard_map/all_gather | solution.py:29
  1406.0 111.6 %while.31 = (s32[]{:T(128)}, f32[64,128]{1,0:T(8,128)S(1)}, s32[]{:T(128)}, f32[128,64]{1,0:T(8,128)S(1)}, f32[128,64,128]{2,1,0:T(8,128)}, /*index=5*/s32[]{:T(128)}, s32[]{:T(128)}, s32[]{:T(128)}, s32[]{:T(128)}) while((s32[]{:T(128)}, f32[64,128]{1,0:T(8,128)S(1)}, s32[]{:T(128)}, f32[128,64]{1,0:T(8,128)S(1)}, ...), condition=%wide.region_5.6_spmd.clone, body=%wide.region_4.5_spmd.clone.sunk | while | flops 32776 | bytes 99239 | solution.py:42
  1519.7 8.1 collective-permute-done.9
  1530.8 3.8 collective-permute-done.8
  1539.8 5.3 collective-permute-done.11
  1546.5 6.1 collective-permute-start.12
  1554.6 8.5 collective-permute-done.13
  1567.9 2.8 collective-permute-done.14
  1570.7 5.8 collective-permute-done.15
  1579.7 3.9 collective-permute-start.17
  1583.9 6.1 collective-permute-done.17
  1596.7 5.3 collective-permute-done.19
  1605.6 3.6 collective-permute-start.21
  1609.5 6.5 collective-permute-done.21
  1618.1 2.4 collective-permute-start.23
  1622.6 5.3 collective-permute-done.23
  (619 shorter events, 277.3 us)
Async XLA Ops:
  7.2 44.7 %copy-start = (f32[64,8,256]{2,1,0:T(8,128)S(1)}, f32[64,8,256]{2,1,0:T(8,128)}, u32[]{:S(2)}) copy-start(f32[64,8,256]{2,1,0:T(8,128)} %param.7) | copy-start | bytes 1572868
  7.2 44.7 %copy-start.1 = (f32[8,256]{1,0:T(8,128)S(1)}, f32[8,256]{1,0:T(8,128)}, u32[]{:S(2)}) copy-start(f32[8,256]{1,0:T(8,128)} %param.8) | copy-start | bytes 24580
  7.2 696.3 %all-gather.5.cloned.1.call-start = ((), (), s32[]{:S(2)}) async-start(), calls=%async_computation | async-start | bytes 4227072 | tf_op jit(solution)/shard_map/all_gather | solution.py:29
  22.4 6.9 collective-permute-start
  27.3 10.4 collective-permute-start.1
  29.3 8.4 copy-start.2
  37.7 0.6 copy-start.3
  38.6 7.0 collective-permute-start.2
  40.5 11.4 collective-permute-start.3
  51.9 26.6 %copy-start.4 = (f32[64]{0:T(128)S(1)}, f32[64]{0:T(128)}, u32[]{:S(2)}) copy-start(f32[64]{0:T(128)} %param.9) | copy-start | bytes 772
  54.1 6.2 collective-permute-start.4
  56.1 10.4 collective-permute-start.5
  66.6 6.5 collective-permute-start.6
  68.6 9.9 collective-permute-start.7
  98.7 1307.4 %all-gather.7.cloned.1.call-start = ((), (), s32[]{:S(2)}) async-start(), calls=%async_computation.1 | async-start | bytes 4227072 | tf_op jit(solution)/shard_map/all_gather | solution.py:29
  1517.7 10.0 collective-permute-start.9
  1528.8 5.8 collective-permute-start.8
  1534.7 5.1 collective-permute-start.10
  1536.6 8.5 collective-permute-start.11
  1546.5 8.1 collective-permute-start.12
  1552.7 10.4 collective-permute-start.13
  1563.3 7.4 collective-permute-start.14
  1565.4 11.1 collective-permute-start.15
  1577.7 6.2 collective-permute-start.16
  1579.7 10.4 collective-permute-start.17
  1590.2 6.5 collective-permute-start.18
  1592.2 9.9 collective-permute-start.19
  1603.3 6.2 collective-permute-start.20
  1605.6 10.4 collective-permute-start.21
  1616.1 6.5 collective-permute-start.22
  1618.1 9.9 collective-permute-start.23
Sparse Core Ops, SparseCore 0:
  98.8 591.7 all-gather.4
  814.2 591.7 all-gather.6
where the time goes:
time: 1650 us; the launch traced here: 1640 us
  waiting for transfers between devices  681 us (41%)
  blocking collectives  605 us (37%)
  other arithmetic  232 us (14%)
  starting transfers between devices  63.3 us (4%)
  local copies, waits for them, and re-layouts  28 us (2%)
    unnamed x1, blocking collectives  605 us
    all_gather x2, waiting for transfers between devices, entering_2(): everything = jax.tree.map(lambda part: lax.all_gather(part, axis), array)  591 us
    select_n x256, other arithmetic, turn(): return jax.tree.map(lambda a, b: jnp.where(reached, a, b), new, before)  215 us
    ppermute x12, waiting for transfers between devices, extended(): lax.ppermute(tail, axis, [(i, (i + 1) % count) for i in range(ends)])  77.2 us
  transfers between devices with their start and end apart: 26, of which 22 were waited for; matrix products, arithmetic and copies ran while one was open for 0% of the time, Pallas kernels for 0%

commit v1 on v0

v1 whole, which is shorter than its diff:
```python
import functools

import jax
import jax.numpy as jnp
from jax import lax
from jax.experimental import pallas as pl
from jax.experimental.pallas import tpu as pltpu
from jax.sharding import PartitionSpec as P

K = 64
KA = 72
HX = 6
HY = 8
NR = 8 + 2 * HX
YP = -(-HY * NR // 128) * 128
LX = 384
PLANE = 8
f32, bf16 = jnp.float32, jnp.bfloat16
LIMIT = 32 * 1024 * 1024


def call(kernel, outs, scratch=(), specs=None):
    vmem = pl.BlockSpec(memory_space=pltpu.VMEM)
    return pl.pallas_call(
        kernel,
        out_shape=[jax.ShapeDtypeStruct(s, d) for s, d in outs],
        in_specs=specs,
        out_specs=[vmem] * len(outs),
        scratch_shapes=list(scratch),
        compiler_params=pltpu.CompilerParams(vmem_limit_bytes=LIMIT),
    )


def on_vmem(n):
    return [pl.BlockSpec(memory_space=pltpu.VMEM)] * n


def lanes(shape):
    return lax.broadcasted_iota(jnp.int32, shape, len(shape) - 1)


def wide3(table):
    return jnp.concatenate([table] * (LX // 128), axis=1)


def apply3(cat, x):
    high = x.astype(bf16)
    low = (x - high.astype(f32)).astype(bf16)
    return jnp.dot(cat, jnp.concatenate([high, high, low], axis=0), preferred_element_type=f32)


def split3(matrix):
    high = matrix.astype(bf16)
    low = (matrix - high.astype(f32)).astype(bf16)
    return jnp.concatenate([high, low, high], axis=1)


def own_row(rhs_ref, areas_ref, x):
    return (
        jnp.concatenate([rhs_ref[pl.ds(8 * t + x, K, stride=16), :] for t in range(2)], axis=1),
        jnp.broadcast_to(areas_ref[pl.ds(x, 1), :], (KA - K, 256)),
    )


def pack_x(rhs_ref, areas_ref, up_ref, down_ref):
    for x in range(8):
        field, area = own_row(rhs_ref, areas_ref, x)
        if x < HX:
            down_ref[x, :K, :] = field
            down_ref[x, K:, :] = area
        if x >= 8 - HX:
            up_ref[x - 8 + HX, :K, :] = field
            up_ref[x - 8 + HX, K:, :] = area


def tables(stiff_ref, smooth_ref, vert_ref, retain_ref, weight_ref, lead, trail):
    scale = 7.5
    row = lax.broadcasted_iota(jnp.int32, (K, 128), 0)
    col = lax.broadcasted_iota(jnp.int32, (K, 128), 1)
    lane = lanes((1, 128))
    one = jnp.ones((1, 128), f32)
    zero = jnp.zeros((1, 128), f32)
    before, now, lead_row = zero, one, zero
    after, later, trail_row = zero, one, zero
    for k in range(K):
        lead[pl.ds(k, 1), :] = now
        lead_row = jnp.where(lane == k, now, lead_row)
        now, before = (stiff_ref[k] + 8.0) * (1.0 / scale) * now - (4.0 / scale**2) * before, now
        at = K - 1 - k
        trail[pl.ds(at, 1), :] = later
        trail_row = jnp.where(lane == at, later, trail_row)
        later, after = (stiff_ref[at] + 8.0) * (1.0 / scale) * later - (4.0 / scale**2) * after, later
    gap = jnp.abs(row - col)
    decay = jnp.ones((K, 128), f32)
    for b in range(6):
        decay = decay * jnp.where((gap >> b) & 1 == 1, (2.0 / scale) ** (1 << b), 1.0)
    upper = lead[...] * trail_row
    lower = lead_row * trail[...]
    inverse = decay * jnp.where(row <= col, upper, lower) / (scale * now)
    smooth_ref[...] = split3((0.4 * inverse)[:, :K])
    stiff_row = zero
    for k in range(K):
        stiff_row = jnp.where(lane == k, stiff_ref[k], stiff_row)
    diagonal = jnp.where(row == col, stiff_row, 0.0)
    stiff = jnp.broadcast_to(jnp.sum(diagonal, axis=1, keepdims=True), (K, 128))
    vert = jnp.where(row == col, stiff + 4.0, jnp.where(gap == 1, -2.0, 0.0))
    vert_ref[...] = split3(vert[:, :K])
    keep = jnp.sqrt(stiff + 0.25 * stiff * stiff) - 0.5 * stiff
    retain_ref[...] = 1.0 - keep
    weight_ref[...] = keep / (2.0 - keep)


def ext_row(rhs_ref, areas_ref, left_ref, right_ref, r):
    if r < HX:
        return left_ref[r]
    if r >= HX + 8:
        return right_ref[r - HX - 8]
    return jnp.concatenate(own_row(rhs_ref, areas_ref, r - HX), axis=0)


def pack_y(rhs_ref, areas_ref, left_ref, right_ref, low_ref, high_ref):
    lane = lanes((KA, 128))
    low = [jnp.zeros((KA, 128), f32)] * (YP // 128)
    high = list(low)
    for r in range(NR):
        row = ext_row(rhs_ref, areas_ref, left_ref, right_ref, r)
        t, o = divmod(HY * r, 128)
        here = (lane >= o) & (lane < o + HY)
        low[t] = jnp.where(here, pltpu.roll(row[:, :128], o, 1), low[t])
        high[t] = jnp.where(here, pltpu.roll(row[:, 128:], (o + HY) % 128, 1), high[t])
    low_ref[...] = jnp.concatenate(low, axis=1)
    high_ref[...] = jnp.concatenate(high, axis=1)


def smooth_term(u, rhs, area, above, below, step):
    beside = above + below + pltpu.roll(u, step, 1) + pltpu.roll(u, LX - step, 1)
    return rhs - area * (4.0 * u - beside)


def pair_sum(v):
    even = lanes(v.shape) % 2 == 0
    return v + jnp.where(even, pltpu.roll(v, LX - 1, 1), pltpu.roll(v, 1, 1))


def before_scan(
    rhs_ref, areas_ref, left_ref, right_ref, from_left, from_right, smooth_ref, vert_ref, retain_ref,
    sent_ref, ext_ref, u2_ref, coarse_ref, u1, fine,
):
    lane = lanes((KA, 128))
    for r in range(NR):
        row = ext_row(rhs_ref, areas_ref, left_ref, right_ref, r)
        t, o = divmod(HY * r, 128)
        right = pltpu.roll(from_right[:, 128 * t : 128 * t + 128], (128 - o) % 128, 1)
        left = pltpu.roll(from_left[:, 128 * t : 128 * t + 128], (128 - HY - o) % 128, 1)
        beyond = jnp.where(lane < HY, right, jnp.where(lane >= 128 - HY, left, 0.0))
        ext_ref[r, :, :256] = row
        ext_ref[r, :, 256:] = beyond

    smooth = smooth_ref[...]

    def first(r, _):
        u1[r] = apply3(smooth, ext_ref[r, :K, :])
        return 0

    lax.fori_loop(0, NR, first, 0, unroll=2)

    def second(r, _):
        u = u1[r]
        term = smooth_term(u, ext_ref[r, :K, :] + 4.0 * u, ext_ref[r, K : K + 1, :], u1[r - 1], u1[r + 1], 1)
        fine[r] = 0.6 * u + apply3(smooth, term)
        return 0

    lax.fori_loop(1, NR - 1, second, 0, unroll=2)
    vert = vert_ref[...]

    def third(j, _):
        r = 2 * j + HX - 4
        total, field = 0.0, 0.0
        for at in (r, r + 1):
            u = fine[at]
            total += smooth_term(u, ext_ref[at, :K, :], ext_ref[at, K : K + 1, :], fine[at - 1], fine[at + 1], 1)
            field += u
        coarse_ref[j] = 0.25 * (pair_sum(total) - apply3(vert, pair_sum(field)))
        return 0

    lax.fori_loop(0, 8, third, 0)
    for r in range(14):
        u2_ref[r] = fine[r + HX - 3]
    retain = wide3(retain_ref[...])
    ahead = coarse_ref[2]
    back = coarse_ref[5]
    for j in range(1, 4):
        ahead = retain * ahead + coarse_ref[2 + j]
        back = retain * back + coarse_ref[5 - j]
    fine_lane = lax.broadcasted_iota(jnp.int32, (LX, 256), 0)
    coarse_lane = lax.broadcasted_iota(jnp.int32, (LX, 256), 1)
    pick = jnp.where(fine_lane == 2 * coarse_lane, 1.0, 0.0)
    both = jnp.dot(
        jnp.concatenate([ahead, back], axis=0), pick, precision=lax.Precision.HIGHEST, preferred_element_type=f32
    )
    sent_ref[:, :128] = both[:K, :128]
    sent_ref[:, 128:256] = both[K:, :128]
    sent_ref[:, 256:] = both[:K, 128:] + pltpu.roll(both[K:, 128:], 64, 1)


def power(x, n):
    out = None
    while n:
        if n & 1:
            out = x if out is None else out * x
        x = x * x
        n >>= 1
    return out


def my_retain(retain_ref):
    at = lax.rem(lax.axis_index("wide"), PLANE)
    return retain_ref[pl.ds(pl.multiple_of(at * 8, 8), 8), :]


def plane_ends(blocks, retain):
    four = power(retain, 4)
    ends = []
    for order, part in ((range(PLANE), 0), (reversed(range(PLANE)), 1)):
        main, tail = 0.0, 0.0
        for m in order:
            main = four * main + blocks[m, :, 128 * part : 128 * part + 128]
            tail = four * tail + blocks[m, :, 256:]
        ends += [main, tail if part == 0 else pltpu.roll(tail, 64, 1)]
    return ends


def across_out(planes, blocks_ref, retain_ref, out_ref):
    retain = my_retain(retain_ref)
    here = lax.div(lax.axis_index("wide"), PLANE)
    ahead, ahead_tail, back, back_tail = plane_ends(blocks_ref, retain)
    reflect = power(retain, 33)
    step = power(retain, 64)
    for q in range(planes):
        reflect = jnp.where(q > here, reflect * step, reflect)
    back = back - reflect * ahead
    back_tail = back_tail - reflect * ahead_tail
    for q in range(planes):
        out_ref[q, :, :128] = jnp.where(q > here, ahead, back)
        out_ref[q, :, 128:] = jnp.where(q > here, ahead_tail, back_tail)


def across_in(planes, blocks_ref, others_ref, retain_ref, out_ref):
    retain = my_retain(retain_ref)
    here = lax.div(lax.axis_index("wide"), PLANE)
    ahead, ahead_tail, _, _ = plane_ends(blocks_ref, retain)
    four, plane = power(retain, 4), power(retain, 32)
    reflect, step = retain, power(retain, 64)
    enter, leave = [0.0, 0.0], [0.0, 0.0]
    for q in range(planes):
        reflect = jnp.where(q > here, reflect * step, reflect)
        back = planes - 1 - q
        for part in range(2):
            at = slice(128 * part, 128 * part + 128)
            enter[part] = jnp.where(q < here, plane * enter[part] + others_ref[q, :, at], enter[part])
            leave[part] = jnp.where(back > here, plane * leave[part] + others_ref[back, :, at], leave[part])
    leave[0] = leave[0] - reflect * (ahead + plane * enter[0])
    leave[1] = leave[1] - reflect * (ahead_tail + plane * enter[1])
    left = lanes((8, 128)) < 64
    leave[1] = pltpu.roll(leave[1], 64, 1)
    tails = []
    for m in range(PLANE):
        out_ref[m, :, :128] = enter[0]
        tails.append(enter[1])
        enter[0] = four * enter[0] + blocks_ref[m, :, :128]
        enter[1] = four * enter[1] + blocks_ref[m, :, 256:]
    for m in reversed(range(PLANE)):
        out_ref[m, :, 128:256] = leave[0]
        out_ref[m, :, 256:] = jnp.where(left, tails[m], leave[1])
        leave[0] = four * leave[0] + blocks_ref[m, :, 128:256]
        leave[1] = four * leave[1] + blocks_ref[m, :, 256:]


def after_scan(
    got_ref, ext_ref, u2_ref, coarse_ref, smooth_ref, vert_ref, retain_ref, weight_ref,
    pressure_ref, residual_ref, line, corr, ua, ub,
):
    retain, weight = wide3(retain_ref[...]), wide3(weight_ref[...])
    inv_retain = 1.0 / retain
    coarse_lane = lax.broadcasted_iota(jnp.int32, (256, LX), 0)
    fine_lane = lax.broadcasted_iota(jnp.int32, (256, LX), 1)
    spread = jnp.where(fine_lane // 2 == coarse_lane, 1.0, 0.0)
    keep_left = lanes((K, 128)) < 64
    tail = got_ref[:, 256:]
    both = jnp.concatenate(
        [
            jnp.concatenate([got_ref[:, :128], jnp.where(keep_left, tail, 0.0)], axis=1),
            jnp.concatenate([got_ref[:, 128:256], jnp.where(keep_left, pltpu.roll(tail, 64, 1), 0.0)], axis=1),
        ],
        axis=0,
    )
    both = jnp.dot(both, spread, precision=lax.Precision.HIGHEST, preferred_element_type=f32)

    def coef(j):
        r = 2 * j + HX - 4
        return 0.0625 * pair_sum(ext_ref[r, K : K + 1, :] + ext_ref[r + 1, K : K + 1, :])

    enter, leave = both[:K], both[K:]
    reach = leave
    for j in (4, 5):
        reach = (reach - coarse_ref[j + 2]) * inv_retain
        line[j + 1 + 3] = reach
    reach = leave
    line[4 + 3] = reach
    for j in (3, 2, 1, 0, -1, -2):
        reach = coarse_ref[j + 2] + retain * reach
        line[j + 3] = reach
    ahead = (enter - coarse_ref[1]) * inv_retain
    ahead = (ahead - coarse_ref[0]) * inv_retain
    line[0] = jnp.where(coef(0) > 0.0, weight * (ahead + retain * line[1]), 0.0)
    for j in range(-2, 7):
        inside = coef(min(max(j + 2, 0), 7)) > 0.0
        start = retain * ahead
        line[j + 3] = jnp.where(inside, weight * (start + line[j + 3]), 0.0)
        if j < 6:
            ahead = enter if j == -1 else coarse_ref[j + 2] + start

    smooth = smooth_ref[...]

    def coarse(j, _):
        v = line[j + 1]
        area = coef(j)
        term = smooth_term(v, coarse_ref[j] + 4.0 * v, area, line[j], line[j + 2], 2)
        corr[j] = 0.6 * v + apply3(smooth, term)
        return 0

    lax.fori_loop(0, 8, coarse, 0)
    for i in range(14):
        ua[i] = u2_ref[i] + corr[(i - 3) // 2 + 2]

    def smoothing(source, target, i):
        u = source[i]
        r = i + HX - 3
        term = smooth_term(u, ext_ref[r, :K, :] + 4.0 * u, ext_ref[r, K : K + 1, :], source[i - 1], source[i + 1], 1)
        target[i] = 0.6 * u + apply3(smooth, term)
        return 0

    lax.fori_loop(1, 13, lambda i, _: smoothing(ua, ub, i), 0, unroll=2)
    lax.fori_loop(2, 12, lambda i, _: smoothing(ub, ua, i), 0, unroll=2)
    vert = vert_ref[...]
    for x in range(8):
        i = x + 3
        u = ua[i]
        r = x + HX
        term = smooth_term(u, ext_ref[r, :K, :], ext_ref[r, K : K + 1, :], ua[i - 1], ua[i + 1], 1)
        rest = term[:, :256] - apply3(vert, u[:, :256])
        for t in range(2):
            here = pl.ds(8 * t + x, K, stride=16)
            pressure_ref[here, :] = u[:, 128 * t : 128 * t + 128]
            residual_ref[here, :] = rest[:, 128 * t : 128 * t + 128]


def local(rhs, areas, stiffness):
    wide, narrow = lax.axis_size("wide"), lax.axis_size("narrow")
    planes = wide // PLANE
    rhs = rhs.reshape(K, 8, 2, 128).transpose(0, 2, 1, 3).reshape(K * 16, 128)
    up, down = call(pack_x, [((HX, KA, 256), f32)] * 2, specs=on_vmem(2))(rhs, areas)

    def shift(array, axis, count, by):
        pairs = [(i, i + by) for i in range(count) if 0 <= i + by < count]
        return lax.ppermute(array, axis, pairs)

    left = shift(up, "wide", wide, 1)
    right = shift(down, "wide", wide, -1)
    smooth, vert, retain, weight = call(
        tables,
        [((K, 192), bf16)] * 2 + [((K, 128), f32)] * 2,
        [pltpu.VMEM((K, 128), f32)] * 2,
        [pl.BlockSpec(memory_space=pltpu.SMEM)],
    )(stiffness)
    low, high = call(pack_y, [((KA, YP), f32)] * 2, specs=on_vmem(4))(rhs, areas, left, right)
    from_left = shift(high, "narrow", narrow, 1)
    from_right = shift(low, "narrow", narrow, -1)
    sent, ext, u2, coarse = call(
        before_scan,
        [((K, LX), f32), ((NR, KA, LX), f32), ((14, K, LX), f32), ((8, K, LX), f32)],
        [pltpu.VMEM((NR, K, LX), f32)] * 2,
        on_vmem(9),
    )(rhs, areas, left, right, from_left, from_right, smooth, vert, retain)
    in_plane = [[p * PLANE + m for m in range(PLANE)] for p in range(planes)]
    over_planes = [[p * PLANE + m for p in range(planes)] for m in range(PLANE)]

    def exchange(array, groups):
        return lax.all_to_all(array, "wide", 0, 0, tiled=True, axis_index_groups=groups)

    blocks = exchange(sent.reshape(PLANE, 8, LX), in_plane)
    (out,) = call(functools.partial(across_out, planes), [((planes, 8, 256), f32)], specs=on_vmem(2))(blocks, retain)
    others = exchange(out, over_planes)
    (back,) = call(functools.partial(across_in, planes), [((PLANE, 8, LX), f32)], specs=on_vmem(3))(
        blocks, others, retain
    )
    got = exchange(back, in_plane).reshape(K, LX)
    pressure, residual = call(
        after_scan,
        [((K * 16, 128), f32)] * 2,
        [pltpu.VMEM((10, K, LX), f32), pltpu.VMEM((8, K, LX), f32)] + [pltpu.VMEM((14, K, LX), f32)] * 2,
        on_vmem(8),
    )(got, ext, u2, coarse, smooth, vert, retain, weight)
    return tuple(
        out.reshape(K, 2, 8, 128).transpose(0, 2, 1, 3).reshape(K, 8, 256) for out in (pressure, residual)
    )


def solution(mesh):
    placed = (P(None, "wide", "narrow"), P("wide", "narrow"), P())
    return jax.shard_map(
        local,
        mesh=mesh,
        in_specs=placed,
        out_specs=(P(None, "wide", "narrow"), P(None, "wide", "narrow")),
        check_vma=False,
    )
```

time: 1650 us -> 104 us (0.06)
  the two profiles are of different devices: /device:TPU:144 before, /device:TPU:1 now
where the time goes in v1:
time: 104 us; the launch traced here: 103 us
  blocking collectives  47 us (45%)
  Pallas kernels  19.2 us (18%)
  waiting for transfers between devices  17.8 us (17%)
  starting transfers between devices  16.2 us (16%)
  local copies, waits for them, and re-layouts  2.39 us (2%)
    all_to_all x3, blocking collectives, exchange(): lax.all_to_all(array, 'wide', 0, 0, tiled=True, axis_index_groups=groups)  47 us
    ppermute x4, waiting for transfers between devices, shift(): return lax.ppermute(array, axis, pairs)  17.8 us
    ppermute x4, starting transfers between devices, shift(): return lax.ppermute(array, axis, pairs)  16.2 us
    pallas_call x1, Pallas kernels, local(): call(before_scan, [((K, LX), f32), ((NR, KA, LX), f32), ((14, K, LX), f32...  9.13 us
    pallas_call x1, Pallas kernels, local(): call(after_scan, [((K * 16, 128), f32)] * 2, [pltpu.VMEM((10, K, LX), f32...  8.41 us
    unnamed x8, local copies, waits for them, and re-layouts  2.39 us
  transfers between devices with their start and end apart: 4, of which 2 were waited for; matrix products, arithmetic and copies ran while one was open for 0% of the time, Pallas kernels for 1%

profile of v1, /device:TPU:1, one launch (start us, length us, event | category | flops | bytes accessed | tf_op | source)
XLA Modules:
  0.0 103.2 jit_solution(14903296317684239692)
XLA Ops:
  0.6 0.0 copy-start
  0.6 1.0 %copy-done = f32[64,8,256]{2,1,0:T(8,128)S(1)} copy-done((f32[64,8,256]{2,1,0:T(8,128)S(1)}, f32[64,8,256]{2,1,0:T(8,128)}, u32[]{:S(2)}) %copy-start) | copy-done | bytes 524312
  1.7 0.0 copy-start.2
  1.7 0.7 copy-done.2
  2.4 0.0 copy-start.1
  2.4 0.2 shard_map.50
  2.5 4.1 %collective-permute-start = (f32[6,72,256]{2,1,0:T(8,128)S(1)}, f32[6,72,256]{2,1,0:T(8,128)S(1)}, u32[]{:S(2)}, u32[]{:S(2)}) collective-permute-start(f32[6,72,256]{2,1,0:T(8,128)S(1)} %get-tuple-element.16), channel_id=1, source_target_pairs={{0,4},{4,8},{8,12},{12,16},{16,20},{20,24},{24,28},{28,32},{32,36}... | collective-permute-start | bytes 1327112 | tf_op jit(solution)/shard_map/ppermute | solution.py:366
  6.6 1.3 %collective-permute-start.1 = (f32[6,72,256]{2,1,0:T(8,128)S(1)}, f32[6,72,256]{2,1,0:T(8,128)S(1)}, u32[]{:S(2)}, u32[]{:S(2)}) collective-permute-start(f32[6,72,256]{2,1,0:T(8,128)S(1)} %get-tuple-element.17), channel_id=1, source_target_pairs={{4,0},{8,4},{12,8},{16,12},{20,16},{24,20},{28,24},{32,28},{36,32}... | collective-permute-start | bytes 1327112 | tf_op jit(solution)/shard_map/ppermute | solution.py:366
  7.9 14.0 %collective-permute-done.left_ref = f32[6,72,256]{2,1,0:T(8,128)S(1)} collective-permute-done((f32[6,72,256]{2,1,0:T(8,128)S(1)}, f32[6,72,256]{2,1,0:T(8,128)S(1)}, u32[]{:S(2)}, u32[]{:S(2)}) %collective-permute-start) | collective-permute-done | bytes 442400 | tf_op jit(solution)/shard_map/ppermute | solution.py:366
  22.0 0.0 collective-permute-done.1.right_ref
  22.0 0.5 shard_map.51
  22.4 8.9 %collective-permute-start.2 = (f32[72,256]{1,0:T(8,128)S(1)}, f32[72,256]{1,0:T(8,128)S(1)}, u32[]{:S(2)}, u32[]{:S(2)}) collective-permute-start(f32[72,256]{1,0:T(8,128)S(1)} %get-tuple-element.18), channel_id=1, source_target_pairs={{0,1},{1,2},{2,3},{4,5},{5,6},{6,7},{8,9},{9,10},{10,11},{12,13},{... | collective-permute-start | bytes 221192 | tf_op jit(solution)/shard_map/ppermute | solution.py:366
  31.3 1.9 %collective-permute-start.3 = (f32[72,256]{1,0:T(8,128)S(1)}, f32[72,256]{1,0:T(8,128)S(1)}, u32[]{:S(2)}, u32[]{:S(2)}) collective-permute-start(f32[72,256]{1,0:T(8,128)S(1)} %get-tuple-element.19), channel_id=1, source_target_pairs={{1,0},{2,1},{3,2},{5,4},{6,5},{7,6},{9,8},{10,9},{11,10},{13,12},{... | collective-permute-start | bytes 221192 | tf_op jit(solution)/shard_map/ppermute | solution.py:366
  33.2 0.0 copy-start.3
  33.3 0.6 copy-done.3
  33.9 0.8 shard_map.52
  34.7 0.0 collective-permute-done.2.from_left
  34.7 3.8 %collective-permute-done.3.from_right = f32[72,256]{1,0:T(8,128)S(1)} collective-permute-done((f32[72,256]{1,0:T(8,128)S(1)}, f32[72,256]{1,0:T(8,128)S(1)}, u32[]{:S(2)}, u32[]{:S(2)}) %collective-permute-start.3) | collective-permute-done | bytes 73760 | tf_op jit(solution)/shard_map/ppermute | solution.py:366
  38.5 0.0 copy-done.1
  38.5 9.1 %shard_map.53 = (f32[64,384]{1,0:T(8,128)S(1)}, f32[20,72,384]{2,1,0:T(8,128)S(1)}, f32[14,64,384]{2,1,0:T(8,128)S(1)}, f32[8,64,384]{2,1,0:T(8,128)S(1)}) custom-call(f32[1024,128]{1,0:T(8,128)S(1)} %bitcast.19, f32[8,256]{1,0:T(8,128)S(1)} %copy-done.2, f32[6,72,256]{2,1,0:T(8,128)S(1)} %collective-permute-done.left_ref, ...), custom_call_target="tpu_custom_call" | custom-call | tf_op jit(solution)/shard_map/pallas_call | solution.py:379
  47.6 11.1 %all_to_all.15.blocks_ref = f32[8,8,384]{2,1,0:T(8,128)S(1)} all-to-all(f32[8,8,384]{2,1,0:T(8,128)S(1)} %bitcast.21), channel_id=1, replica_groups={{0,4,8,12,16,20,24,28},{32,36,40,44,48,52,56,60},{64,68,72,76,80,84,88,..., dimensions={0} | all-to-all | bytes 196608 | tf_op jit(solution)/shard_map/all_to_all | solution.py:389
  58.7 0.1 shard_map.54
  58.8 28.3 %all_to_all.16.others_ref = f32[16,8,256]{2,1,0:T(8,128)S(1)} all-to-all(f32[16,8,256]{2,1,0:T(8,128)S(1)} %shard_map.54), channel_id=1, replica_groups={{0,32,64,96,128,160,192,224,256,288,320,352,384,416,448,480},{4,36,68,1..., dimensions={0} | all-to-all | bytes 262144 | tf_op jit(solution)/shard_map/all_to_all | solution.py:389
  87.1 0.1 shard_map.55
  87.3 7.5 %all_to_all.17 = f32[8,8,384]{2,1,0:T(8,128)S(1)} all-to-all(f32[8,8,384]{2,1,0:T(8,128)S(1)} %shard_map.55), channel_id=1, replica_groups={{0,4,8,12,16,20,24,28},{32,36,40,44,48,52,56,60},{64,68,72,76,80,84,88,..., dimensions={0} | all-to-all | bytes 196608 | tf_op jit(solution)/shard_map/all_to_all | solution.py:389
  94.8 8.4 %shard_map.56 = (f32[1024,128]{1,0:T(8,128)}, f32[1024,128]{1,0:T(8,128)}) custom-call(f32[64,384]{1,0:T(8,128)S(1)} %bitcast.20, f32[20,72,384]{2,1,0:T(8,128)S(1)} %get-tuple-element.24.ext_ref, f32[14,64,384]{2,1,0:T(8,128)S(1)} %get-tuple-element.25.u2_ref, f32[8,64,384]{2,1,0:T(8,128)S(1)} %get-tuple-element.26.coarse_ref, ...), custom_call_target="tpu_custom_call" | custom-call | tf_op jit(solution)/shard_map/pallas_call | solution.py:398
Async XLA Ops:
  0.6 1.0 %copy-start = (f32[64,8,256]{2,1,0:T(8,128)S(1)}, f32[64,8,256]{2,1,0:T(8,128)}, u32[]{:S(2)}) copy-start(f32[64,8,256]{2,1,0:T(8,128)} %param.3) | copy-start | bytes 1572868
  1.7 0.7 copy-start.2
  2.4 36.1 %copy-start.1 = (f32[64,8,256]{2,1,0:T(8,128)S(1)}, f32[64,8,256]{2,1,0:T(8,128)}, u32[]{:S(2)}) copy-start(f32[64,8,256]{2,1,0:T(8,128)} %param.3) | copy-start | bytes 1572868
  2.5 19.4 %collective-permute-start = (f32[6,72,256]{2,1,0:T(8,128)S(1)}, f32[6,72,256]{2,1,0:T(8,128)S(1)}, u32[]{:S(2)}, u32[]{:S(2)}) collective-permute-start(f32[6,72,256]{2,1,0:T(8,128)S(1)} %get-tuple-element.16), channel_id=1, source_target_pairs={{0,4},{4,8},{8,12},{12,16},{16,20},{20,24},{24,28},{28,32},{32,36}... | collective-permute-start | bytes 1327112 | tf_op jit(solution)/shard_map/ppermute | solution.py:366
  6.6 15.3 %collective-permute-start.1 = (f32[6,72,256]{2,1,0:T(8,128)S(1)}, f32[6,72,256]{2,1,0:T(8,128)S(1)}, u32[]{:S(2)}, u32[]{:S(2)}) collective-permute-start(f32[6,72,256]{2,1,0:T(8,128)S(1)} %get-tuple-element.17), channel_id=1, source_target_pairs={{4,0},{8,4},{12,8},{16,12},{20,16},{24,20},{28,24},{32,28},{36,32}... | collective-permute-start | bytes 1327112 | tf_op jit(solution)/shard_map/ppermute | solution.py:366
  22.4 12.3 %collective-permute-start.2 = (f32[72,256]{1,0:T(8,128)S(1)}, f32[72,256]{1,0:T(8,128)S(1)}, u32[]{:S(2)}, u32[]{:S(2)}) collective-permute-start(f32[72,256]{1,0:T(8,128)S(1)} %get-tuple-element.18), channel_id=1, source_target_pairs={{0,1},{1,2},{2,3},{4,5},{5,6},{6,7},{8,9},{9,10},{10,11},{12,13},{... | collective-permute-start | bytes 221192 | tf_op jit(solution)/shard_map/ppermute | solution.py:366
  31.3 7.2 %collective-permute-start.3 = (f32[72,256]{1,0:T(8,128)S(1)}, f32[72,256]{1,0:T(8,128)S(1)}, u32[]{:S(2)}, u32[]{:S(2)}) collective-permute-start(f32[72,256]{1,0:T(8,128)S(1)} %get-tuple-element.19), channel_id=1, source_target_pairs={{1,0},{2,1},{3,2},{5,4},{6,5},{7,6},{9,8},{10,9},{11,10},{13,12},{... | collective-permute-start | bytes 221192 | tf_op jit(solution)/shard_map/ppermute | solution.py:366
  33.2 0.7 copy-start.3

commit v2 on v1

--- a/solution.py
+++ b/solution.py
@@ -9,14 +9,17 @@
 
 K = 64
 KA = 72
-HX = 6
+HX = 2
 HY = 8
 NR = 8 + 2 * HX
-YP = -(-HY * NR // 128) * 128
 LX = 384
 PLANE = 8
 f32, bf16 = jnp.float32, jnp.bfloat16
-LIMIT = 32 * 1024 * 1024
+DEEP_LATE = True
+K2_OUTS = [((K, LX), f32), ((NR, KA, 128), f32), ((8, K, LX), f32), ((4, K, LX), f32)]
+K2_SCRATCH = [pltpu.VMEM((NR, K, 128), f32), pltpu.VMEM((NR, K, LX), f32)]
+K4_SCRATCH = [pltpu.VMEM(s, f32) for s in ((8, K, LX), (10, K, LX), (8, K, LX), (14, K, LX), (14, K, LX))]
+LIMIT = 16 * 1024 * 1024
 
 
 def call(kernel, outs, scratch=(), specs=None):
@@ -49,28 +52,46 @@
     return jnp.dot(cat, jnp.concatenate([high, high, low], axis=0), preferred_element_type=f32)
 
 
+def select(x, picks):
+    high = x.astype(bf16)
+    rest = x - high.astype(f32)
+    middle = rest.astype(bf16)
+    low = (rest - middle.astype(f32)).astype(bf16)
+    rows = x.shape[0]
+    parts = jnp.dot(jnp.concatenate([high, middle, low], axis=0), picks.astype(bf16), preferred_element_type=f32)
+    return parts[:rows] + (parts[rows : 2 * rows] + parts[2 * rows :])
+
+
 def split3(matrix):
     high = matrix.astype(bf16)
     low = (matrix - high.astype(f32)).astype(bf16)
     return jnp.concatenate([high, low, high], axis=1)
 
 
-def own_row(rhs_ref, areas_ref, x):
-    return (
-        jnp.concatenate([rhs_ref[pl.ds(8 * t + x, K, stride=16), :] for t in range(2)], axis=1),
-        jnp.broadcast_to(areas_ref[pl.ds(x, 1), :], (KA - K, 256)),
-    )
-
-
-def pack_x(rhs_ref, areas_ref, up_ref, down_ref):
+def pack_x(rhs_hbm, areas_hbm, up_ref, down_ref, own_ref, rhs, areas, sems):
+    copies = [
+        pltpu.make_async_copy(rhs_hbm, rhs, sems.at[0]),
+        pltpu.make_async_copy(areas_hbm, areas, sems.at[1]),
+    ]
+    for copy in copies:
+        copy.start()
+    for copy in copies:
+        copy.wait()
+    first = lax.broadcasted_iota(jnp.int32, (KA - K, 256), 0) == 0
+
+    def area(x, beyond):
+        return jnp.where(first, areas[x : x + 1, :], areas[beyond : beyond + 1, :])
+
     for x in range(8):
-        field, area = own_row(rhs_ref, areas_ref, x)
+        for t in range(2):
+            own_ref[x, :K, 128 * t : 128 * t + 128] = rhs[pl.ds(8 * t + x, K, stride=16), :]
+        own_ref[x, K:, :] = area(x, x)
         if x < HX:
-            down_ref[x, :K, :] = field
-            down_ref[x, K:, :] = area
+            down_ref[x, :K, :] = own_ref[x, :K, :]
+            down_ref[x, K:, :] = area(x, x + HX)
         if x >= 8 - HX:
-            up_ref[x - 8 + HX, :K, :] = field
-            up_ref[x - 8 + HX, K:, :] = area
+            up_ref[x - 8 + HX, :K, :] = own_ref[x, :K, :]
+            up_ref[x - 8 + HX, K:, :] = area(x, x - HX)
 
 
 def tables(stiff_ref, smooth_ref, vert_ref, retain_ref, weight_ref, lead, trail):
@@ -110,26 +131,42 @@
     weight_ref[...] = keep / (2.0 - keep)
 
 
-def ext_row(rhs_ref, areas_ref, left_ref, right_ref, r):
+def ext_row(own_ref, left_ref, right_ref, r):
     if r < HX:
         return left_ref[r]
     if r >= HX + 8:
         return right_ref[r - HX - 8]
-    return jnp.concatenate(own_row(rhs_ref, areas_ref, r - HX), axis=0)
-
-
-def pack_y(rhs_ref, areas_ref, left_ref, right_ref, low_ref, high_ref):
+    return own_ref[r - HX]
+
+
+def whole_row(own_ref, left_ref, right_ref, tails_ref, r, levels=K):
+    main = ext_row(own_ref, left_ref, right_ref, r)
+    tail = tails_ref[r]
+    at = slice(levels, levels + 1)
+    return (
+        jnp.concatenate([main[:K], tail[:K]], axis=1),
+        jnp.concatenate([main[at], tail[at]], axis=1),
+    )
+
+
+def pack_y(own_ref, left_ref, right_ref, _, first_ref, second_ref):
     lane = lanes((KA, 128))
-    low = [jnp.zeros((KA, 128), f32)] * (YP // 128)
-    high = list(low)
+    low = high = jnp.zeros((KA, 128), f32)
     for r in range(NR):
-        row = ext_row(rhs_ref, areas_ref, left_ref, right_ref, r)
-        t, o = divmod(HY * r, 128)
+        row = ext_row(own_ref, left_ref, right_ref, r)
+        o = HY * r
         here = (lane >= o) & (lane < o + HY)
-        low[t] = jnp.where(here, pltpu.roll(row[:, :128], o, 1), low[t])
-        high[t] = jnp.where(here, pltpu.roll(row[:, 128:], (o + HY) % 128, 1), high[t])
-    low_ref[...] = jnp.concatenate(low, axis=1)
-    high_ref[...] = jnp.concatenate(high, axis=1)
+        low = jnp.where(here, pltpu.roll(row[:, :128], o, 1), low)
+        high = jnp.where(here, pltpu.roll(row[:, 128:], o + HY, 1), high)
+    even = lax.rem(lax.axis_index("narrow"), 2) == 0
+    first_ref[...] = jnp.where(even, high, low)
+    second_ref[...] = jnp.where(even, low, high)
+
+
+def first_main(own_ref, left_ref, right_ref, smooth_ref, u1_ref):
+    smooth = smooth_ref[...]
+    for r in range(NR):
+        u1_ref[r] = apply3(smooth, ext_row(own_ref, left_ref, right_ref, r)[:K])
 
 
 def smooth_term(u, rhs, area, above, below, step):
@@ -142,62 +179,89 @@
     return v + jnp.where(even, pltpu.roll(v, LX - 1, 1), pltpu.roll(v, 1, 1))
 
 
+def pack_deep(u2_ref, coarse_ref, up_ref, down_ref):
+    pack_side([u2_ref[x] for x in (5, 6, 7)], [coarse_ref[2], coarse_ref[3]], up_ref)
+    pack_side([u2_ref[x] for x in (0, 1, 2)], [coarse_ref[0], coarse_ref[1]], down_ref)
+
+
+def pack_side(rows, coarse, out_ref):
+    lane = lanes((K, 128))
+    even = lanes((K, LX)) % 2 == 0
+    rows = rows + [jnp.where(even, coarse[0], coarse[1])]
+    tails = jnp.zeros((K, 128), f32)
+    for i, row in enumerate(rows):
+        out_ref[2 * i] = row[:, :128]
+        out_ref[2 * i + 1] = row[:, 128:256]
+        here = (lane >= 16 * i) & (lane < 16 * i + 16)
+        tails = jnp.where(here, pltpu.roll(row[:, 256:], HY + 16 * i, 1), tails)
+    out_ref[8] = tails
+
+
+def unpack_deep(got_ref):
+    lane = lanes((K, 128))
+    edge = (lane < HY) | (lane >= 128 - HY)
+    rows = []
+    for i in range(4):
+        tail = jnp.where(edge, pltpu.roll(got_ref[8], 128 - HY - 16 * i, 1), 0.0)
+        rows.append(jnp.concatenate([got_ref[2 * i], got_ref[2 * i + 1], tail], axis=1))
+    both = rows.pop()
+    even = lanes((K, LX)) % 2 == 0
+    first = jnp.where(even, both, pltpu.roll(both, 1, 1))
+    second = jnp.where(even, pltpu.roll(both, LX - 1, 1), both)
+    return rows, (first, second)
+
+
 def before_scan(
-    rhs_ref, areas_ref, left_ref, right_ref, from_left, from_right, smooth_ref, vert_ref, retain_ref,
-    sent_ref, ext_ref, u2_ref, coarse_ref, u1, fine,
+    own_ref, left_ref, right_ref, first_ref, second_ref, u1_ref, smooth_ref, vert_ref, retain_ref,
+    sent_ref, tails_ref, u2_ref, coarse_ref, u1, fine,
 ):
+    smooth = smooth_ref[...]
     lane = lanes((KA, 128))
+    even = lax.rem(lax.axis_index("narrow"), 2) == 0
+    low = jnp.where(even, first_ref[...], second_ref[...])
+    high = jnp.where(even, second_ref[...], first_ref[...])
+    tails = apply3(smooth, jnp.concatenate([low[:K], high[:K]], axis=1))
+
+    def beyond(right, left, o):
+        at = lane[: right.shape[0]]
+        right = pltpu.roll(right, (128 - o) % 128, 1)
+        left = pltpu.roll(left, 128 - HY - o, 1)
+        return jnp.where(at < HY, right, jnp.where(at >= 128 - HY, left, 0.0))
+
     for r in range(NR):
-        row = ext_row(rhs_ref, areas_ref, left_ref, right_ref, r)
-        t, o = divmod(HY * r, 128)
-        right = pltpu.roll(from_right[:, 128 * t : 128 * t + 128], (128 - o) % 128, 1)
-        left = pltpu.roll(from_left[:, 128 * t : 128 * t + 128], (128 - HY - o) % 128, 1)
-        beyond = jnp.where(lane < HY, right, jnp.where(lane >= 128 - HY, left, 0.0))
-        ext_ref[r, :, :256] = row
-        ext_ref[r, :, 256:] = beyond
-
-    smooth = smooth_ref[...]
-
-    def first(r, _):
-        u1[r] = apply3(smooth, ext_ref[r, :K, :])
-        return 0
-
-    lax.fori_loop(0, NR, first, 0, unroll=2)
-
-    def second(r, _):
-        u = u1[r]
-        term = smooth_term(u, ext_ref[r, :K, :] + 4.0 * u, ext_ref[r, K : K + 1, :], u1[r - 1], u1[r + 1], 1)
+        tails_ref[r] = beyond(low, high, HY * r)
+        u1[r] = beyond(tails[:, :128], tails[:, 128:], HY * r)
+
+    def row(r):
+        return whole_row(own_ref, left_ref, right_ref, tails_ref, r)
+
+    def first(r):
+        return jnp.concatenate([u1_ref[r], u1[r]], axis=1)
+
+    for r in range(1, NR - 1):
+        u, (rhs, area) = first(r), row(r)
+        term = smooth_term(u, rhs + 4.0 * u, area, first(r - 1), first(r + 1), 1)
         fine[r] = 0.6 * u + apply3(smooth, term)
-        return 0
-
-    lax.fori_loop(1, NR - 1, second, 0, unroll=2)
     vert = vert_ref[...]
-
-    def third(j, _):
-        r = 2 * j + HX - 4
+    for j in range(4):
         total, field = 0.0, 0.0
-        for at in (r, r + 1):
-            u = fine[at]
-            total += smooth_term(u, ext_ref[at, :K, :], ext_ref[at, K : K + 1, :], fine[at - 1], fine[at + 1], 1)
+        for at in (2 * j + HX, 2 * j + HX + 1):
+            u, (rhs, area) = fine[at], row(at)
+            total += smooth_term(u, rhs, area, fine[at - 1], fine[at + 1], 1)
             field += u
         coarse_ref[j] = 0.25 * (pair_sum(total) - apply3(vert, pair_sum(field)))
-        return 0
-
-    lax.fori_loop(0, 8, third, 0)
-    for r in range(14):
-        u2_ref[r] = fine[r + HX - 3]
+    for x in range(8):
+        u2_ref[x] = fine[x + HX]
     retain = wide3(retain_ref[...])
-    ahead = coarse_ref[2]
-    back = coarse_ref[5]
+    ahead = coarse_ref[0]
+    back = coarse_ref[3]
     for j in range(1, 4):
-        ahead = retain * ahead + coarse_ref[2 + j]
-        back = retain * back + coarse_ref[5 - j]
+        ahead = retain * ahead + coarse_ref[j]
+        back = retain * back + coarse_ref[3 - j]
     fine_lane = lax.broadcasted_iota(jnp.int32, (LX, 256), 0)
     coarse_lane = lax.broadcasted_iota(jnp.int32, (LX, 256), 1)
     pick = jnp.where(fine_lane == 2 * coarse_lane, 1.0, 0.0)
-    both = jnp.dot(
-        jnp.concatenate([ahead, back], axis=0), pick, precision=lax.Precision.HIGHEST, preferred_element_type=f32
-    )
+    both = select(jnp.concatenate([ahead, back], axis=0), pick)
     sent_ref[:, :128] = both[:K, :128]
     sent_ref[:, 128:256] = both[K:, :128]
     sent_ref[:, 256:] = both[:K, 128:] + pltpu.roll(both[K:, 128:], 64, 1)
@@ -277,9 +341,16 @@
 
 
 def after_scan(
-    got_ref, ext_ref, u2_ref, coarse_ref, smooth_ref, vert_ref, retain_ref, weight_ref,
-    pressure_ref, residual_ref, line, corr, ua, ub,
+    got_ref, own_ref, left_ref, right_ref, tails_ref, u2_ref, own_coarse_ref, deep_left, deep_right, smooth_ref, vert_ref, retain_ref, weight_ref,
+    pressure_ref, residual_ref, coarse_ref, line, corr, ua, ub,
 ):
+    left_rows, left_coarse = unpack_deep(deep_left)
+    right_rows, right_coarse = unpack_deep(deep_right)
+    for j in range(2):
+        coarse_ref[j] = left_coarse[j]
+        coarse_ref[6 + j] = right_coarse[j]
+    for j in range(4):
+        coarse_ref[2 + j] = own_coarse_ref[j]
     retain, weight = wide3(retain_ref[...]), wide3(weight_ref[...])
     inv_retain = 1.0 / retain
     coarse_lane = lax.broadcasted_iota(jnp.int32, (256, LX), 0)
@@ -294,12 +365,21 @@
         ],
         axis=0,
     )
-    both = jnp.dot(both, spread, precision=lax.Precision.HIGHEST, preferred_element_type=f32)
+    both = select(both, spread)
+
+    def row(r, levels=K):
+        return whole_row(own_ref, left_ref, right_ref, tails_ref, r, levels)
 
     def coef(j):
-        r = 2 * j + HX - 4
-        return 0.0625 * pair_sum(ext_ref[r, K : K + 1, :] + ext_ref[r + 1, K : K + 1, :])
-
+        if j == 0:
+            pair = row(0, K + 1)[1] + row(1, K + 1)[1]
+        elif j == 7:
+            pair = row(NR - 2, K + 1)[1] + row(NR - 1, K + 1)[1]
+        else:
+            pair = row(2 * j + HX - 4)[1] + row(2 * j + HX - 3)[1]
+        return 0.0625 * pair_sum(pair)
+
+    coefs = [coef(j) for j in range(8)]
     enter, leave = both[:K], both[K:]
     reach = leave
     for j in (4, 5):
@@ -312,9 +392,9 @@
         line[j + 3] = reach
     ahead = (enter - coarse_ref[1]) * inv_retain
     ahead = (ahead - coarse_ref[0]) * inv_retain
-    line[0] = jnp.where(coef(0) > 0.0, weight * (ahead + retain * line[1]), 0.0)
+    line[0] = jnp.where(coefs[0] > 0.0, weight * (ahead + retain * line[1]), 0.0)
     for j in range(-2, 7):
-        inside = coef(min(max(j + 2, 0), 7)) > 0.0
+        inside = coefs[min(max(j + 2, 0), 7)] > 0.0
         start = retain * ahead
         line[j + 3] = jnp.where(inside, weight * (start + line[j + 3]), 0.0)
         if j < 6:
@@ -322,32 +402,25 @@
 
     smooth = smooth_ref[...]
 
-    def coarse(j, _):
+    for j in range(8):
         v = line[j + 1]
-        area = coef(j)
-        term = smooth_term(v, coarse_ref[j] + 4.0 * v, area, line[j], line[j + 2], 2)
+        term = smooth_term(v, coarse_ref[j] + 4.0 * v, coefs[j], line[j], line[j + 2], 2)
         corr[j] = 0.6 * v + apply3(smooth, term)
-        return 0
-
-    lax.fori_loop(0, 8, coarse, 0)
     for i in range(14):
-        ua[i] = u2_ref[i] + corr[(i - 3) // 2 + 2]
-
-    def smoothing(source, target, i):
-        u = source[i]
-        r = i + HX - 3
-        term = smooth_term(u, ext_ref[r, :K, :] + 4.0 * u, ext_ref[r, K : K + 1, :], source[i - 1], source[i + 1], 1)
-        target[i] = 0.6 * u + apply3(smooth, term)
-        return 0
-
-    lax.fori_loop(1, 13, lambda i, _: smoothing(ua, ub, i), 0, unroll=2)
-    lax.fori_loop(2, 12, lambda i, _: smoothing(ub, ua, i), 0, unroll=2)
+        field = left_rows[i] if i < 3 else right_rows[i - 11] if i >= 11 else u2_ref[i - 3]
+        ua[i] = field + corr[(i - 3) // 2 + 2]
+
+    for source, target, least, most in ((ua, ub, 1, 13), (ub, ua, 2, 12)):
+        for i in range(least, most):
+            u, (rhs, area) = source[i], row(i + HX - 3)
+            term = smooth_term(u, rhs + 4.0 * u, area, source[i - 1], source[i + 1], 1)
+            target[i] = 0.6 * u + apply3(smooth, term)
     vert = vert_ref[...]
     for x in range(8):
         i = x + 3
         u = ua[i]
-        r = x + HX
-        term = smooth_term(u, ext_ref[r, :K, :], ext_ref[r, K : K + 1, :], ua[i - 1], ua[i + 1], 1)
+        rhs, area = row(x + HX)
+        term = smooth_term(u, rhs, area, ua[i - 1], ua[i + 1], 1)
         rest = term[:, :256] - apply3(vert, u[:, :256])
         for t in range(2):
             here = pl.ds(8 * t + x, K, stride=16)
@@ -359,7 +432,13 @@
     wide, narrow = lax.axis_size("wide"), lax.axis_size("narrow")
     planes = wide // PLANE
     rhs = rhs.reshape(K, 8, 2, 128).transpose(0, 2, 1, 3).reshape(K * 16, 128)
-    up, down = call(pack_x, [((HX, KA, 256), f32)] * 2, specs=on_vmem(2))(rhs, areas)
+    anywhere = [pl.BlockSpec(memory_space=pltpu.HBM)] * 2
+    up, down, own = call(
+        pack_x,
+        [((HX, KA, 256), f32)] * 2 + [((8, KA, 256), f32)],
+        [pltpu.VMEM((K * 16, 128), f32), pltpu.VMEM((8, 256), f32), pltpu.SemaphoreType.DMA((2,))],
+        anywhere,
+    )(rhs, areas)
 
     def shift(array, axis, count, by):
         pairs = [(i, i + by) for i in range(count) if 0 <= i + by < count]
@@ -373,15 +452,16 @@
         [pltpu.VMEM((K, 128), f32)] * 2,
         [pl.BlockSpec(memory_space=pltpu.SMEM)],
     )(stiffness)
-    low, high = call(pack_y, [((KA, YP), f32)] * 2, specs=on_vmem(4))(rhs, areas, left, right)
-    from_left = shift(high, "narrow", narrow, 1)
-    from_right = shift(low, "narrow", narrow, -1)
-    sent, ext, u2, coarse = call(
+    first, second = call(pack_y, [((KA, 128), f32)] * 2, specs=on_vmem(4))(own, left, right, retain)
+    first = lax.ppermute(first, "narrow", [(i, i ^ 1) for i in range(narrow)])
+    second = lax.ppermute(second, "narrow", [(i, ((i + 1) ^ 1) - 1) for i in range(1, narrow - 1)])
+    (u1,) = call(first_main, [((NR, K, 256), f32)], specs=on_vmem(4))(own, left, right, smooth)
+    sent, tails, u2, coarse = call(
         before_scan,
-        [((K, LX), f32), ((NR, KA, LX), f32), ((14, K, LX), f32), ((8, K, LX), f32)],
-        [pltpu.VMEM((NR, K, LX), f32)] * 2,
+        K2_OUTS,
+        K2_SCRATCH,
         on_vmem(9),
-    )(rhs, areas, left, right, from_left, from_right, smooth, vert, retain)
+    )(own, left, right, first, second, u1, smooth, vert, retain)
     in_plane = [[p * PLANE + m for m in range(PLANE)] for p in range(planes)]
     over_planes = [[p * PLANE + m for p in range(planes)] for m in range(PLANE)]
 
@@ -389,6 +469,11 @@
         return lax.all_to_all(array, "wide", 0, 0, tiled=True, axis_index_groups=groups)
 
     blocks = exchange(sent.reshape(PLANE, 8, LX), in_plane)
+    if DEEP_LATE:
+        blocks, u2, coarse = lax.optimization_barrier((blocks, u2, coarse))
+    deep_up, deep_down = call(pack_deep, [((9, K, 128), f32)] * 2, specs=on_vmem(2))(u2, coarse)
+    deep_left = shift(deep_up, "wide", wide, 1)
+    deep_right = shift(deep_down, "wide", wide, -1)
     (out,) = call(functools.partial(across_out, planes), [((planes, 8, 256), f32)], specs=on_vmem(2))(blocks, retain)
     others = exchange(out, over_planes)
     (back,) = call(functools.partial(across_in, planes), [((PLANE, 8, LX), f32)], specs=on_vmem(3))(
@@ -398,9 +483,9 @@
     pressure, residual = call(
         after_scan,
         [((K * 16, 128), f32)] * 2,
-        [pltpu.VMEM((10, K, LX), f32), pltpu.VMEM((8, K, LX), f32)] + [pltpu.VMEM((14, K, LX), f32)] * 2,
-        on_vmem(8),
-    )(got, ext, u2, coarse, smooth, vert, retain, weight)
+        K4_SCRATCH,
+        on_vmem(13),
+    )(got, own, left, right, tails, u2, coarse, deep_left, deep_right, smooth, vert, retain, weight)
     return tuple(
         out.reshape(K, 2, 8, 128).transpose(0, 2, 1, 3).reshape(K, 8, 256) for out in (pressure, residual)
     )

time: 104 us -> 83.9 us (0.81)
  the two profiles are of different devices: /device:TPU:1 before, /device:TPU:16 now
where the time goes in v2:
time: 83.9 us; the launch traced here: 83.3 us
  starting transfers between devices  34.6 us (41%)
  waiting for transfers between devices  20.7 us (25%)
  blocking collectives  14.1 us (17%)
  Pallas kernels  11.4 us (14%)
  local copies, waits for them, and re-layouts  1.74 us (2%)
    all_to_all x2, starting transfers between devices, exchange(): lax.all_to_all(array, 'wide', 0, 0, tiled=True, axis_index_groups=groups)  18.4 us
    all_to_all x2, waiting for transfers between devices, exchange(): lax.all_to_all(array, 'wide', 0, 0, tiled=True, axis_index_groups=groups)  14.4 us
    all_to_all x1, blocking collectives, exchange(): lax.all_to_all(array, 'wide', 0, 0, tiled=True, axis_index_groups=groups)  14.1 us
    ppermute x4, starting transfers between devices, shift(): return lax.ppermute(array, axis, pairs)  8.65 us
    ppermute x1, starting transfers between devices, local(): lax.ppermute(second, 'narrow', [(i, (i + 1 ^ 1) - 1) for i in range(1, na...  5.66 us
    ppermute x4, waiting for transfers between devices, shift(): return lax.ppermute(array, axis, pairs)  5.07 us
    pallas_call x1, Pallas kernels, local(): call(after_scan, [((K * 16, 128), f32)] * 2, K4_SCRATCH, on_vmem(13))  4.57 us
    pallas_call x1, Pallas kernels, local(): call(before_scan, K2_OUTS, K2_SCRATCH, on_vmem(9))  2.64 us
  transfers between devices with their start and end apart: 8, of which 5 were waited for; matrix products, arithmetic and copies ran while one was open for 0% of the time, Pallas kernels for 3%

profile of v2, /device:TPU:16, one launch (start us, length us, event | category | flops | bytes accessed | tf_op | source)
XLA Modules:
  0.0 83.3 jit_solution(17454055354181480103)
XLA Ops:
  0.6 0.0 copy-start
  0.6 1.0 %copy-done = f32[64,8,256]{2,1,0:T(8,128)S(1)} copy-done((f32[64,8,256]{2,1,0:T(8,128)S(1)}, f32[64,8,256]{2,1,0:T(8,128)}, u32[]{:S(2)}) %copy-start) | copy-done | bytes 524312
  1.7 0.0 copy-start.1
  1.7 0.7 copy-done.1
  2.4 0.2 shard_map.50
  2.6 0.0 copy-start.2
  2.6 3.2 %collective-permute-start = (f32[2,72,256]{2,1,0:T(8,128)S(1)}, f32[2,72,256]{2,1,0:T(8,128)S(1)}, u32[]{:S(2)}, u32[]{:S(2)}) collective-permute-start(f32[2,72,256]{2,1,0:T(8,128)S(1)} %get-tuple-element.23), channel_id=1, source_target_pairs={{0,4},{4,8},{8,12},{12,16},{16,20},{20,24},{24,28},{28,32},{32,36}... | collective-permute-start | bytes 442376 | tf_op jit(solution)/shard_map/ppermute | solution.py:445
  5.8 1.3 %collective-permute-start.1 = (f32[2,72,256]{2,1,0:T(8,128)S(1)}, f32[2,72,256]{2,1,0:T(8,128)S(1)}, u32[]{:S(2)}, u32[]{:S(2)}) collective-permute-start(f32[2,72,256]{2,1,0:T(8,128)S(1)} %get-tuple-element.24), channel_id=1, source_target_pairs={{4,0},{8,4},{12,8},{16,12},{20,16},{24,20},{28,24},{32,28},{36,32}... | collective-permute-start | bytes 442376 | tf_op jit(solution)/shard_map/ppermute | solution.py:445
  7.1 0.0 copy-done.2
  7.1 0.8 shard_map.51
  8.0 0.9 %collective-permute-done.left_ref = f32[2,72,256]{2,1,0:T(8,128)S(1)} collective-permute-done((f32[2,72,256]{2,1,0:T(8,128)S(1)}, f32[2,72,256]{2,1,0:T(8,128)S(1)}, u32[]{:S(2)}, u32[]{:S(2)}) %collective-permute-start) | collective-permute-done | bytes 147488 | tf_op jit(solution)/shard_map/ppermute | solution.py:445
  8.9 4.1 %collective-permute-done.1.right_ref = f32[2,72,256]{2,1,0:T(8,128)S(1)} collective-permute-done((f32[2,72,256]{2,1,0:T(8,128)S(1)}, f32[2,72,256]{2,1,0:T(8,128)S(1)}, u32[]{:S(2)}, u32[]{:S(2)}) %collective-permute-start.1) | collective-permute-done | bytes 147488 | tf_op jit(solution)/shard_map/ppermute | solution.py:445
  13.0 0.3 shard_map.52
  13.3 1.9 %collective-permute-start.2 = (f32[72,128]{1,0:T(8,128)S(1)}, f32[72,128]{1,0:T(8,128)S(1)}, u32[]{:S(2)}, u32[]{:S(2)}) collective-permute-start(f32[72,128]{1,0:T(8,128)S(1)} %get-tuple-element.26), channel_id=1, source_target_pairs={{0,1},{1,0},{2,3},{3,2},{4,5},{5,4},{6,7},{7,6},{8,9},{9,8},{10,11... | collective-permute-start | bytes 110600 | tf_op jit(solution)/shard_map/ppermute | solution.py:456
  15.3 5.7 %collective-permute-start.3 = (f32[72,128]{1,0:T(8,128)S(1)}, f32[72,128]{1,0:T(8,128)S(1)}, u32[]{:S(2)}, u32[]{:S(2)}) collective-permute-start(f32[72,128]{1,0:T(8,128)S(1)} %get-tuple-element.27), channel_id=1, source_target_pairs={{1,2},{2,1},{5,6},{6,5},{9,10},{10,9},{13,14},{14,13},{17,18},{18,... | collective-permute-start | bytes 110600 | tf_op jit(solution)/shard_map/ppermute | solution.py:457
  20.9 0.3 shard_map.53.u1_ref
  21.3 0.0 collective-permute-done.2.first_ref
  21.3 1.3 %collective-permute-done.3.second_ref = f32[72,128]{1,0:T(8,128)S(1)} collective-permute-done((f32[72,128]{1,0:T(8,128)S(1)}, f32[72,128]{1,0:T(8,128)S(1)}, u32[]{:S(2)}, u32[]{:S(2)}) %collective-permute-start.3) | collective-permute-done | bytes 36896 | tf_op jit(solution)/shard_map/ppermute | solution.py:457
  22.5 2.6 %shard_map.54 = (f32[64,384]{1,0:T(8,128)S(1)}, f32[12,72,128]{2,1,0:T(8,128)S(1)}, f32[8,64,384]{2,1,0:T(8,128)S(1)}, f32[4,64,384]{2,1,0:T(8,128)S(1)}) custom-call(f32[8,72,256]{2,1,0:T(8,128)S(1)} %get-tuple-element.22.own_ref, f32[2,72,256]{2,1,0:T(8,128)S(1)} %collective-permute-done.left_ref, f32[2,72,256]{2,1,0:T(8,128)S(1)} %collective-permute-done.1.right_ref, ...), custom_call_target="tpu_custom_call" | custom-call | tf_op jit(solution)/shard_map/pallas_call | solution.py:459
  25.2 14.1 %all_to_all.15.blocks_ref = f32[8,8,384]{2,1,0:T(8,128)S(1)} all-to-all(f32[8,8,384]{2,1,0:T(8,128)S(1)} %bitcast.19), channel_id=1, replica_groups={{0,4,8,12,16,20,24,28},{32,36,40,44,48,52,56,60},{64,68,72,76,80,84,88,..., dimensions={0} | all-to-all | bytes 196608 | tf_op jit(solution)/shard_map/all_to_all | solution.py:469
  39.3 0.8 shard_map.55
  40.0 15.1 %all-to-all-start.1 = ((f32[16,8,256]{2,1,0:T(8,128)}), f32[16,8,256]{2,1,0:T(8,128)S(1)}, u32[]{:S(2)}, u32[]{:S(2)}) async-start(f32[16,8,256]{2,1,0:T(8,128)} %shard_map.55), calls=%async_computation.1 | async-start | bytes 262144 | tf_op jit(solution)/shard_map/all_to_all | solution.py:469
  55.1 0.9 %shard_map.57 = (f32[9,64,128]{2,1,0:T(8,128)}, f32[9,64,128]{2,1,0:T(8,128)}) custom-call(f32[8,64,384]{2,1,0:T(8,128)S(1)} %get-tuple-element.35.u2_ref, f32[4,64,384]{2,1,0:T(8,128)S(1)} %get-tuple-element.36.coarse_ref.own_coarse_ref), custom_call_target="tpu_custom_call" | custom-call | tf_op jit(solution)/shard_map/pallas_call | solution.py:474
  56.0 2.9 %collective-permute-start.4 = (f32[9,64,128]{2,1,0:T(8,128)}, f32[9,64,128]{2,1,0:T(8,128)S(1)}, u32[]{:S(2)}, u32[]{:S(2)}) collective-permute-start(f32[9,64,128]{2,1,0:T(8,128)} %get-tuple-element.37), channel_id=1, source_target_pairs={{0,4},{4,8},{8,12},{12,16},{16,20},{20,24},{24,28},{28,32},{32,36}... | collective-permute-start | bytes 884744 | tf_op jit(solution)/shard_map/ppermute | solution.py:445
  58.9 1.3 %collective-permute-start.5 = (f32[9,64,128]{2,1,0:T(8,128)}, f32[9,64,128]{2,1,0:T(8,128)S(1)}, u32[]{:S(2)}, u32[]{:S(2)}) collective-permute-start(f32[9,64,128]{2,1,0:T(8,128)} %get-tuple-element.38), channel_id=1, source_target_pairs={{4,0},{8,4},{12,8},{16,12},{20,16},{24,20},{28,24},{32,28},{36,32}... | collective-permute-start | bytes 884744 | tf_op jit(solution)/shard_map/ppermute | solution.py:445
  60.2 8.1 %all-to-all-done.1.others_ref = f32[16,8,256]{2,1,0:T(8,128)S(1)} async-done(((f32[16,8,256]{2,1,0:T(8,128)}), f32[16,8,256]{2,1,0:T(8,128)S(1)}, u32[]{:S(2)}, u32[]{:S(2)}) %all-to-all-start.1) | async-done | bytes 131104 | tf_op jit(solution)/shard_map/all_to_all | solution.py:469
  68.3 0.8 shard_map.56
  69.1 3.4 %all-to-all-start.2 = ((f32[8,8,384]{2,1,0:T(8,128)}), f32[8,8,384]{2,1,0:T(8,128)S(1)}, u32[]{:S(2)}, u32[]{:S(2)}) async-start(f32[8,8,384]{2,1,0:T(8,128)} %shard_map.56), calls=%async_computation.2 | async-start | bytes 196608 | tf_op jit(solution)/shard_map/all_to_all | solution.py:469
  72.5 0.0 collective-permute-done.4.deep_left
  72.5 0.0 collective-permute-done.5.deep_right
  72.5 6.3 %all-to-all-done.2 = f32[8,8,384]{2,1,0:T(8,128)S(1)} async-done(((f32[8,8,384]{2,1,0:T(8,128)}), f32[8,8,384]{2,1,0:T(8,128)S(1)}, u32[]{:S(2)}, u32[]{:S(2)}) %all-to-all-start.2) | async-done | bytes 98336 | tf_op jit(solution)/shard_map/all_to_all | solution.py:469
  78.8 4.6 %shard_map.58 = (f32[1024,128]{1,0:T(8,128)}, f32[1024,128]{1,0:T(8,128)}) custom-call(f32[64,384]{1,0:T(8,128)S(1)} %bitcast.18, f32[8,72,256]{2,1,0:T(8,128)S(1)} %get-tuple-element.22.own_ref, f32[2,72,256]{2,1,0:T(8,128)S(1)} %collective-permute-done.left_ref, f32[2,72,256]{2,1,0:T(8,128)S(1)} %collective-permute-done.1.right_ref, ...), custom_call_target="tpu_custom_call" | custom-call | tf_op jit(solution)/shard_map/pallas_call | solution.py:483
Async XLA Ops:
  0.6 1.0 %copy-start = (f32[64,8,256]{2,1,0:T(8,128)S(1)}, f32[64,8,256]{2,1,0:T(8,128)}, u32[]{:S(2)}) copy-start(f32[64,8,256]{2,1,0:T(8,128)} %param.3) | copy-start | bytes 1572868
  1.7 0.7 copy-start.1
  2.6 4.5 %copy-start.2 = (f32[64]{0:T(128)S(1)}, f32[64]{0:T(128)}, u32[]{:S(2)}) copy-start(f32[64]{0:T(128)} %stiff_ref.1) | copy-start | bytes 772
  2.6 6.3 %collective-permute-start = (f32[2,72,256]{2,1,0:T(8,128)S(1)}, f32[2,72,256]{2,1,0:T(8,128)S(1)}, u32[]{:S(2)}, u32[]{:S(2)}) collective-permute-start(f32[2,72,256]{2,1,0:T(8,128)S(1)} %get-tuple-element.23), channel_id=1, source_target_pairs={{0,4},{4,8},{8,12},{12,16},{16,20},{20,24},{24,28},{28,32},{32,36}... | collective-permute-start | bytes 442376 | tf_op jit(solution)/shard_map/ppermute | solution.py:445
  5.8 7.2 %collective-permute-start.1 = (f32[2,72,256]{2,1,0:T(8,128)S(1)}, f32[2,72,256]{2,1,0:T(8,128)S(1)}, u32[]{:S(2)}, u32[]{:S(2)}) collective-permute-start(f32[2,72,256]{2,1,0:T(8,128)S(1)} %get-tuple-element.24), channel_id=1, source_target_pairs={{4,0},{8,4},{12,8},{16,12},{20,16},{24,20},{28,24},{32,28},{36,32}... | collective-permute-start | bytes 442376 | tf_op jit(solution)/shard_map/ppermute | solution.py:445
  13.3 7.9 %collective-permute-start.2 = (f32[72,128]{1,0:T(8,128)S(1)}, f32[72,128]{1,0:T(8,128)S(1)}, u32[]{:S(2)}, u32[]{:S(2)}) collective-permute-start(f32[72,128]{1,0:T(8,128)S(1)} %get-tuple-element.26), channel_id=1, source_target_pairs={{0,1},{1,0},{2,3},{3,2},{4,5},{5,4},{6,7},{7,6},{8,9},{9,8},{10,11... | collective-permute-start | bytes 110600 | tf_op jit(solution)/shard_map/ppermute | solution.py:456
  15.3 7.3 %collective-permute-start.3 = (f32[72,128]{1,0:T(8,128)S(1)}, f32[72,128]{1,0:T(8,128)S(1)}, u32[]{:S(2)}, u32[]{:S(2)}) collective-permute-start(f32[72,128]{1,0:T(8,128)S(1)} %get-tuple-element.27), channel_id=1, source_target_pairs={{1,2},{2,1},{5,6},{6,5},{9,10},{10,9},{13,14},{14,13},{17,18},{18,... | collective-permute-start | bytes 110600 | tf_op jit(solution)/shard_map/ppermute | solution.py:457
  40.0 28.3 %all-to-all-start.1 = ((f32[16,8,256]{2,1,0:T(8,128)}), f32[16,8,256]{2,1,0:T(8,128)S(1)}, u32[]{:S(2)}, u32[]{:S(2)}) async-start(f32[16,8,256]{2,1,0:T(8,128)} %shard_map.55), calls=%async_computation.1 | async-start | bytes 262144 | tf_op jit(solution)/shard_map/all_to_all | solution.py:469
  56.0 16.5 %collective-permute-start.4 = (f32[9,64,128]{2,1,0:T(8,128)}, f32[9,64,128]{2,1,0:T(8,128)S(1)}, u32[]{:S(2)}, u32[]{:S(2)}) collective-permute-start(f32[9,64,128]{2,1,0:T(8,128)} %get-tuple-element.37), channel_id=1, source_target_pairs={{0,4},{4,8},{8,12},{12,16},{16,20},{20,24},{24,28},{28,32},{32,36}... | collective-permute-start | bytes 884744 | tf_op jit(solution)/shard_map/ppermute | solution.py:445
  58.9 13.6 %collective-permute-start.5 = (f32[9,64,128]{2,1,0:T(8,128)}, f32[9,64,128]{2,1,0:T(8,128)S(1)}, u32[]{:S(2)}, u32[]{:S(2)}) collective-permute-start(f32[9,64,128]{2,1,0:T(8,128)} %get-tuple-element.38), channel_id=1, source_target_pairs={{4,0},{8,4},{12,8},{16,12},{20,16},{24,20},{28,24},{32,28},{36,32}... | collective-permute-start | bytes 884744 | tf_op jit(solution)/shard_map/ppermute | solution.py:445
  69.1 9.7 %all-to-all-start.2 = ((f32[8,8,384]{2,1,0:T(8,128)}), f32[8,8,384]{2,1,0:T(8,128)S(1)}, u32[]{:S(2)}, u32[]{:S(2)}) async-start(f32[8,8,384]{2,1,0:T(8,128)} %shard_map.56), calls=%async_computation.2 | async-start | bytes 196608 | tf_op jit(solution)/shard_map/all_to_all | solution.py:469

commit v3 on v2

--- a/solution.py
+++ b/solution.py
@@ -68,7 +68,7 @@
     return jnp.concatenate([high, low, high], axis=1)
 
 
-def pack_x(rhs_hbm, areas_hbm, up_ref, down_ref, own_ref, rhs, areas, sems):
+def pack_x(rhs_hbm, areas_hbm, first_ref, second_ref, own_ref, rhs, areas, sems):
     copies = [
         pltpu.make_async_copy(rhs_hbm, rhs, sems.at[0]),
         pltpu.make_async_copy(areas_hbm, areas, sems.at[1]),
@@ -86,12 +86,14 @@
         for t in range(2):
             own_ref[x, :K, 128 * t : 128 * t + 128] = rhs[pl.ds(8 * t + x, K, stride=16), :]
         own_ref[x, K:, :] = area(x, x)
-        if x < HX:
-            down_ref[x, :K, :] = own_ref[x, :K, :]
-            down_ref[x, K:, :] = area(x, x + HX)
-        if x >= 8 - HX:
-            up_ref[x - 8 + HX, :K, :] = own_ref[x, :K, :]
-            up_ref[x - 8 + HX, K:, :] = area(x, x - HX)
+    even = lax.rem(lax.axis_index("wide"), 2) == 0
+    for x in range(HX):
+        up, down = own_ref[8 - HX + x, :K, :], own_ref[x, :K, :]
+        up_area, down_area = area(8 - HX + x, 8 - 2 * HX + x), area(x, x + HX)
+        first_ref[x, :K, :] = jnp.where(even, up, down)
+        first_ref[x, K:, :] = jnp.where(even, up_area, down_area)
+        second_ref[x, :K, :] = jnp.where(even, down, up)
+        second_ref[x, K:, :] = jnp.where(even, down_area, up_area)
 
 
 def tables(stiff_ref, smooth_ref, vert_ref, retain_ref, weight_ref, lead, trail):
@@ -149,7 +151,10 @@
     )
 
 
-def pack_y(own_ref, left_ref, right_ref, _, first_ref, second_ref):
+def pack_y(own_ref, x_second_ref, x_first_ref, _, first_ref, second_ref, left_ref, right_ref):
+    even = lax.rem(lax.axis_index("wide"), 2) == 0
+    left_ref[...] = jnp.where(even, x_second_ref[...], x_first_ref[...])
+    right_ref[...] = jnp.where(even, x_first_ref[...], x_second_ref[...])
     lane = lanes((KA, 128))
     low = high = jnp.zeros((KA, 128), f32)
     for r in range(NR):
@@ -212,7 +217,7 @@
 
 
 def before_scan(
-    own_ref, left_ref, right_ref, first_ref, second_ref, u1_ref, smooth_ref, vert_ref, retain_ref,
+    own_ref, left_ref, right_ref, second_ref, first_ref, u1_ref, smooth_ref, vert_ref, retain_ref,
     sent_ref, tails_ref, u2_ref, coarse_ref, u1, fine,
 ):
     smooth = smooth_ref[...]
@@ -440,28 +445,32 @@
         anywhere,
     )(rhs, areas)
 
+    def in_pairs(first, second, axis, count):
+        second = lax.ppermute(second, axis, [(i, ((i + 1) ^ 1) - 1) for i in range(1, count - 1)])
+        return lax.ppermute(first, axis, [(i, i ^ 1) for i in range(count)]), second
+
     def shift(array, axis, count, by):
         pairs = [(i, i + by) for i in range(count) if 0 <= i + by < count]
         return lax.ppermute(array, axis, pairs)
 
-    left = shift(up, "wide", wide, 1)
-    right = shift(down, "wide", wide, -1)
+    x_first, x_second = in_pairs(up, down, "wide", wide)
     smooth, vert, retain, weight = call(
         tables,
         [((K, 192), bf16)] * 2 + [((K, 128), f32)] * 2,
         [pltpu.VMEM((K, 128), f32)] * 2,
         [pl.BlockSpec(memory_space=pltpu.SMEM)],
     )(stiffness)
-    first, second = call(pack_y, [((KA, 128), f32)] * 2, specs=on_vmem(4))(own, left, right, retain)
-    first = lax.ppermute(first, "narrow", [(i, i ^ 1) for i in range(narrow)])
-    second = lax.ppermute(second, "narrow", [(i, ((i + 1) ^ 1) - 1) for i in range(1, narrow - 1)])
+    first, second, left, right = call(
+        pack_y, [((KA, 128), f32)] * 2 + [((HX, KA, 256), f32)] * 2, specs=on_vmem(4)
+    )(own, x_second, x_first, retain)
+    first, second = in_pairs(first, second, "narrow", narrow)
     (u1,) = call(first_main, [((NR, K, 256), f32)], specs=on_vmem(4))(own, left, right, smooth)
     sent, tails, u2, coarse = call(
         before_scan,
         K2_OUTS,
         K2_SCRATCH,
         on_vmem(9),
-    )(own, left, right, first, second, u1, smooth, vert, retain)
+    )(own, left, right, second, first, u1, smooth, vert, retain)
     in_plane = [[p * PLANE + m for m in range(PLANE)] for p in range(planes)]
     over_planes = [[p * PLANE + m for p in range(planes)] for m in range(PLANE)]
 

time: 83.9 us -> 82 us (0.977)
  the two profiles are of different devices: /device:TPU:16 before, /device:TPU:8 now
where the time goes in v3:
time: 82 us; the launch traced here: 81.5 us
  starting transfers between devices  39.6 us (48%)
  waiting for transfers between devices  15.4 us (19%)
  blocking collectives  12.6 us (15%)
  Pallas kernels  11.4 us (14%)
  local copies, waits for them, and re-layouts  1.74 us (2%)
    all_to_all x2, starting transfers between devices, exchange(): lax.all_to_all(array, 'wide', 0, 0, tiled=True, axis_index_groups=groups)  19.1 us
    all_to_all x1, blocking collectives, exchange(): lax.all_to_all(array, 'wide', 0, 0, tiled=True, axis_index_groups=groups)  12.6 us
    all_to_all x2, waiting for transfers between devices, exchange(): lax.all_to_all(array, 'wide', 0, 0, tiled=True, axis_index_groups=groups)  12.6 us
    ppermute x2, starting transfers between devices, in_pairs(): lax.ppermute(first, axis, [(i, i ^ 1) for i in range(count)])  10.7 us
    ppermute x2, starting transfers between devices, shift(): return lax.ppermute(array, axis, pairs)  5.84 us
    pallas_call x1, Pallas kernels, local(): call(after_scan, [((K * 16, 128), f32)] * 2, K4_SCRATCH, on_vmem(13))  4.57 us
    ppermute x2, starting transfers between devices, in_pairs(): lax.ppermute(second, axis, [(i, (i + 1 ^ 1) - 1) for i in range(1, count...  3.95 us
    ppermute x2, waiting for transfers between devices, in_pairs(): lax.ppermute(first, axis, [(i, i ^ 1) for i in range(count)])  2.77 us
  transfers between devices with their start and end apart: 8, of which 4 were waited for; matrix products, arithmetic and copies ran while one was open for 0% of the time, Pallas kernels for 4%

profile of v3, /device:TPU:8, one launch (start us, length us, event | category | flops | bytes accessed | tf_op | source)
XLA Modules:
  0.0 81.5 jit_solution(1003537459490125321)
XLA Ops:
  0.6 0.0 copy-start
  0.6 1.0 %copy-done = f32[64,8,256]{2,1,0:T(8,128)S(1)} copy-done((f32[64,8,256]{2,1,0:T(8,128)S(1)}, f32[64,8,256]{2,1,0:T(8,128)}, u32[]{:S(2)}) %copy-start) | copy-done | bytes 524312
  1.7 0.0 copy-start.1
  1.7 0.7 copy-done.1
  2.4 0.2 shard_map.50
  2.6 0.0 copy-start.2
  2.6 3.3 %collective-permute-start = (f32[2,72,256]{2,1,0:T(8,128)S(1)}, f32[2,72,256]{2,1,0:T(8,128)S(1)}, u32[]{:S(2)}, u32[]{:S(2)}) collective-permute-start(f32[2,72,256]{2,1,0:T(8,128)S(1)} %get-tuple-element.25), channel_id=1, source_target_pairs={{4,8},{8,4},{12,16},{16,12},{20,24},{24,20},{28,32},{32,28},{36,40... | collective-permute-start | bytes 442376 | tf_op jit(solution)/shard_map/ppermute | solution.py:449
  5.9 5.1 %collective-permute-start.1 = (f32[2,72,256]{2,1,0:T(8,128)S(1)}, f32[2,72,256]{2,1,0:T(8,128)S(1)}, u32[]{:S(2)}, u32[]{:S(2)}) collective-permute-start(f32[2,72,256]{2,1,0:T(8,128)S(1)} %get-tuple-element.26), channel_id=1, source_target_pairs={{0,4},{4,0},{8,12},{12,8},{16,20},{20,16},{24,28},{28,24},{32,36},... | collective-permute-start | bytes 442376 | tf_op jit(solution)/shard_map/ppermute | solution.py:450
  11.1 0.0 copy-done.2
  11.1 0.8 %shard_map.51 = (bf16[64,192]{1,0:T(8,128)(2,1)S(1)}, bf16[64,192]{1,0:T(8,128)(2,1)S(1)}, f32[64,128]{1,0:T(8,128)S(1)}, f32[64,128]{1,0:T(8,128)S(1)}) custom-call(f32[64]{0:T(128)S(1)} %copy-done.2), custom_call_target="tpu_custom_call" | custom-call | tf_op jit(solution)/shard_map/pallas_call | solution.py:457
  11.9 0.0 collective-permute-done.x_second_ref
  11.9 2.3 %collective-permute-done.1.x_first_ref = f32[2,72,256]{2,1,0:T(8,128)S(1)} collective-permute-done((f32[2,72,256]{2,1,0:T(8,128)S(1)}, f32[2,72,256]{2,1,0:T(8,128)S(1)}, u32[]{:S(2)}, u32[]{:S(2)}) %collective-permute-start.1) | collective-permute-done | bytes 147488 | tf_op jit(solution)/shard_map/ppermute | solution.py:450
  14.2 0.3 shard_map.52
  14.5 0.7 collective-permute-start.2
  15.2 5.6 %collective-permute-start.3 = (f32[72,128]{1,0:T(8,128)S(1)}, f32[72,128]{1,0:T(8,128)S(1)}, u32[]{:S(2)}, u32[]{:S(2)}) collective-permute-start(f32[72,128]{1,0:T(8,128)S(1)} %get-tuple-element.31), channel_id=1, source_target_pairs={{0,1},{1,0},{2,3},{3,2},{4,5},{5,4},{6,7},{7,6},{8,9},{9,8},{10,11... | collective-permute-start | bytes 110600 | tf_op jit(solution)/shard_map/ppermute | solution.py:450
  20.7 0.3 shard_map.53.u1_ref
  21.1 0.0 collective-permute-done.2.second_ref
  21.1 0.5 collective-permute-done.3.first_ref
  21.6 2.6 %shard_map.54 = (f32[64,384]{1,0:T(8,128)S(1)}, f32[12,72,128]{2,1,0:T(8,128)S(1)}, f32[8,64,384]{2,1,0:T(8,128)S(1)}, f32[4,64,384]{2,1,0:T(8,128)S(1)}) custom-call(f32[8,72,256]{2,1,0:T(8,128)S(1)} %get-tuple-element.24.own_ref, f32[2,72,256]{2,1,0:T(8,128)S(1)} %get-tuple-element.28.left_ref, f32[2,72,256]{2,1,0:T(8,128)S(1)} %get-tuple-element.29.right_ref, ...), custom_call_target="tpu_custom_call" | custom-call | tf_op jit(solution)/shard_map/pallas_call | solution.py:468
  24.2 12.6 %all_to_all.15.blocks_ref = f32[8,8,384]{2,1,0:T(8,128)S(1)} all-to-all(f32[8,8,384]{2,1,0:T(8,128)S(1)} %bitcast.19), channel_id=1, replica_groups={{0,4,8,12,16,20,24,28},{32,36,40,44,48,52,56,60},{64,68,72,76,80,84,88,..., dimensions={0} | all-to-all | bytes 196608 | tf_op jit(solution)/shard_map/all_to_all | solution.py:478
  36.8 0.8 shard_map.55
  37.6 14.9 %all-to-all-start.1 = ((f32[16,8,256]{2,1,0:T(8,128)}), f32[16,8,256]{2,1,0:T(8,128)S(1)}, u32[]{:S(2)}, u32[]{:S(2)}) async-start(f32[16,8,256]{2,1,0:T(8,128)} %shard_map.55), calls=%async_computation.1 | async-start | bytes 262144 | tf_op jit(solution)/shard_map/all_to_all | solution.py:478
  52.6 0.9 %shard_map.57 = (f32[9,64,128]{2,1,0:T(8,128)}, f32[9,64,128]{2,1,0:T(8,128)}) custom-call(f32[8,64,384]{2,1,0:T(8,128)S(1)} %get-tuple-element.39.u2_ref, f32[4,64,384]{2,1,0:T(8,128)S(1)} %get-tuple-element.40.coarse_ref.own_coarse_ref), custom_call_target="tpu_custom_call" | custom-call | tf_op jit(solution)/shard_map/pallas_call | solution.py:483
  53.5 3.0 %collective-permute-start.4 = (f32[9,64,128]{2,1,0:T(8,128)}, f32[9,64,128]{2,1,0:T(8,128)S(1)}, u32[]{:S(2)}, u32[]{:S(2)}) collective-permute-start(f32[9,64,128]{2,1,0:T(8,128)} %get-tuple-element.41), channel_id=1, source_target_pairs={{0,4},{4,8},{8,12},{12,16},{16,20},{20,24},{24,28},{28,32},{32,36}... | collective-permute-start | bytes 884744 | tf_op jit(solution)/shard_map/ppermute | solution.py:454
  56.5 2.9 %collective-permute-start.5 = (f32[9,64,128]{2,1,0:T(8,128)}, f32[9,64,128]{2,1,0:T(8,128)S(1)}, u32[]{:S(2)}, u32[]{:S(2)}) collective-permute-start(f32[9,64,128]{2,1,0:T(8,128)} %get-tuple-element.42), channel_id=1, source_target_pairs={{4,0},{8,4},{12,8},{16,12},{20,16},{24,20},{28,24},{32,28},{36,32}... | collective-permute-start | bytes 884744 | tf_op jit(solution)/shard_map/ppermute | solution.py:454
  59.3 7.4 %all-to-all-done.1.others_ref = f32[16,8,256]{2,1,0:T(8,128)S(1)} async-done(((f32[16,8,256]{2,1,0:T(8,128)}), f32[16,8,256]{2,1,0:T(8,128)S(1)}, u32[]{:S(2)}, u32[]{:S(2)}) %all-to-all-start.1) | async-done | bytes 131104 | tf_op jit(solution)/shard_map/all_to_all | solution.py:478
  66.7 0.8 shard_map.56
  67.5 4.2 %all-to-all-start.2 = ((f32[8,8,384]{2,1,0:T(8,128)}), f32[8,8,384]{2,1,0:T(8,128)S(1)}, u32[]{:S(2)}, u32[]{:S(2)}) async-start(f32[8,8,384]{2,1,0:T(8,128)} %shard_map.56), calls=%async_computation.2 | async-start | bytes 196608 | tf_op jit(solution)/shard_map/all_to_all | solution.py:478
  71.7 0.0 collective-permute-done.4.deep_left
  71.7 0.0 collective-permute-done.5.deep_right
  71.7 5.3 %all-to-all-done.2 = f32[8,8,384]{2,1,0:T(8,128)S(1)} async-done(((f32[8,8,384]{2,1,0:T(8,128)}), f32[8,8,384]{2,1,0:T(8,128)S(1)}, u32[]{:S(2)}, u32[]{:S(2)}) %all-to-all-start.2) | async-done | bytes 98336 | tf_op jit(solution)/shard_map/all_to_all | solution.py:478
  76.9 4.6 %shard_map.58 = (f32[1024,128]{1,0:T(8,128)}, f32[1024,128]{1,0:T(8,128)}) custom-call(f32[64,384]{1,0:T(8,128)S(1)} %bitcast.18, f32[8,72,256]{2,1,0:T(8,128)S(1)} %get-tuple-element.24.own_ref, f32[2,72,256]{2,1,0:T(8,128)S(1)} %get-tuple-element.28.left_ref, f32[2,72,256]{2,1,0:T(8,128)S(1)} %get-tuple-element.29.right_ref, ...), custom_call_target="tpu_custom_call" | custom-call | tf_op jit(solution)/shard_map/pallas_call | solution.py:492
Async XLA Ops:
  0.6 1.0 %copy-start = (f32[64,8,256]{2,1,0:T(8,128)S(1)}, f32[64,8,256]{2,1,0:T(8,128)}, u32[]{:S(2)}) copy-start(f32[64,8,256]{2,1,0:T(8,128)} %param.3) | copy-start | bytes 1572868
  1.7 0.7 copy-start.1
  2.6 8.4 %copy-start.2 = (f32[64]{0:T(128)S(1)}, f32[64]{0:T(128)}, u32[]{:S(2)}) copy-start(f32[64]{0:T(128)} %stiff_ref.1) | copy-start | bytes 772
  2.6 9.3 %collective-permute-start = (f32[2,72,256]{2,1,0:T(8,128)S(1)}, f32[2,72,256]{2,1,0:T(8,128)S(1)}, u32[]{:S(2)}, u32[]{:S(2)}) collective-permute-start(f32[2,72,256]{2,1,0:T(8,128)S(1)} %get-tuple-element.25), channel_id=1, source_target_pairs={{4,8},{8,4},{12,16},{16,12},{20,24},{24,20},{28,32},{32,28},{36,40... | collective-permute-start | bytes 442376 | tf_op jit(solution)/shard_map/ppermute | solution.py:449
  5.9 8.2 %collective-permute-start.1 = (f32[2,72,256]{2,1,0:T(8,128)S(1)}, f32[2,72,256]{2,1,0:T(8,128)S(1)}, u32[]{:S(2)}, u32[]{:S(2)}) collective-permute-start(f32[2,72,256]{2,1,0:T(8,128)S(1)} %get-tuple-element.26), channel_id=1, source_target_pairs={{0,4},{4,0},{8,12},{12,8},{16,20},{20,16},{24,28},{28,24},{32,36},... | collective-permute-start | bytes 442376 | tf_op jit(solution)/shard_map/ppermute | solution.py:450
  14.5 6.6 %collective-permute-start.2 = (f32[72,128]{1,0:T(8,128)S(1)}, f32[72,128]{1,0:T(8,128)S(1)}, u32[]{:S(2)}, u32[]{:S(2)}) collective-permute-start(f32[72,128]{1,0:T(8,128)S(1)} %get-tuple-element.30), channel_id=1, source_target_pairs={{1,2},{2,1},{5,6},{6,5},{9,10},{10,9},{13,14},{14,13},{17,18},{18,... | collective-permute-start | bytes 110600 | tf_op jit(solution)/shard_map/ppermute | solution.py:449
  15.2 6.4 %collective-permute-start.3 = (f32[72,128]{1,0:T(8,128)S(1)}, f32[72,128]{1,0:T(8,128)S(1)}, u32[]{:S(2)}, u32[]{:S(2)}) collective-permute-start(f32[72,128]{1,0:T(8,128)S(1)} %get-tuple-element.31), channel_id=1, source_target_pairs={{0,1},{1,0},{2,3},{3,2},{4,5},{5,4},{6,7},{7,6},{8,9},{9,8},{10,11... | collective-permute-start | bytes 110600 | tf_op jit(solution)/shard_map/ppermute | solution.py:450
  37.6 29.1 %all-to-all-start.1 = ((f32[16,8,256]{2,1,0:T(8,128)}), f32[16,8,256]{2,1,0:T(8,128)S(1)}, u32[]{:S(2)}, u32[]{:S(2)}) async-start(f32[16,8,256]{2,1,0:T(8,128)} %shard_map.55), calls=%async_computation.1 | async-start | bytes 262144 | tf_op jit(solution)/shard_map/all_to_all | solution.py:478
  53.5 18.2 %collective-permute-start.4 = (f32[9,64,128]{2,1,0:T(8,128)}, f32[9,64,128]{2,1,0:T(8,128)S(1)}, u32[]{:S(2)}, u32[]{:S(2)}) collective-permute-start(f32[9,64,128]{2,1,0:T(8,128)} %get-tuple-element.41), channel_id=1, source_target_pairs={{0,4},{4,8},{8,12},{12,16},{16,20},{20,24},{24,28},{28,32},{32,36}... | collective-permute-start | bytes 884744 | tf_op jit(solution)/shard_map/ppermute | solution.py:454
  56.5 15.2 %collective-permute-start.5 = (f32[9,64,128]{2,1,0:T(8,128)}, f32[9,64,128]{2,1,0:T(8,128)S(1)}, u32[]{:S(2)}, u32[]{:S(2)}) collective-permute-start(f32[9,64,128]{2,1,0:T(8,128)} %get-tuple-element.42), channel_id=1, source_target_pairs={{4,0},{8,4},{12,8},{16,12},{20,16},{24,20},{28,24},{32,28},{36,32}... | collective-permute-start | bytes 884744 | tf_op jit(solution)/shard_map/ppermute | solution.py:454
  67.5 9.4 %all-to-all-start.2 = ((f32[8,8,384]{2,1,0:T(8,128)}), f32[8,8,384]{2,1,0:T(8,128)S(1)}, u32[]{:S(2)}, u32[]{:S(2)}) async-start(f32[8,8,384]{2,1,0:T(8,128)} %shard_map.56), calls=%async_computation.2 | async-start | bytes 196608 | tf_op jit(solution)/shard_map/all_to_all | solution.py:478

commit v4 on v3

--- a/solution.py
+++ b/solution.py
@@ -14,11 +14,15 @@
 NR = 8 + 2 * HX
 LX = 384
 PLANE = 8
+FIRST_M = 5
+FIRST_Z = 8
 f32, bf16 = jnp.float32, jnp.bfloat16
-DEEP_LATE = True
-K2_OUTS = [((K, LX), f32), ((NR, KA, 128), f32), ((8, K, LX), f32), ((4, K, LX), f32)]
-K2_SCRATCH = [pltpu.VMEM((NR, K, 128), f32), pltpu.VMEM((NR, K, LX), f32)]
-K4_SCRATCH = [pltpu.VMEM(s, f32) for s in ((8, K, LX), (10, K, LX), (8, K, LX), (14, K, LX), (14, K, LX))]
+K2_OUTS = [((K, LX), f32), ((10, K, LX), f32), ((2, K, LX), f32)]
+K2_SCRATCH = [pltpu.VMEM(s, f32) for s in ((NR, KA, 128), (NR, K, LX), (4, K, LX), (NR, K, 128))]
+K4_SCRATCH = [
+    pltpu.VMEM(s, f32)
+    for s in ((NR, KA, 128), (8, K, LX), (10, K, LX), (8, K, LX), (14, K, LX), (14, K, LX))
+]
 LIMIT = 16 * 1024 * 1024
 
 
@@ -184,58 +188,66 @@
     return v + jnp.where(even, pltpu.roll(v, LX - 1, 1), pltpu.roll(v, 1, 1))
 
 
-def pack_deep(u2_ref, coarse_ref, up_ref, down_ref):
-    pack_side([u2_ref[x] for x in (5, 6, 7)], [coarse_ref[2], coarse_ref[3]], up_ref)
-    pack_side([u2_ref[x] for x in (0, 1, 2)], [coarse_ref[0], coarse_ref[1]], down_ref)
-
-
-def pack_side(rows, coarse, out_ref):
+def y_sides(first_ref, second_ref):
+    even = lax.rem(lax.axis_index("narrow"), 2) == 0
+    first, second = first_ref[...], second_ref[...]
+    return jnp.where(even, first, second), jnp.where(even, second, first)
+
+
+def beyond(right, left, r):
+    lane = lanes(right.shape)
+    right = pltpu.roll(right, (128 - HY * r) % 128, 1)
+    left = pltpu.roll(left, 128 - HY - HY * r, 1)
+    return jnp.where(lane < HY, right, jnp.where(lane >= 128 - HY, left, 0.0))
+
+
+def pack_deep(u2_ref, both_ref, first_ref, second_ref):
     lane = lanes((K, 128))
-    even = lanes((K, LX)) % 2 == 0
-    rows = rows + [jnp.where(even, coarse[0], coarse[1])]
-    tails = jnp.zeros((K, 128), f32)
-    for i, row in enumerate(rows):
-        out_ref[2 * i] = row[:, :128]
-        out_ref[2 * i + 1] = row[:, 128:256]
+    even = lax.rem(lax.axis_index("wide"), 2) == 0
+    tails = [jnp.zeros((K, 128), f32)] * 2
+    for i in range(3):
+        if i < 2:
+            sides = u2_ref[6 + i], u2_ref[2 + i]
+        else:
+            sides = both_ref[1], both_ref[0]
         here = (lane >= 16 * i) & (lane < 16 * i + 16)
-        tails = jnp.where(here, pltpu.roll(row[:, 256:], HY + 16 * i, 1), tails)
-    out_ref[8] = tails
-
-
-def unpack_deep(got_ref):
+        rows = jnp.where(even, sides[0], sides[1]), jnp.where(even, sides[1], sides[0])
+        for n, ref in enumerate((first_ref, second_ref)):
+            ref[2 * i] = rows[n][:, :128]
+            ref[2 * i + 1] = rows[n][:, 128:256]
+            tails[n] = jnp.where(here, pltpu.roll(rows[n][:, 256:], HY + 16 * i, 1), tails[n])
+    first_ref[6] = tails[0]
+    second_ref[6] = tails[1]
+
+
+def unpack_deep(got):
     lane = lanes((K, 128))
     edge = (lane < HY) | (lane >= 128 - HY)
     rows = []
-    for i in range(4):
-        tail = jnp.where(edge, pltpu.roll(got_ref[8], 128 - HY - 16 * i, 1), 0.0)
-        rows.append(jnp.concatenate([got_ref[2 * i], got_ref[2 * i + 1], tail], axis=1))
-    both = rows.pop()
+    for i in range(3):
+        tail = jnp.where(edge, pltpu.roll(got(6), 128 - HY - 16 * i, 1), 0.0)
+        rows.append(jnp.concatenate([got(2 * i), got(2 * i + 1), tail], axis=1))
+    return rows, unfold(rows.pop())
+
+
+def unfold(both):
     even = lanes((K, LX)) % 2 == 0
     first = jnp.where(even, both, pltpu.roll(both, 1, 1))
     second = jnp.where(even, pltpu.roll(both, LX - 1, 1), both)
-    return rows, (first, second)
+    return first, second
 
 
 def before_scan(
     own_ref, left_ref, right_ref, second_ref, first_ref, u1_ref, smooth_ref, vert_ref, retain_ref,
-    sent_ref, tails_ref, u2_ref, coarse_ref, u1, fine,
+    sent_ref, u2_ref, both_ref, tails_ref, fine, coarse_ref, u1,
 ):
     smooth = smooth_ref[...]
-    lane = lanes((KA, 128))
-    even = lax.rem(lax.axis_index("narrow"), 2) == 0
-    low = jnp.where(even, first_ref[...], second_ref[...])
-    high = jnp.where(even, second_ref[...], first_ref[...])
+    low, high = y_sides(first_ref, second_ref)
     tails = apply3(smooth, jnp.concatenate([low[:K], high[:K]], axis=1))
 
-    def beyond(right, left, o):
-        at = lane[: right.shape[0]]
-        right = pltpu.roll(right, (128 - o) % 128, 1)
-        left = pltpu.roll(left, 128 - HY - o, 1)
-        return jnp.where(at < HY, right, jnp.where(at >= 128 - HY, left, 0.0))
-
     for r in range(NR):
-        tails_ref[r] = beyond(low, high, HY * r)
-        u1[r] = beyond(tails[:, :128], tails[:, 128:], HY * r)
+        tails_ref[r] = beyond(low, high, r)
+        u1[r] = beyond(tails[:, :128], tails[:, 128:], r)
 
     def row(r):
         return whole_row(own_ref, left_ref, right_ref, tails_ref, r)
@@ -255,8 +267,11 @@
             total += smooth_term(u, rhs, area, fine[at - 1], fine[at + 1], 1)
             field += u
         coarse_ref[j] = 0.25 * (pair_sum(total) - apply3(vert, pair_sum(field)))
-    for x in range(8):
-        u2_ref[x] = fine[x + HX]
+    for x in range(10):
+        u2_ref[x] = fine[x + 1]
+    parity = lanes((K, LX)) % 2 == 0
+    for j in range(2):
+        both_ref[j] = jnp.where(parity, coarse_ref[2 * j], coarse_ref[2 * j + 1])
     retain = wide3(retain_ref[...])
     ahead = coarse_ref[0]
     back = coarse_ref[3]
@@ -283,8 +298,16 @@
 
 
 def my_retain(retain_ref):
-    at = lax.rem(lax.axis_index("wide"), PLANE)
+    at = lax.rem(lax.axis_index("wide") + PLANE - FIRST_M, PLANE)
     return retain_ref[pl.ds(pl.multiple_of(at * 8, 8), 8), :]
+
+
+def slot_m(m):
+    return (m - FIRST_M) % PLANE
+
+
+def slot_z(q, planes):
+    return (q - FIRST_Z) % planes
 
 
 def plane_ends(blocks, retain):
@@ -293,8 +316,8 @@
     for order, part in ((range(PLANE), 0), (reversed(range(PLANE)), 1)):
         main, tail = 0.0, 0.0
         for m in order:
-            main = four * main + blocks[m, :, 128 * part : 128 * part + 128]
-            tail = four * tail + blocks[m, :, 256:]
+            main = four * main + blocks[slot_m(m), :, 128 * part : 128 * part + 128]
+            tail = four * tail + blocks[slot_m(m), :, 256:]
         ends += [main, tail if part == 0 else pltpu.roll(tail, 64, 1)]
     return ends
 
@@ -310,8 +333,8 @@
     back = back - reflect * ahead
     back_tail = back_tail - reflect * ahead_tail
     for q in range(planes):
-        out_ref[q, :, :128] = jnp.where(q > here, ahead, back)
-        out_ref[q, :, 128:] = jnp.where(q > here, ahead_tail, back_tail)
+        out_ref[slot_z(q, planes), :, :128] = jnp.where(q > here, ahead, back)
+        out_ref[slot_z(q, planes), :, 128:] = jnp.where(q > here, ahead_tail, back_tail)
 
 
 def across_in(planes, blocks_ref, others_ref, retain_ref, out_ref):
@@ -326,36 +349,40 @@
         back = planes - 1 - q
         for part in range(2):
             at = slice(128 * part, 128 * part + 128)
-            enter[part] = jnp.where(q < here, plane * enter[part] + others_ref[q, :, at], enter[part])
-            leave[part] = jnp.where(back > here, plane * leave[part] + others_ref[back, :, at], leave[part])
+            enter[part] = jnp.where(q < here, plane * enter[part] + others_ref[slot_z(q, planes), :, at], enter[part])
+            leave[part] = jnp.where(back > here, plane * leave[part] + others_ref[slot_z(back, planes), :, at], leave[part])
     leave[0] = leave[0] - reflect * (ahead + plane * enter[0])
     leave[1] = leave[1] - reflect * (ahead_tail + plane * enter[1])
     left = lanes((8, 128)) < 64
     leave[1] = pltpu.roll(leave[1], 64, 1)
     tails = []
     for m in range(PLANE):
-        out_ref[m, :, :128] = enter[0]
+        out_ref[slot_m(m), :, :128] = enter[0]
         tails.append(enter[1])
-        enter[0] = four * enter[0] + blocks_ref[m, :, :128]
-        enter[1] = four * enter[1] + blocks_ref[m, :, 256:]
+        enter[0] = four * enter[0] + blocks_ref[slot_m(m), :, :128]
+        enter[1] = four * enter[1] + blocks_ref[slot_m(m), :, 256:]
     for m in reversed(range(PLANE)):
-        out_ref[m, :, 128:256] = leave[0]
-        out_ref[m, :, 256:] = jnp.where(left, tails[m], leave[1])
-        leave[0] = four * leave[0] + blocks_ref[m, :, 128:256]
-        leave[1] = four * leave[1] + blocks_ref[m, :, 256:]
+        out_ref[slot_m(m), :, 128:256] = leave[0]
+        out_ref[slot_m(m), :, 256:] = jnp.where(left, tails[m], leave[1])
+        leave[0] = four * leave[0] + blocks_ref[slot_m(m), :, 128:256]
+        leave[1] = four * leave[1] + blocks_ref[slot_m(m), :, 256:]
 
 
 def after_scan(
-    got_ref, own_ref, left_ref, right_ref, tails_ref, u2_ref, own_coarse_ref, deep_left, deep_right, smooth_ref, vert_ref, retain_ref, weight_ref,
-    pressure_ref, residual_ref, coarse_ref, line, corr, ua, ub,
+    got_ref, own_ref, left_ref, right_ref, y_second_ref, y_first_ref, u2_ref, both_ref, deep_second_ref, deep_first_ref, smooth_ref, vert_ref, retain_ref, weight_ref,
+    pressure_ref, residual_ref, tails_ref, coarse_ref, line, corr, ua, ub,
 ):
-    left_rows, left_coarse = unpack_deep(deep_left)
-    right_rows, right_coarse = unpack_deep(deep_right)
+    even = lax.rem(lax.axis_index("wide"), 2) == 0
+    left_rows, left_coarse = unpack_deep(lambda i: jnp.where(even, deep_second_ref[i], deep_first_ref[i]))
+    right_rows, right_coarse = unpack_deep(lambda i: jnp.where(even, deep_first_ref[i], deep_second_ref[i]))
     for j in range(2):
         coarse_ref[j] = left_coarse[j]
         coarse_ref[6 + j] = right_coarse[j]
-    for j in range(4):
-        coarse_ref[2 + j] = own_coarse_ref[j]
+    for j in range(2):
+        coarse_ref[2 + 2 * j], coarse_ref[3 + 2 * j] = unfold(both_ref[j])
+    low, high = y_sides(y_first_ref, y_second_ref)
+    for r in range(NR):
+        tails_ref[r] = beyond(low, high, r)
     retain, weight = wide3(retain_ref[...]), wide3(weight_ref[...])
     inv_retain = 1.0 / retain
     coarse_lane = lax.broadcasted_iota(jnp.int32, (256, LX), 0)
@@ -412,7 +439,7 @@
         term = smooth_term(v, coarse_ref[j] + 4.0 * v, coefs[j], line[j], line[j + 2], 2)
         corr[j] = 0.6 * v + apply3(smooth, term)
     for i in range(14):
-        field = left_rows[i] if i < 3 else right_rows[i - 11] if i >= 11 else u2_ref[i - 3]
+        field = left_rows[i] if i < 2 else right_rows[i - 12] if i >= 12 else u2_ref[i - 2]
         ua[i] = field + corr[(i - 3) // 2 + 2]
 
     for source, target, least, most in ((ua, ub, 1, 13), (ub, ua, 2, 12)):
@@ -449,10 +476,6 @@
         second = lax.ppermute(second, axis, [(i, ((i + 1) ^ 1) - 1) for i in range(1, count - 1)])
         return lax.ppermute(first, axis, [(i, i ^ 1) for i in range(count)]), second
 
-    def shift(array, axis, count, by):
-        pairs = [(i, i + by) for i in range(count) if 0 <= i + by < count]
-        return lax.ppermute(array, axis, pairs)
-
     x_first, x_second = in_pairs(up, down, "wide", wide)
     smooth, vert, retain, weight = call(
         tables,
@@ -465,24 +488,22 @@
     )(own, x_second, x_first, retain)
     first, second = in_pairs(first, second, "narrow", narrow)
     (u1,) = call(first_main, [((NR, K, 256), f32)], specs=on_vmem(4))(own, left, right, smooth)
-    sent, tails, u2, coarse = call(
+    sent, u2, coarse = call(
         before_scan,
         K2_OUTS,
         K2_SCRATCH,
         on_vmem(9),
     )(own, left, right, second, first, u1, smooth, vert, retain)
-    in_plane = [[p * PLANE + m for m in range(PLANE)] for p in range(planes)]
-    over_planes = [[p * PLANE + m for p in range(planes)] for m in range(PLANE)]
+    in_plane = [[p * PLANE + (s + FIRST_M) % PLANE for s in range(PLANE)] for p in range(planes)]
+    over_planes = [[(s + FIRST_Z) % planes * PLANE + m for s in range(planes)] for m in range(PLANE)]
 
     def exchange(array, groups):
         return lax.all_to_all(array, "wide", 0, 0, tiled=True, axis_index_groups=groups)
 
     blocks = exchange(sent.reshape(PLANE, 8, LX), in_plane)
-    if DEEP_LATE:
-        blocks, u2, coarse = lax.optimization_barrier((blocks, u2, coarse))
-    deep_up, deep_down = call(pack_deep, [((9, K, 128), f32)] * 2, specs=on_vmem(2))(u2, coarse)
-    deep_left = shift(deep_up, "wide", wide, 1)
-    deep_right = shift(deep_down, "wide", wide, -1)
+    blocks, u2, coarse = lax.optimization_barrier((blocks, u2, coarse))
+    deep_first, deep_second = call(pack_deep, [((7, K, 128), f32)] * 2, specs=on_vmem(2))(u2, coarse)
+    deep_first, deep_second = in_pairs(deep_first, deep_second, "wide", wide)
     (out,) = call(functools.partial(across_out, planes), [((planes, 8, 256), f32)], specs=on_vmem(2))(blocks, retain)
     others = exchange(out, over_planes)
     (back,) = call(functools.partial(across_in, planes), [((PLANE, 8, LX), f32)], specs=on_vmem(3))(
@@ -493,8 +514,8 @@
         after_scan,
         [((K * 16, 128), f32)] * 2,
         K4_SCRATCH,
-        on_vmem(13),
-    )(got, own, left, right, tails, u2, coarse, deep_left, deep_right, smooth, vert, retain, weight)
+        on_vmem(14),
+    )(got, own, left, right, second, first, u2, coarse, deep_second, deep_first, smooth, vert, retain, weight)
     return tuple(
         out.reshape(K, 2, 8, 128).transpose(0, 2, 1, 3).reshape(K, 8, 256) for out in (pressure, residual)
     )

time: 82 us -> 78.6 us (0.959)
  the two profiles are of different devices: /device:TPU:8 before, /device:TPU:32 now
where the time goes in v4:
time: 78.6 us; the launch traced here: 78 us
  starting transfers between devices  45.9 us (58%)
  Pallas kernels  10.9 us (14%)
  waiting for transfers between devices  10.4 us (13%)
  blocking collectives  8.34 us (11%)
  local copies, waits for them, and re-layouts  1.74 us (2%)
    all_to_all x2, starting transfers between devices, exchange(): lax.all_to_all(array, 'wide', 0, 0, tiled=True, axis_index_groups=groups)  23.7 us
    ppermute x3, starting transfers between devices, in_pairs(): lax.ppermute(second, axis, [(i, (i + 1 ^ 1) - 1) for i in range(1, count...  11.9 us
    ppermute x3, starting transfers between devices, in_pairs(): lax.ppermute(first, axis, [(i, i ^ 1) for i in range(count)])  10.3 us
    all_to_all x1, blocking collectives, exchange(): lax.all_to_all(array, 'wide', 0, 0, tiled=True, axis_index_groups=groups)  8.34 us
    ppermute x3, waiting for transfers between devices, in_pairs(): lax.ppermute(first, axis, [(i, i ^ 1) for i in range(count)])  7.64 us
    pallas_call x1, Pallas kernels, local(): call(after_scan, [((K * 16, 128), f32)] * 2, K4_SCRATCH, on_vmem(14))  4.88 us
    pallas_call x1, Pallas kernels, local(): call(before_scan, K2_OUTS, K2_SCRATCH, on_vmem(9))  2.65 us
    ppermute x3, waiting for transfers between devices, in_pairs(): lax.ppermute(second, axis, [(i, (i + 1 ^ 1) - 1) for i in range(1, count...  2.6 us
  transfers between devices with their start and end apart: 8, of which 5 were waited for; matrix products, arithmetic and copies ran while one was open for 0% of the time, Pallas kernels for 3%

profile of v4, /device:TPU:32, one launch (start us, length us, event | category | flops | bytes accessed | tf_op | source)
XLA Modules:
  0.0 78.0 jit_solution(8571719979179648312)
XLA Ops:
  0.6 0.0 copy-start
  0.6 1.0 %copy-done = f32[64,8,256]{2,1,0:T(8,128)S(1)} copy-done((f32[64,8,256]{2,1,0:T(8,128)S(1)}, f32[64,8,256]{2,1,0:T(8,128)}, u32[]{:S(2)}) %copy-start) | copy-done | bytes 524312
  1.7 0.0 copy-start.1
  1.7 0.7 copy-done.1
  2.4 0.2 shard_map.50
  2.6 0.0 copy-start.2
  2.6 5.2 %collective-permute-start = (f32[2,72,256]{2,1,0:T(8,128)S(1)}, f32[2,72,256]{2,1,0:T(8,128)S(1)}, u32[]{:S(2)}, u32[]{:S(2)}) collective-permute-start(f32[2,72,256]{2,1,0:T(8,128)S(1)} %get-tuple-element.24), channel_id=1, source_target_pairs={{4,8},{8,4},{12,16},{16,12},{20,24},{24,20},{28,32},{32,28},{36,40... | collective-permute-start | bytes 442376 | tf_op jit(solution)/shard_map/ppermute | solution.py:476
  7.9 1.9 %collective-permute-start.1 = (f32[2,72,256]{2,1,0:T(8,128)S(1)}, f32[2,72,256]{2,1,0:T(8,128)S(1)}, u32[]{:S(2)}, u32[]{:S(2)}) collective-permute-start(f32[2,72,256]{2,1,0:T(8,128)S(1)} %get-tuple-element.25), channel_id=1, source_target_pairs={{0,4},{4,0},{8,12},{12,8},{16,20},{20,16},{24,28},{28,24},{32,36},... | collective-permute-start | bytes 442376 | tf_op jit(solution)/shard_map/ppermute | solution.py:477
  9.8 0.0 copy-done.2
  9.8 0.8 %shard_map.51 = (bf16[64,192]{1,0:T(8,128)(2,1)S(1)}, bf16[64,192]{1,0:T(8,128)(2,1)S(1)}, f32[64,128]{1,0:T(8,128)S(1)}, f32[64,128]{1,0:T(8,128)S(1)}) custom-call(f32[64]{0:T(128)S(1)} %copy-done.2), custom_call_target="tpu_custom_call" | custom-call | tf_op jit(solution)/shard_map/pallas_call | solution.py:480
  10.6 2.6 %collective-permute-done.x_second_ref = f32[2,72,256]{2,1,0:T(8,128)S(1)} collective-permute-done((f32[2,72,256]{2,1,0:T(8,128)S(1)}, f32[2,72,256]{2,1,0:T(8,128)S(1)}, u32[]{:S(2)}, u32[]{:S(2)}) %collective-permute-start) | collective-permute-done | bytes 147488 | tf_op jit(solution)/shard_map/ppermute | solution.py:476
  13.2 3.1 %collective-permute-done.1.x_first_ref = f32[2,72,256]{2,1,0:T(8,128)S(1)} collective-permute-done((f32[2,72,256]{2,1,0:T(8,128)S(1)}, f32[2,72,256]{2,1,0:T(8,128)S(1)}, u32[]{:S(2)}, u32[]{:S(2)}) %collective-permute-start.1) | collective-permute-done | bytes 147488 | tf_op jit(solution)/shard_map/ppermute | solution.py:477
  16.3 0.3 shard_map.52
  16.6 0.7 collective-permute-start.2
  17.3 6.5 %collective-permute-start.3 = (f32[72,128]{1,0:T(8,128)S(1)}, f32[72,128]{1,0:T(8,128)S(1)}, u32[]{:S(2)}, u32[]{:S(2)}) collective-permute-start(f32[72,128]{1,0:T(8,128)S(1)} %get-tuple-element.30), channel_id=1, source_target_pairs={{0,1},{1,0},{2,3},{3,2},{4,5},{5,4},{6,7},{7,6},{8,9},{9,8},{10,11... | collective-permute-start | bytes 110600 | tf_op jit(solution)/shard_map/ppermute | solution.py:477
  23.7 0.3 shard_map.53.u1_ref
  24.1 0.0 collective-permute-done.2.second_ref.y_second_ref
  24.1 0.5 collective-permute-done.3.first_ref.y_first_ref
  24.6 2.6 %shard_map.54 = (f32[64,384]{1,0:T(8,128)S(1)}, f32[10,64,384]{2,1,0:T(8,128)S(1)}, f32[2,64,384]{2,1,0:T(8,128)S(1)}) custom-call(f32[8,72,256]{2,1,0:T(8,128)S(1)} %get-tuple-element.23.own_ref, f32[2,72,256]{2,1,0:T(8,128)S(1)} %get-tuple-element.27.left_ref, f32[2,72,256]{2,1,0:T(8,128)S(1)} %get-tuple-element.28.right_ref, ...), custom_call_target="tpu_custom_call" | custom-call | tf_op jit(solution)/shard_map/pallas_call | solution.py:491
  27.2 8.3 %all_to_all.15.blocks_ref = f32[8,8,384]{2,1,0:T(8,128)S(1)} all-to-all(f32[8,8,384]{2,1,0:T(8,128)S(1)} %bitcast.19), channel_id=1, replica_groups={{20,24,28,0,4,8,12,16},{52,56,60,32,36,40,44,48},{84,88,92,64,68,72,76,..., dimensions={0} | all-to-all | bytes 196608 | tf_op jit(solution)/shard_map/all_to_all | solution.py:501
  35.6 0.8 shard_map.55
  36.3 17.5 %all-to-all-start.1 = ((f32[16,8,256]{2,1,0:T(8,128)}), f32[16,8,256]{2,1,0:T(8,128)S(1)}, u32[]{:S(2)}, u32[]{:S(2)}) async-start(f32[16,8,256]{2,1,0:T(8,128)} %shard_map.55), calls=%async_computation.1 | async-start | bytes 262144 | tf_op jit(solution)/shard_map/all_to_all | solution.py:501
  53.8 0.1 shard_map.57
  53.9 6.0 %collective-permute-start.4 = (f32[7,64,128]{2,1,0:T(8,128)S(1)}, f32[7,64,128]{2,1,0:T(8,128)S(1)}, u32[]{:S(2)}, u32[]{:S(2)}) collective-permute-start(f32[7,64,128]{2,1,0:T(8,128)S(1)} %get-tuple-element.39), channel_id=1, source_target_pairs={{4,8},{8,4},{12,16},{16,12},{20,24},{24,20},{28,32},{32,28},{36,40... | collective-permute-start | bytes 688136 | tf_op jit(solution)/shard_map/ppermute | solution.py:476
  59.9 1.9 %collective-permute-start.5 = (f32[7,64,128]{2,1,0:T(8,128)S(1)}, f32[7,64,128]{2,1,0:T(8,128)S(1)}, u32[]{:S(2)}, u32[]{:S(2)}) collective-permute-start(f32[7,64,128]{2,1,0:T(8,128)S(1)} %get-tuple-element.40), channel_id=1, source_target_pairs={{0,4},{4,0},{8,12},{12,8},{16,20},{20,16},{24,28},{28,24},{32,36},... | collective-permute-start | bytes 688136 | tf_op jit(solution)/shard_map/ppermute | solution.py:477
  61.8 0.0 all-to-all-done.1.others_ref
  61.9 0.8 %shard_map.56 = f32[8,8,384]{2,1,0:T(8,128)} custom-call(f32[8,8,384]{2,1,0:T(8,128)S(1)} %all_to_all.15.blocks_ref, f32[16,8,256]{2,1,0:T(8,128)S(1)} %all-to-all-done.1.others_ref, f32[64,128]{1,0:T(8,128)S(1)} %get-tuple-element.26._.retain_ref), custom_call_target="tpu_custom_call" | custom-call | tf_op jit(solution)/shard_map/pallas_call | solution.py:509
  62.7 6.3 %all-to-all-start.2 = ((f32[8,8,384]{2,1,0:T(8,128)}), f32[8,8,384]{2,1,0:T(8,128)S(1)}, u32[]{:S(2)}, u32[]{:S(2)}) async-start(f32[8,8,384]{2,1,0:T(8,128)} %shard_map.56), calls=%async_computation.2 | async-start | bytes 196608 | tf_op jit(solution)/shard_map/all_to_all | solution.py:501
  68.9 0.0 collective-permute-done.4.deep_second_ref
  68.9 4.1 %collective-permute-done.5.deep_first_ref = f32[7,64,128]{2,1,0:T(8,128)S(1)} collective-permute-done((f32[7,64,128]{2,1,0:T(8,128)S(1)}, f32[7,64,128]{2,1,0:T(8,128)S(1)}, u32[]{:S(2)}, u32[]{:S(2)}) %collective-permute-start.5) | collective-permute-done | bytes 229408 | tf_op jit(solution)/shard_map/ppermute | solution.py:477
  73.0 0.1 all-to-all-done.2
  73.1 4.9 %shard_map.58 = (f32[1024,128]{1,0:T(8,128)}, f32[1024,128]{1,0:T(8,128)}) custom-call(f32[64,384]{1,0:T(8,128)S(1)} %bitcast.18, f32[8,72,256]{2,1,0:T(8,128)S(1)} %get-tuple-element.23.own_ref, f32[2,72,256]{2,1,0:T(8,128)S(1)} %get-tuple-element.27.left_ref, f32[2,72,256]{2,1,0:T(8,128)S(1)} %get-tuple-element.28.right_ref, ...), custom_call_target="tpu_custom_call" | custom-call | tf_op jit(solution)/shard_map/pallas_call | solution.py:513
Async XLA Ops:
  0.6 1.0 %copy-start = (f32[64,8,256]{2,1,0:T(8,128)S(1)}, f32[64,8,256]{2,1,0:T(8,128)}, u32[]{:S(2)}) copy-start(f32[64,8,256]{2,1,0:T(8,128)} %param.3) | copy-start | bytes 1572868
  1.7 0.7 copy-start.1
  2.6 7.2 %copy-start.2 = (f32[64]{0:T(128)S(1)}, f32[64]{0:T(128)}, u32[]{:S(2)}) copy-start(f32[64]{0:T(128)} %stiff_ref.1) | copy-start | bytes 772
  2.6 10.6 %collective-permute-start = (f32[2,72,256]{2,1,0:T(8,128)S(1)}, f32[2,72,256]{2,1,0:T(8,128)S(1)}, u32[]{:S(2)}, u32[]{:S(2)}) collective-permute-start(f32[2,72,256]{2,1,0:T(8,128)S(1)} %get-tuple-element.24), channel_id=1, source_target_pairs={{4,8},{8,4},{12,16},{16,12},{20,24},{24,20},{28,32},{32,28},{36,40... | collective-permute-start | bytes 442376 | tf_op jit(solution)/shard_map/ppermute | solution.py:476
  7.9 8.4 %collective-permute-start.1 = (f32[2,72,256]{2,1,0:T(8,128)S(1)}, f32[2,72,256]{2,1,0:T(8,128)S(1)}, u32[]{:S(2)}, u32[]{:S(2)}) collective-permute-start(f32[2,72,256]{2,1,0:T(8,128)S(1)} %get-tuple-element.25), channel_id=1, source_target_pairs={{0,4},{4,0},{8,12},{12,8},{16,20},{20,16},{24,28},{28,24},{32,36},... | collective-permute-start | bytes 442376 | tf_op jit(solution)/shard_map/ppermute | solution.py:477
  16.6 7.5 %collective-permute-start.2 = (f32[72,128]{1,0:T(8,128)S(1)}, f32[72,128]{1,0:T(8,128)S(1)}, u32[]{:S(2)}, u32[]{:S(2)}) collective-permute-start(f32[72,128]{1,0:T(8,128)S(1)} %get-tuple-element.29), channel_id=1, source_target_pairs={{1,2},{2,1},{5,6},{6,5},{9,10},{10,9},{13,14},{14,13},{17,18},{18,... | collective-permute-start | bytes 110600 | tf_op jit(solution)/shard_map/ppermute | solution.py:476
  17.3 7.3 %collective-permute-start.3 = (f32[72,128]{1,0:T(8,128)S(1)}, f32[72,128]{1,0:T(8,128)S(1)}, u32[]{:S(2)}, u32[]{:S(2)}) collective-permute-start(f32[72,128]{1,0:T(8,128)S(1)} %get-tuple-element.30), channel_id=1, source_target_pairs={{0,1},{1,0},{2,3},{3,2},{4,5},{5,4},{6,7},{7,6},{8,9},{9,8},{10,11... | collective-permute-start | bytes 110600 | tf_op jit(solution)/shard_map/ppermute | solution.py:477
  36.3 25.5 %all-to-all-start.1 = ((f32[16,8,256]{2,1,0:T(8,128)}), f32[16,8,256]{2,1,0:T(8,128)S(1)}, u32[]{:S(2)}, u32[]{:S(2)}) async-start(f32[16,8,256]{2,1,0:T(8,128)} %shard_map.55), calls=%async_computation.1 | async-start | bytes 262144 | tf_op jit(solution)/shard_map/all_to_all | solution.py:501
  53.9 15.0 %collective-permute-start.4 = (f32[7,64,128]{2,1,0:T(8,128)S(1)}, f32[7,64,128]{2,1,0:T(8,128)S(1)}, u32[]{:S(2)}, u32[]{:S(2)}) collective-permute-start(f32[7,64,128]{2,1,0:T(8,128)S(1)} %get-tuple-element.39), channel_id=1, source_target_pairs={{4,8},{8,4},{12,16},{16,12},{20,24},{24,20},{28,32},{32,28},{36,40... | collective-permute-start | bytes 688136 | tf_op jit(solution)/shard_map/ppermute | solution.py:476
  59.9 13.1 %collective-permute-start.5 = (f32[7,64,128]{2,1,0:T(8,128)S(1)}, f32[7,64,128]{2,1,0:T(8,128)S(1)}, u32[]{:S(2)}, u32[]{:S(2)}) collective-permute-start(f32[7,64,128]{2,1,0:T(8,128)S(1)} %get-tuple-element.40), channel_id=1, source_target_pairs={{0,4},{4,0},{8,12},{12,8},{16,20},{20,16},{24,28},{28,24},{32,36},... | collective-permute-start | bytes 688136 | tf_op jit(solution)/shard_map/ppermute | solution.py:477
  62.7 10.5 %all-to-all-start.2 = ((f32[8,8,384]{2,1,0:T(8,128)}), f32[8,8,384]{2,1,0:T(8,128)S(1)}, u32[]{:S(2)}, u32[]{:S(2)}) async-start(f32[8,8,384]{2,1,0:T(8,128)} %shard_map.56), calls=%async_computation.2 | async-start | bytes 196608 | tf_op jit(solution)/shard_map/all_to_all | solution.py:501

commit v5 on v4

--- a/solution.py
+++ b/solution.py
@@ -14,8 +14,8 @@
 NR = 8 + 2 * HX
 LX = 384
 PLANE = 8
-FIRST_M = 5
-FIRST_Z = 8
+FIRST_M = 4
+FIRST_Z = 10
 f32, bf16 = jnp.float32, jnp.bfloat16
 K2_OUTS = [((K, LX), f32), ((10, K, LX), f32), ((2, K, LX), f32)]
 K2_SCRATCH = [pltpu.VMEM(s, f32) for s in ((NR, KA, 128), (NR, K, LX), (4, K, LX), (NR, K, 128))]
@@ -369,7 +369,7 @@
 
 
 def after_scan(
-    got_ref, own_ref, left_ref, right_ref, y_second_ref, y_first_ref, u2_ref, both_ref, deep_second_ref, deep_first_ref, smooth_ref, vert_ref, retain_ref, weight_ref,
+    got_ref, own_ref, left_ref, right_ref, y_second_ref, y_first_ref, u2_ref, both_ref, deep_first_ref, deep_second_ref, smooth_ref, vert_ref, retain_ref, weight_ref,
     pressure_ref, residual_ref, tails_ref, coarse_ref, line, corr, ua, ub,
 ):
     even = lax.rem(lax.axis_index("wide"), 2) == 0
@@ -515,7 +515,7 @@
         [((K * 16, 128), f32)] * 2,
         K4_SCRATCH,
         on_vmem(14),
-    )(got, own, left, right, second, first, u2, coarse, deep_second, deep_first, smooth, vert, retain, weight)
+    )(got, own, left, right, second, first, u2, coarse, deep_first, deep_second, smooth, vert, retain, weight)
     return tuple(
         out.reshape(K, 2, 8, 128).transpose(0, 2, 1, 3).reshape(K, 8, 256) for out in (pressure, residual)
     )

time: 78.6 us -> 76.5 us (0.973)
  the two profiles are of different devices: /device:TPU:32 before, /device:TPU:2 now
where the time goes in v5:
time: 76.5 us; the launch traced here: 75.9 us
  starting transfers between devices  40.4 us (53%)
  waiting for transfers between devices  11.1 us (15%)
  blocking collectives  11.1 us (15%)
  Pallas kernels  10.9 us (14%)
  local copies, waits for them, and re-layouts  1.74 us (2%)
    all_to_all x2, starting transfers between devices, exchange(): lax.all_to_all(array, 'wide', 0, 0, tiled=True, axis_index_groups=groups)  20.6 us
    ppermute x3, starting transfers between devices, in_pairs(): lax.ppermute(first, axis, [(i, i ^ 1) for i in range(count)])  12.1 us
    all_to_all x1, blocking collectives, exchange(): lax.all_to_all(array, 'wide', 0, 0, tiled=True, axis_index_groups=groups)  11.1 us
    ppermute x3, starting transfers between devices, in_pairs(): lax.ppermute(second, axis, [(i, (i + 1 ^ 1) - 1) for i in range(1, count...  7.62 us
    all_to_all x2, waiting for transfers between devices, exchange(): lax.all_to_all(array, 'wide', 0, 0, tiled=True, axis_index_groups=groups)  5.8 us
    pallas_call x1, Pallas kernels, local(): call(after_scan, [((K * 16, 128), f32)] * 2, K4_SCRATCH, on_vmem(14))  4.88 us
    ppermute x3, waiting for transfers between devices, in_pairs(): lax.ppermute(first, axis, [(i, i ^ 1) for i in range(count)])  4.47 us
    pallas_call x1, Pallas kernels, local(): call(before_scan, K2_OUTS, K2_SCRATCH, on_vmem(9))  2.64 us
  transfers between devices with their start and end apart: 8, of which 6 were waited for; matrix products, arithmetic and copies ran while one was open for 0% of the time, Pallas kernels for 3%

profile of v5, /device:TPU:2, one launch (start us, length us, event | category | flops | bytes accessed | tf_op | source)
XLA Modules:
  0.0 75.9 jit_solution(18016253021823344019)
XLA Ops:
  0.6 0.0 copy-start
  0.6 1.0 %copy-done = f32[64,8,256]{2,1,0:T(8,128)S(1)} copy-done((f32[64,8,256]{2,1,0:T(8,128)S(1)}, f32[64,8,256]{2,1,0:T(8,128)}, u32[]{:S(2)}) %copy-start) | copy-done | bytes 524312
  1.7 0.0 copy-start.1
  1.7 0.7 copy-done.1
  2.4 0.2 shard_map.50
  2.6 0.0 copy-start.2
  2.6 3.5 %collective-permute-start = (f32[2,72,256]{2,1,0:T(8,128)S(1)}, f32[2,72,256]{2,1,0:T(8,128)S(1)}, u32[]{:S(2)}, u32[]{:S(2)}) collective-permute-start(f32[2,72,256]{2,1,0:T(8,128)S(1)} %get-tuple-element.24), channel_id=1, source_target_pairs={{4,8},{8,4},{12,16},{16,12},{20,24},{24,20},{28,32},{32,28},{36,40... | collective-permute-start | bytes 442376 | tf_op jit(solution)/shard_map/ppermute | solution.py:476
  6.1 3.3 %collective-permute-start.1 = (f32[2,72,256]{2,1,0:T(8,128)S(1)}, f32[2,72,256]{2,1,0:T(8,128)S(1)}, u32[]{:S(2)}, u32[]{:S(2)}) collective-permute-start(f32[2,72,256]{2,1,0:T(8,128)S(1)} %get-tuple-element.25), channel_id=1, source_target_pairs={{0,4},{4,0},{8,12},{12,8},{16,20},{20,16},{24,28},{28,24},{32,36},... | collective-permute-start | bytes 442376 | tf_op jit(solution)/shard_map/ppermute | solution.py:477
  9.4 0.0 copy-done.2
  9.4 0.8 %shard_map.51 = (bf16[64,192]{1,0:T(8,128)(2,1)S(1)}, bf16[64,192]{1,0:T(8,128)(2,1)S(1)}, f32[64,128]{1,0:T(8,128)S(1)}, f32[64,128]{1,0:T(8,128)S(1)}) custom-call(f32[64]{0:T(128)S(1)} %copy-done.2), custom_call_target="tpu_custom_call" | custom-call | tf_op jit(solution)/shard_map/pallas_call | solution.py:480
  10.3 0.8 %collective-permute-done.x_second_ref = f32[2,72,256]{2,1,0:T(8,128)S(1)} collective-permute-done((f32[2,72,256]{2,1,0:T(8,128)S(1)}, f32[2,72,256]{2,1,0:T(8,128)S(1)}, u32[]{:S(2)}, u32[]{:S(2)}) %collective-permute-start) | collective-permute-done | bytes 147488 | tf_op jit(solution)/shard_map/ppermute | solution.py:476
  11.1 3.1 %collective-permute-done.1.x_first_ref = f32[2,72,256]{2,1,0:T(8,128)S(1)} collective-permute-done((f32[2,72,256]{2,1,0:T(8,128)S(1)}, f32[2,72,256]{2,1,0:T(8,128)S(1)}, u32[]{:S(2)}, u32[]{:S(2)}) %collective-permute-start.1) | collective-permute-done | bytes 147488 | tf_op jit(solution)/shard_map/ppermute | solution.py:477
  14.2 0.3 shard_map.52
  14.5 0.7 collective-permute-start.2
  15.2 6.5 %collective-permute-start.3 = (f32[72,128]{1,0:T(8,128)S(1)}, f32[72,128]{1,0:T(8,128)S(1)}, u32[]{:S(2)}, u32[]{:S(2)}) collective-permute-start(f32[72,128]{1,0:T(8,128)S(1)} %get-tuple-element.30), channel_id=1, source_target_pairs={{0,1},{1,0},{2,3},{3,2},{4,5},{5,4},{6,7},{7,6},{8,9},{9,8},{10,11... | collective-permute-start | bytes 110600 | tf_op jit(solution)/shard_map/ppermute | solution.py:477
  21.6 0.3 shard_map.53.u1_ref
  22.0 0.0 collective-permute-done.2.second_ref.y_second_ref
  22.0 0.5 collective-permute-done.3.first_ref.y_first_ref
  22.5 2.6 %shard_map.54 = (f32[64,384]{1,0:T(8,128)S(1)}, f32[10,64,384]{2,1,0:T(8,128)S(1)}, f32[2,64,384]{2,1,0:T(8,128)S(1)}) custom-call(f32[8,72,256]{2,1,0:T(8,128)S(1)} %get-tuple-element.23.own_ref, f32[2,72,256]{2,1,0:T(8,128)S(1)} %get-tuple-element.27.left_ref, f32[2,72,256]{2,1,0:T(8,128)S(1)} %get-tuple-element.28.right_ref, ...), custom_call_target="tpu_custom_call" | custom-call | tf_op jit(solution)/shard_map/pallas_call | solution.py:491
  25.1 11.1 %all_to_all.15.blocks_ref = f32[8,8,384]{2,1,0:T(8,128)S(1)} all-to-all(f32[8,8,384]{2,1,0:T(8,128)S(1)} %bitcast.19), channel_id=1, replica_groups={{16,20,24,28,0,4,8,12},{48,52,56,60,32,36,40,44},{80,84,88,92,64,68,72,..., dimensions={0} | all-to-all | bytes 196608 | tf_op jit(solution)/shard_map/all_to_all | solution.py:501
  36.2 0.8 shard_map.55
  36.9 16.4 %all-to-all-start.1 = ((f32[16,8,256]{2,1,0:T(8,128)}), f32[16,8,256]{2,1,0:T(8,128)S(1)}, u32[]{:S(2)}, u32[]{:S(2)}) async-start(f32[16,8,256]{2,1,0:T(8,128)} %shard_map.55), calls=%async_computation.1 | async-start | bytes 262144 | tf_op jit(solution)/shard_map/all_to_all | solution.py:501
  53.4 0.1 shard_map.57
  53.5 2.3 %collective-permute-start.4 = (f32[7,64,128]{2,1,0:T(8,128)S(1)}, f32[7,64,128]{2,1,0:T(8,128)S(1)}, u32[]{:S(2)}, u32[]{:S(2)}) collective-permute-start(f32[7,64,128]{2,1,0:T(8,128)S(1)} %get-tuple-element.39), channel_id=1, source_target_pairs={{0,4},{4,0},{8,12},{12,8},{16,20},{20,16},{24,28},{28,24},{32,36},... | collective-permute-start | bytes 688136 | tf_op jit(solution)/shard_map/ppermute | solution.py:477
  55.8 3.5 %collective-permute-start.5 = (f32[7,64,128]{2,1,0:T(8,128)S(1)}, f32[7,64,128]{2,1,0:T(8,128)S(1)}, u32[]{:S(2)}, u32[]{:S(2)}) collective-permute-start(f32[7,64,128]{2,1,0:T(8,128)S(1)} %get-tuple-element.40), channel_id=1, source_target_pairs={{4,8},{8,4},{12,16},{16,12},{20,24},{24,20},{28,32},{32,28},{36,40... | collective-permute-start | bytes 688136 | tf_op jit(solution)/shard_map/ppermute | solution.py:476
  59.4 1.6 %all-to-all-done.1.others_ref = f32[16,8,256]{2,1,0:T(8,128)S(1)} async-done(((f32[16,8,256]{2,1,0:T(8,128)}), f32[16,8,256]{2,1,0:T(8,128)S(1)}, u32[]{:S(2)}, u32[]{:S(2)}) %all-to-all-start.1) | async-done | bytes 131104 | tf_op jit(solution)/shard_map/all_to_all | solution.py:501
  61.0 0.8 %shard_map.56 = f32[8,8,384]{2,1,0:T(8,128)} custom-call(f32[8,8,384]{2,1,0:T(8,128)S(1)} %all_to_all.15.blocks_ref, f32[16,8,256]{2,1,0:T(8,128)S(1)} %all-to-all-done.1.others_ref, f32[64,128]{1,0:T(8,128)S(1)} %get-tuple-element.26._.retain_ref), custom_call_target="tpu_custom_call" | custom-call | tf_op jit(solution)/shard_map/pallas_call | solution.py:509
  61.8 4.2 %all-to-all-start.2 = ((f32[8,8,384]{2,1,0:T(8,128)}), f32[8,8,384]{2,1,0:T(8,128)S(1)}, u32[]{:S(2)}, u32[]{:S(2)}) async-start(f32[8,8,384]{2,1,0:T(8,128)} %shard_map.56), calls=%async_computation.2 | async-start | bytes 196608 | tf_op jit(solution)/shard_map/all_to_all | solution.py:501
  66.0 0.9 %collective-permute-done.4.deep_first_ref = f32[7,64,128]{2,1,0:T(8,128)S(1)} collective-permute-done((f32[7,64,128]{2,1,0:T(8,128)S(1)}, f32[7,64,128]{2,1,0:T(8,128)S(1)}, u32[]{:S(2)}, u32[]{:S(2)}) %collective-permute-start.4) | collective-permute-done | bytes 229408 | tf_op jit(solution)/shard_map/ppermute | solution.py:477
  66.9 0.0 collective-permute-done.5.deep_second_ref
  66.9 4.2 %all-to-all-done.2 = f32[8,8,384]{2,1,0:T(8,128)S(1)} async-done(((f32[8,8,384]{2,1,0:T(8,128)}), f32[8,8,384]{2,1,0:T(8,128)S(1)}, u32[]{:S(2)}, u32[]{:S(2)}) %all-to-all-start.2) | async-done | bytes 98336 | tf_op jit(solution)/shard_map/all_to_all | solution.py:501
  71.1 4.9 %shard_map.58 = (f32[1024,128]{1,0:T(8,128)}, f32[1024,128]{1,0:T(8,128)}) custom-call(f32[64,384]{1,0:T(8,128)S(1)} %bitcast.18, f32[8,72,256]{2,1,0:T(8,128)S(1)} %get-tuple-element.23.own_ref, f32[2,72,256]{2,1,0:T(8,128)S(1)} %get-tuple-element.27.left_ref, f32[2,72,256]{2,1,0:T(8,128)S(1)} %get-tuple-element.28.right_ref, ...), custom_call_target="tpu_custom_call" | custom-call | tf_op jit(solution)/shard_map/pallas_call | solution.py:513
Async XLA Ops:
  0.6 1.0 %copy-start = (f32[64,8,256]{2,1,0:T(8,128)S(1)}, f32[64,8,256]{2,1,0:T(8,128)}, u32[]{:S(2)}) copy-start(f32[64,8,256]{2,1,0:T(8,128)} %param.3) | copy-start | bytes 1572868
  1.7 0.7 copy-start.1
  2.6 6.8 %copy-start.2 = (f32[64]{0:T(128)S(1)}, f32[64]{0:T(128)}, u32[]{:S(2)}) copy-start(f32[64]{0:T(128)} %stiff_ref.1) | copy-start | bytes 772
  2.6 8.5 %collective-permute-start = (f32[2,72,256]{2,1,0:T(8,128)S(1)}, f32[2,72,256]{2,1,0:T(8,128)S(1)}, u32[]{:S(2)}, u32[]{:S(2)}) collective-permute-start(f32[2,72,256]{2,1,0:T(8,128)S(1)} %get-tuple-element.24), channel_id=1, source_target_pairs={{4,8},{8,4},{12,16},{16,12},{20,24},{24,20},{28,32},{32,28},{36,40... | collective-permute-start | bytes 442376 | tf_op jit(solution)/shard_map/ppermute | solution.py:476
  6.1 8.1 %collective-permute-start.1 = (f32[2,72,256]{2,1,0:T(8,128)S(1)}, f32[2,72,256]{2,1,0:T(8,128)S(1)}, u32[]{:S(2)}, u32[]{:S(2)}) collective-permute-start(f32[2,72,256]{2,1,0:T(8,128)S(1)} %get-tuple-element.25), channel_id=1, source_target_pairs={{0,4},{4,0},{8,12},{12,8},{16,20},{20,16},{24,28},{28,24},{32,36},... | collective-permute-start | bytes 442376 | tf_op jit(solution)/shard_map/ppermute | solution.py:477
  14.5 7.5 %collective-permute-start.2 = (f32[72,128]{1,0:T(8,128)S(1)}, f32[72,128]{1,0:T(8,128)S(1)}, u32[]{:S(2)}, u32[]{:S(2)}) collective-permute-start(f32[72,128]{1,0:T(8,128)S(1)} %get-tuple-element.29), channel_id=1, source_target_pairs={{1,2},{2,1},{5,6},{6,5},{9,10},{10,9},{13,14},{14,13},{17,18},{18,... | collective-permute-start | bytes 110600 | tf_op jit(solution)/shard_map/ppermute | solution.py:476
  15.2 7.3 %collective-permute-start.3 = (f32[72,128]{1,0:T(8,128)S(1)}, f32[72,128]{1,0:T(8,128)S(1)}, u32[]{:S(2)}, u32[]{:S(2)}) collective-permute-start(f32[72,128]{1,0:T(8,128)S(1)} %get-tuple-element.30), channel_id=1, source_target_pairs={{0,1},{1,0},{2,3},{3,2},{4,5},{5,4},{6,7},{7,6},{8,9},{9,8},{10,11... | collective-permute-start | bytes 110600 | tf_op jit(solution)/shard_map/ppermute | solution.py:477
  36.9 24.0 %all-to-all-start.1 = ((f32[16,8,256]{2,1,0:T(8,128)}), f32[16,8,256]{2,1,0:T(8,128)S(1)}, u32[]{:S(2)}, u32[]{:S(2)}) async-start(f32[16,8,256]{2,1,0:T(8,128)} %shard_map.55), calls=%async_computation.1 | async-start | bytes 262144 | tf_op jit(solution)/shard_map/all_to_all | solution.py:501
  53.5 13.4 %collective-permute-start.4 = (f32[7,64,128]{2,1,0:T(8,128)S(1)}, f32[7,64,128]{2,1,0:T(8,128)S(1)}, u32[]{:S(2)}, u32[]{:S(2)}) collective-permute-start(f32[7,64,128]{2,1,0:T(8,128)S(1)} %get-tuple-element.39), channel_id=1, source_target_pairs={{0,4},{4,0},{8,12},{12,8},{16,20},{20,16},{24,28},{28,24},{32,36},... | collective-permute-start | bytes 688136 | tf_op jit(solution)/shard_map/ppermute | solution.py:477
  55.8 11.0 %collective-permute-start.5 = (f32[7,64,128]{2,1,0:T(8,128)S(1)}, f32[7,64,128]{2,1,0:T(8,128)S(1)}, u32[]{:S(2)}, u32[]{:S(2)}) collective-permute-start(f32[7,64,128]{2,1,0:T(8,128)S(1)} %get-tuple-element.40), channel_id=1, source_target_pairs={{4,8},{8,4},{12,16},{16,12},{20,24},{24,20},{28,32},{32,28},{36,40... | collective-permute-start | bytes 688136 | tf_op jit(solution)/shard_map/ppermute | solution.py:476
  61.8 9.3 %all-to-all-start.2 = ((f32[8,8,384]{2,1,0:T(8,128)}), f32[8,8,384]{2,1,0:T(8,128)S(1)}, u32[]{:S(2)}, u32[]{:S(2)}) async-start(f32[8,8,384]{2,1,0:T(8,128)} %shard_map.56), calls=%async_computation.2 | async-start | bytes 196608 | tf_op jit(solution)/shard_map/all_to_all | solution.py:501

commit v6 on v5

--- a/solution.py
+++ b/solution.py
@@ -178,9 +178,9 @@
         u1_ref[r] = apply3(smooth, ext_row(own_ref, left_ref, right_ref, r)[:K])
 
 
-def smooth_term(u, rhs, area, above, below, step):
+def smooth_term(u, rhs, area, above, below, step, more=0.0):
     beside = above + below + pltpu.roll(u, step, 1) + pltpu.roll(u, LX - step, 1)
-    return rhs - area * (4.0 * u - beside)
+    return rhs + ((more - 4.0 * area) * u + area * beside)
 
 
 def pair_sum(v):
@@ -257,7 +257,7 @@
 
     for r in range(1, NR - 1):
         u, (rhs, area) = first(r), row(r)
-        term = smooth_term(u, rhs + 4.0 * u, area, first(r - 1), first(r + 1), 1)
+        term = smooth_term(u, rhs, area, first(r - 1), first(r + 1), 1, 4.0)
         fine[r] = 0.6 * u + apply3(smooth, term)
     vert = vert_ref[...]
     for j in range(4):
@@ -302,6 +302,15 @@
     return retain_ref[pl.ds(pl.multiple_of(at * 8, 8), 8), :]
 
 
+def beyond_here(planes, here, retain):
+    left, step = planes - 1 - here, power(retain, 64)
+    out = jnp.ones_like(retain)
+    for b in range((planes - 1).bit_length()):
+        out = jnp.where((left >> b) & 1 == 1, out * step, out)
+        step = step * step
+    return out
+
+
 def slot_m(m):
     return (m - FIRST_M) % PLANE
 
@@ -326,10 +335,7 @@
     retain = my_retain(retain_ref)
     here = lax.div(lax.axis_index("wide"), PLANE)
     ahead, ahead_tail, back, back_tail = plane_ends(blocks_ref, retain)
-    reflect = power(retain, 33)
-    step = power(retain, 64)
-    for q in range(planes):
-        reflect = jnp.where(q > here, reflect * step, reflect)
+    reflect = power(retain, 33) * beyond_here(planes, here, retain)
     back = back - reflect * ahead
     back_tail = back_tail - reflect * ahead_tail
     for q in range(planes):
@@ -342,10 +348,9 @@
     here = lax.div(lax.axis_index("wide"), PLANE)
     ahead, ahead_tail, _, _ = plane_ends(blocks_ref, retain)
     four, plane = power(retain, 4), power(retain, 32)
-    reflect, step = retain, power(retain, 64)
+    reflect = retain * beyond_here(planes, here, retain)
     enter, leave = [0.0, 0.0], [0.0, 0.0]
     for q in range(planes):
-        reflect = jnp.where(q > here, reflect * step, reflect)
         back = planes - 1 - q
         for part in range(2):
             at = slice(128 * part, 128 * part + 128)
@@ -436,7 +441,7 @@
 
     for j in range(8):
         v = line[j + 1]
-        term = smooth_term(v, coarse_ref[j] + 4.0 * v, coefs[j], line[j], line[j + 2], 2)
+        term = smooth_term(v, coarse_ref[j], coefs[j], line[j], line[j + 2], 2, 4.0)
         corr[j] = 0.6 * v + apply3(smooth, term)
     for i in range(14):
         field = left_rows[i] if i < 2 else right_rows[i - 12] if i >= 12 else u2_ref[i - 2]
@@ -445,7 +450,7 @@
     for source, target, least, most in ((ua, ub, 1, 13), (ub, ua, 2, 12)):
         for i in range(least, most):
             u, (rhs, area) = source[i], row(i + HX - 3)
-            term = smooth_term(u, rhs + 4.0 * u, area, source[i - 1], source[i + 1], 1)
+            term = smooth_term(u, rhs, area, source[i - 1], source[i + 1], 1, 4.0)
             target[i] = 0.6 * u + apply3(smooth, term)
     vert = vert_ref[...]
     for x in range(8):
@@ -464,13 +469,12 @@
     wide, narrow = lax.axis_size("wide"), lax.axis_size("narrow")
     planes = wide // PLANE
     rhs = rhs.reshape(K, 8, 2, 128).transpose(0, 2, 1, 3).reshape(K * 16, 128)
-    anywhere = [pl.BlockSpec(memory_space=pltpu.HBM)] * 2
     up, down, own = call(
         pack_x,
         [((HX, KA, 256), f32)] * 2 + [((8, KA, 256), f32)],
         [pltpu.VMEM((K * 16, 128), f32), pltpu.VMEM((8, 256), f32), pltpu.SemaphoreType.DMA((2,))],
-        anywhere,
-    )(rhs, areas)
+        [pl.BlockSpec(memory_space=pltpu.HBM)] * 2,
+    )(*(pltpu.with_memory_space_constraint(x, pltpu.HBM) for x in (rhs, areas)))
 
     def in_pairs(first, second, axis, count):
         second = lax.ppermute(second, axis, [(i, ((i + 1) ^ 1) - 1) for i in range(1, count - 1)])

time: 76.5 us -> 75.5 us (0.987)
  local copies, waits for them, and re-layouts: 1.74 us -> 0.01 us
  Pallas kernels: 10.9 us -> 11.7 us
    unnamed x6 -> x2, local copies, waits for them, and re-layouts: 1.74 us -> 0.01 us
    pallas_call x1, Pallas kernels: 0.25 us -> 1.25 us  [local(): call(pack_x, [((HX, KA, 256), f32)] * 2 + [((8, KA, 256), f32)], [pltpu.V...]
where the time goes in v6:
time: 75.5 us; the launch traced here: 75 us
  starting transfers between devices  40.4 us (54%)
  Pallas kernels  11.7 us (15%)
  waiting for transfers between devices  11.1 us (15%)
  blocking collectives  11.1 us (15%)
    all_to_all x2, starting transfers between devices, exchange(): lax.all_to_all(array, 'wide', 0, 0, tiled=True, axis_index_groups=groups)  20.6 us
    ppermute x3, starting transfers between devices, in_pairs(): lax.ppermute(first, axis, [(i, i ^ 1) for i in range(count)])  12.1 us
    all_to_all x1, blocking collectives, exchange(): lax.all_to_all(array, 'wide', 0, 0, tiled=True, axis_index_groups=groups)  11.1 us
    ppermute x3, starting transfers between devices, in_pairs(): lax.ppermute(second, axis, [(i, (i + 1 ^ 1) - 1) for i in range(1, count...  7.62 us
    all_to_all x2, waiting for transfers between devices, exchange(): lax.all_to_all(array, 'wide', 0, 0, tiled=True, axis_index_groups=groups)  5.8 us
    pallas_call x1, Pallas kernels, local(): call(after_scan, [((K * 16, 128), f32)] * 2, K4_SCRATCH, on_vmem(14))  4.77 us
    ppermute x3, waiting for transfers between devices, in_pairs(): lax.ppermute(first, axis, [(i, i ^ 1) for i in range(count)])  4.47 us
    pallas_call x1, Pallas kernels, local(): call(before_scan, K2_OUTS, K2_SCRATCH, on_vmem(9))  2.56 us
  transfers between devices with their start and end apart: 8, of which 6 were waited for; matrix products, arithmetic and copies ran while one was open for 0% of the time, Pallas kernels for 3%

profile of v6, /device:TPU:2, one launch (start us, length us, event | category | flops | bytes accessed | tf_op | source)
XLA Modules:
  0.0 75.0 jit_solution(5356778307689985932)
XLA Ops:
  0.6 1.2 %shard_map.50 = (f32[2,72,256]{2,1,0:T(8,128)S(1)}, f32[2,72,256]{2,1,0:T(8,128)S(1)}, f32[8,72,256]{2,1,0:T(8,128)S(1)}) custom-call(f32[1024,128]{1,0:T(8,128)} %bitcast.19, f32[8,256]{1,0:T(8,128)} %areas_hbm.1), custom_call_target="tpu_custom_call" | custom-call | tf_op jit(solution)/shard_map/pallas_call | solution.py:472
  1.9 0.0 copy-start
  1.9 3.5 %collective-permute-start = (f32[2,72,256]{2,1,0:T(8,128)S(1)}, f32[2,72,256]{2,1,0:T(8,128)S(1)}, u32[]{:S(2)}, u32[]{:S(2)}) collective-permute-start(f32[2,72,256]{2,1,0:T(8,128)S(1)} %get-tuple-element.24), channel_id=1, source_target_pairs={{4,8},{8,4},{12,16},{16,12},{20,24},{24,20},{28,32},{32,28},{36,40... | collective-permute-start | bytes 442376 | tf_op jit(solution)/shard_map/ppermute | solution.py:480
  5.4 3.3 %collective-permute-start.1 = (f32[2,72,256]{2,1,0:T(8,128)S(1)}, f32[2,72,256]{2,1,0:T(8,128)S(1)}, u32[]{:S(2)}, u32[]{:S(2)}) collective-permute-start(f32[2,72,256]{2,1,0:T(8,128)S(1)} %get-tuple-element.25), channel_id=1, source_target_pairs={{0,4},{4,0},{8,12},{12,8},{16,20},{20,16},{24,28},{28,24},{32,36},... | collective-permute-start | bytes 442376 | tf_op jit(solution)/shard_map/ppermute | solution.py:481
  8.7 0.0 copy-done
  8.7 0.8 %shard_map.51 = (bf16[64,192]{1,0:T(8,128)(2,1)S(1)}, bf16[64,192]{1,0:T(8,128)(2,1)S(1)}, f32[64,128]{1,0:T(8,128)S(1)}, f32[64,128]{1,0:T(8,128)S(1)}) custom-call(f32[64]{0:T(128)S(1)} %copy-done), custom_call_target="tpu_custom_call" | custom-call | tf_op jit(solution)/shard_map/pallas_call | solution.py:484
  9.5 0.8 %collective-permute-done.x_second_ref = f32[2,72,256]{2,1,0:T(8,128)S(1)} collective-permute-done((f32[2,72,256]{2,1,0:T(8,128)S(1)}, f32[2,72,256]{2,1,0:T(8,128)S(1)}, u32[]{:S(2)}, u32[]{:S(2)}) %collective-permute-start) | collective-permute-done | bytes 147488 | tf_op jit(solution)/shard_map/ppermute | solution.py:480
  10.4 3.1 %collective-permute-done.1.x_first_ref = f32[2,72,256]{2,1,0:T(8,128)S(1)} collective-permute-done((f32[2,72,256]{2,1,0:T(8,128)S(1)}, f32[2,72,256]{2,1,0:T(8,128)S(1)}, u32[]{:S(2)}, u32[]{:S(2)}) %collective-permute-start.1) | collective-permute-done | bytes 147488 | tf_op jit(solution)/shard_map/ppermute | solution.py:481
  13.4 0.3 shard_map.52
  13.7 0.7 collective-permute-start.2
  14.4 6.5 %collective-permute-start.3 = (f32[72,128]{1,0:T(8,128)S(1)}, f32[72,128]{1,0:T(8,128)S(1)}, u32[]{:S(2)}, u32[]{:S(2)}) collective-permute-start(f32[72,128]{1,0:T(8,128)S(1)} %get-tuple-element.30), channel_id=1, source_target_pairs={{0,1},{1,0},{2,3},{3,2},{4,5},{5,4},{6,7},{7,6},{8,9},{9,8},{10,11... | collective-permute-start | bytes 110600 | tf_op jit(solution)/shard_map/ppermute | solution.py:481
  20.9 0.3 shard_map.53.u1_ref
  21.2 0.0 collective-permute-done.2.second_ref.y_second_ref
  21.2 0.5 collective-permute-done.3.first_ref.y_first_ref
  21.7 2.6 %shard_map.54 = (f32[64,384]{1,0:T(8,128)S(1)}, f32[10,64,384]{2,1,0:T(8,128)S(1)}, f32[2,64,384]{2,1,0:T(8,128)S(1)}) custom-call(f32[8,72,256]{2,1,0:T(8,128)S(1)} %get-tuple-element.23.own_ref, f32[2,72,256]{2,1,0:T(8,128)S(1)} %get-tuple-element.27.left_ref, f32[2,72,256]{2,1,0:T(8,128)S(1)} %get-tuple-element.28.right_ref, ...), custom_call_target="tpu_custom_call" | custom-call | tf_op jit(solution)/shard_map/pallas_call | solution.py:495
  24.3 11.1 %all_to_all.15.blocks_ref = f32[8,8,384]{2,1,0:T(8,128)S(1)} all-to-all(f32[8,8,384]{2,1,0:T(8,128)S(1)} %bitcast.18), channel_id=1, replica_groups={{16,20,24,28,0,4,8,12},{48,52,56,60,32,36,40,44},{80,84,88,92,64,68,72,..., dimensions={0} | all-to-all | bytes 196608 | tf_op jit(solution)/shard_map/all_to_all | solution.py:505
  35.4 0.8 %shard_map.55 = f32[16,8,256]{2,1,0:T(8,128)} custom-call(f32[8,8,384]{2,1,0:T(8,128)S(1)} %all_to_all.15.blocks_ref, f32[64,128]{1,0:T(8,128)S(1)} %get-tuple-element.26._.retain_ref), custom_call_target="tpu_custom_call" | custom-call | tf_op jit(solution)/shard_map/pallas_call | solution.py:511
  36.1 16.4 %all-to-all-start.1 = ((f32[16,8,256]{2,1,0:T(8,128)}), f32[16,8,256]{2,1,0:T(8,128)S(1)}, u32[]{:S(2)}, u32[]{:S(2)}) async-start(f32[16,8,256]{2,1,0:T(8,128)} %shard_map.55), calls=%async_computation.1 | async-start | bytes 262144 | tf_op jit(solution)/shard_map/all_to_all | solution.py:505
  52.6 0.1 shard_map.57
  52.7 2.3 %collective-permute-start.4 = (f32[7,64,128]{2,1,0:T(8,128)S(1)}, f32[7,64,128]{2,1,0:T(8,128)S(1)}, u32[]{:S(2)}, u32[]{:S(2)}) collective-permute-start(f32[7,64,128]{2,1,0:T(8,128)S(1)} %get-tuple-element.39), channel_id=1, source_target_pairs={{0,4},{4,0},{8,12},{12,8},{16,20},{20,16},{24,28},{28,24},{32,36},... | collective-permute-start | bytes 688136 | tf_op jit(solution)/shard_map/ppermute | solution.py:481
  55.0 3.5 %collective-permute-start.5 = (f32[7,64,128]{2,1,0:T(8,128)S(1)}, f32[7,64,128]{2,1,0:T(8,128)S(1)}, u32[]{:S(2)}, u32[]{:S(2)}) collective-permute-start(f32[7,64,128]{2,1,0:T(8,128)S(1)} %get-tuple-element.40), channel_id=1, source_target_pairs={{4,8},{8,4},{12,16},{16,12},{20,24},{24,20},{28,32},{32,28},{36,40... | collective-permute-start | bytes 688136 | tf_op jit(solution)/shard_map/ppermute | solution.py:480
  58.5 1.6 %all-to-all-done.1.others_ref = f32[16,8,256]{2,1,0:T(8,128)S(1)} async-done(((f32[16,8,256]{2,1,0:T(8,128)}), f32[16,8,256]{2,1,0:T(8,128)S(1)}, u32[]{:S(2)}, u32[]{:S(2)}) %all-to-all-start.1) | async-done | bytes 131104 | tf_op jit(solution)/shard_map/all_to_all | solution.py:505
  60.2 0.8 %shard_map.56 = f32[8,8,384]{2,1,0:T(8,128)} custom-call(f32[8,8,384]{2,1,0:T(8,128)S(1)} %all_to_all.15.blocks_ref, f32[16,8,256]{2,1,0:T(8,128)S(1)} %all-to-all-done.1.others_ref, f32[64,128]{1,0:T(8,128)S(1)} %get-tuple-element.26._.retain_ref), custom_call_target="tpu_custom_call" | custom-call | tf_op jit(solution)/shard_map/pallas_call | solution.py:513
  60.9 4.2 %all-to-all-start.2 = ((f32[8,8,384]{2,1,0:T(8,128)}), f32[8,8,384]{2,1,0:T(8,128)S(1)}, u32[]{:S(2)}, u32[]{:S(2)}) async-start(f32[8,8,384]{2,1,0:T(8,128)} %shard_map.56), calls=%async_computation.2 | async-start | bytes 196608 | tf_op jit(solution)/shard_map/all_to_all | solution.py:505
  65.1 0.9 %collective-permute-done.4.deep_first_ref = f32[7,64,128]{2,1,0:T(8,128)S(1)} collective-permute-done((f32[7,64,128]{2,1,0:T(8,128)S(1)}, f32[7,64,128]{2,1,0:T(8,128)S(1)}, u32[]{:S(2)}, u32[]{:S(2)}) %collective-permute-start.4) | collective-permute-done | bytes 229408 | tf_op jit(solution)/shard_map/ppermute | solution.py:481
  66.1 0.0 collective-permute-done.5.deep_second_ref
  66.1 4.2 %all-to-all-done.2 = f32[8,8,384]{2,1,0:T(8,128)S(1)} async-done(((f32[8,8,384]{2,1,0:T(8,128)}), f32[8,8,384]{2,1,0:T(8,128)S(1)}, u32[]{:S(2)}, u32[]{:S(2)}) %all-to-all-start.2) | async-done | bytes 98336 | tf_op jit(solution)/shard_map/all_to_all | solution.py:505
  70.2 4.8 %shard_map.58 = (f32[1024,128]{1,0:T(8,128)}, f32[1024,128]{1,0:T(8,128)}) custom-call(f32[64,384]{1,0:T(8,128)S(1)} %bitcast.17, f32[8,72,256]{2,1,0:T(8,128)S(1)} %get-tuple-element.23.own_ref, f32[2,72,256]{2,1,0:T(8,128)S(1)} %get-tuple-element.27.left_ref, f32[2,72,256]{2,1,0:T(8,128)S(1)} %get-tuple-element.28.right_ref, ...), custom_call_target="tpu_custom_call" | custom-call | tf_op jit(solution)/shard_map/pallas_call | solution.py:517
Async XLA Ops:
  1.9 6.8 %copy-start = (f32[64]{0:T(128)S(1)}, f32[64]{0:T(128)}, u32[]{:S(2)}) copy-start(f32[64]{0:T(128)} %stiff_ref.1) | copy-start | bytes 772
  1.9 8.5 %collective-permute-start = (f32[2,72,256]{2,1,0:T(8,128)S(1)}, f32[2,72,256]{2,1,0:T(8,128)S(1)}, u32[]{:S(2)}, u32[]{:S(2)}) collective-permute-start(f32[2,72,256]{2,1,0:T(8,128)S(1)} %get-tuple-element.24), channel_id=1, source_target_pairs={{4,8},{8,4},{12,16},{16,12},{20,24},{24,20},{28,32},{32,28},{36,40... | collective-permute-start | bytes 442376 | tf_op jit(solution)/shard_map/ppermute | solution.py:480
  5.4 8.1 %collective-permute-start.1 = (f32[2,72,256]{2,1,0:T(8,128)S(1)}, f32[2,72,256]{2,1,0:T(8,128)S(1)}, u32[]{:S(2)}, u32[]{:S(2)}) collective-permute-start(f32[2,72,256]{2,1,0:T(8,128)S(1)} %get-tuple-element.25), channel_id=1, source_target_pairs={{0,4},{4,0},{8,12},{12,8},{16,20},{20,16},{24,28},{28,24},{32,36},... | collective-permute-start | bytes 442376 | tf_op jit(solution)/shard_map/ppermute | solution.py:481
  13.7 7.5 %collective-permute-start.2 = (f32[72,128]{1,0:T(8,128)S(1)}, f32[72,128]{1,0:T(8,128)S(1)}, u32[]{:S(2)}, u32[]{:S(2)}) collective-permute-start(f32[72,128]{1,0:T(8,128)S(1)} %get-tuple-element.29), channel_id=1, source_target_pairs={{1,2},{2,1},{5,6},{6,5},{9,10},{10,9},{13,14},{14,13},{17,18},{18,... | collective-permute-start | bytes 110600 | tf_op jit(solution)/shard_map/ppermute | solution.py:480
  14.4 7.3 %collective-permute-start.3 = (f32[72,128]{1,0:T(8,128)S(1)}, f32[72,128]{1,0:T(8,128)S(1)}, u32[]{:S(2)}, u32[]{:S(2)}) collective-permute-start(f32[72,128]{1,0:T(8,128)S(1)} %get-tuple-element.30), channel_id=1, source_target_pairs={{0,1},{1,0},{2,3},{3,2},{4,5},{5,4},{6,7},{7,6},{8,9},{9,8},{10,11... | collective-permute-start | bytes 110600 | tf_op jit(solution)/shard_map/ppermute | solution.py:481
  36.1 24.0 %all-to-all-start.1 = ((f32[16,8,256]{2,1,0:T(8,128)}), f32[16,8,256]{2,1,0:T(8,128)S(1)}, u32[]{:S(2)}, u32[]{:S(2)}) async-start(f32[16,8,256]{2,1,0:T(8,128)} %shard_map.55), calls=%async_computation.1 | async-start | bytes 262144 | tf_op jit(solution)/shard_map/all_to_all | solution.py:505
  52.7 13.4 %collective-permute-start.4 = (f32[7,64,128]{2,1,0:T(8,128)S(1)}, f32[7,64,128]{2,1,0:T(8,128)S(1)}, u32[]{:S(2)}, u32[]{:S(2)}) collective-permute-start(f32[7,64,128]{2,1,0:T(8,128)S(1)} %get-tuple-element.39), channel_id=1, source_target_pairs={{0,4},{4,0},{8,12},{12,8},{16,20},{20,16},{24,28},{28,24},{32,36},... | collective-permute-start | bytes 688136 | tf_op jit(solution)/shard_map/ppermute | solution.py:481
  55.0 11.0 %collective-permute-start.5 = (f32[7,64,128]{2,1,0:T(8,128)S(1)}, f32[7,64,128]{2,1,0:T(8,128)S(1)}, u32[]{:S(2)}, u32[]{:S(2)}) collective-permute-start(f32[7,64,128]{2,1,0:T(8,128)S(1)} %get-tuple-element.40), channel_id=1, source_target_pairs={{4,8},{8,4},{12,16},{16,12},{20,24},{24,20},{28,32},{32,28},{36,40... | collective-permute-start | bytes 688136 | tf_op jit(solution)/shard_map/ppermute | solution.py:480
  60.9 9.3 %all-to-all-start.2 = ((f32[8,8,384]{2,1,0:T(8,128)}), f32[8,8,384]{2,1,0:T(8,128)S(1)}, u32[]{:S(2)}, u32[]{:S(2)}) async-start(f32[8,8,384]{2,1,0:T(8,128)} %shard_map.56), calls=%async_computation.2 | async-start | bytes 196608 | tf_op jit(solution)/shard_map/all_to_all | solution.py:505

commit v7 on v6

--- a/solution.py
+++ b/solution.py
@@ -155,7 +155,7 @@
     )
 
 
-def pack_y(own_ref, x_second_ref, x_first_ref, _, first_ref, second_ref, left_ref, right_ref):
+def pack_y(own_ref, x_first_ref, x_second_ref, _, first_ref, second_ref, left_ref, right_ref):
     even = lax.rem(lax.axis_index("wide"), 2) == 0
     left_ref[...] = jnp.where(even, x_second_ref[...], x_first_ref[...])
     right_ref[...] = jnp.where(even, x_first_ref[...], x_second_ref[...])
@@ -489,7 +489,7 @@
     )(stiffness)
     first, second, left, right = call(
         pack_y, [((KA, 128), f32)] * 2 + [((HX, KA, 256), f32)] * 2, specs=on_vmem(4)
-    )(own, x_second, x_first, retain)
+    )(own, x_first, x_second, retain)
     first, second = in_pairs(first, second, "narrow", narrow)
     (u1,) = call(first_main, [((NR, K, 256), f32)], specs=on_vmem(4))(own, left, right, smooth)
     sent, u2, coarse = call(

time: 75.5 us -> 75.1 us (level)
  starting transfers between devices: 40.4 us -> 42.1 us
  waiting for transfers between devices: 11.1 us -> 9.48 us
    ppermute x3, starting transfers between devices: 7.62 us -> 11.9 us  [in_pairs(): lax.ppermute(second, axis, [(i, (i + 1 ^ 1) - 1) for i in range(1, count...]
    ppermute x3, waiting for transfers between devices: 4.47 us -> 1.41 us  [in_pairs(): lax.ppermute(first, axis, [(i, i ^ 1) for i in range(count)])]
    ppermute x3, starting transfers between devices: 12.1 us -> 9.28 us  [in_pairs(): lax.ppermute(first, axis, [(i, i ^ 1) for i in range(count)])]
    ppermute x3, waiting for transfers between devices: 0.85 us -> 2.27 us  [in_pairs(): lax.ppermute(second, axis, [(i, (i + 1 ^ 1) - 1) for i in range(1, count...]
  transfers between devices with their start and end apart: 8 -> 8, of which waited for: 6 -> 5; matrix products, arithmetic and copies ran while one was open for 0% -> 0% of each run, Pallas kernels for 3% -> 3%
where the time goes in v7:
time: 75.1 us; the launch traced here: 74.6 us
  starting transfers between devices  42.1 us (56%)
  Pallas kernels  11.7 us (16%)
  blocking collectives  10.5 us (14%)
  waiting for transfers between devices  9.48 us (13%)
    all_to_all x2, starting transfers between devices, exchange(): lax.all_to_all(array, 'wide', 0, 0, tiled=True, axis_index_groups=groups)  21 us
    ppermute x3, starting transfers between devices, in_pairs(): lax.ppermute(second, axis, [(i, (i + 1 ^ 1) - 1) for i in range(1, count...  11.9 us
    all_to_all x1, blocking collectives, exchange(): lax.all_to_all(array, 'wide', 0, 0, tiled=True, axis_index_groups=groups)  10.5 us
    ppermute x3, starting transfers between devices, in_pairs(): lax.ppermute(first, axis, [(i, i ^ 1) for i in range(count)])  9.28 us
    all_to_all x2, waiting for transfers between devices, exchange(): lax.all_to_all(array, 'wide', 0, 0, tiled=True, axis_index_groups=groups)  5.8 us
    pallas_call x1, Pallas kernels, local(): call(after_scan, [((K * 16, 128), f32)] * 2, K4_SCRATCH, on_vmem(14))  4.76 us
    pallas_call x1, Pallas kernels, local(): call(before_scan, K2_OUTS, K2_SCRATCH, on_vmem(9))  2.57 us
    ppermute x3, waiting for transfers between devices, in_pairs(): lax.ppermute(second, axis, [(i, (i + 1 ^ 1) - 1) for i in range(1, count...  2.27 us
  transfers between devices with their start and end apart: 8, of which 5 were waited for; matrix products, arithmetic and copies ran while one was open for 0% of the time, Pallas kernels for 3%

profile of v7, /device:TPU:2, one launch (start us, length us, event | category | flops | bytes accessed | tf_op | source)
XLA Modules:
  0.0 74.6 jit_solution(8678039180040917543)
XLA Ops:
  0.6 1.2 %shard_map.50 = (f32[2,72,256]{2,1,0:T(8,128)S(1)}, f32[2,72,256]{2,1,0:T(8,128)S(1)}, f32[8,72,256]{2,1,0:T(8,128)S(1)}) custom-call(f32[1024,128]{1,0:T(8,128)} %bitcast.19, f32[8,256]{1,0:T(8,128)} %areas_hbm.1), custom_call_target="tpu_custom_call" | custom-call | tf_op jit(solution)/shard_map/pallas_call | solution.py:472
  1.9 0.0 copy-start
  1.9 3.5 %collective-permute-start = (f32[2,72,256]{2,1,0:T(8,128)S(1)}, f32[2,72,256]{2,1,0:T(8,128)S(1)}, u32[]{:S(2)}, u32[]{:S(2)}) collective-permute-start(f32[2,72,256]{2,1,0:T(8,128)S(1)} %get-tuple-element.24), channel_id=1, source_target_pairs={{0,4},{4,0},{8,12},{12,8},{16,20},{20,16},{24,28},{28,24},{32,36},... | collective-permute-start | bytes 442376 | tf_op jit(solution)/shard_map/ppermute | solution.py:481
  5.4 7.7 %collective-permute-start.1 = (f32[2,72,256]{2,1,0:T(8,128)S(1)}, f32[2,72,256]{2,1,0:T(8,128)S(1)}, u32[]{:S(2)}, u32[]{:S(2)}) collective-permute-start(f32[2,72,256]{2,1,0:T(8,128)S(1)} %get-tuple-element.25), channel_id=1, source_target_pairs={{4,8},{8,4},{12,16},{16,12},{20,24},{24,20},{28,32},{32,28},{36,40... | collective-permute-start | bytes 442376 | tf_op jit(solution)/shard_map/ppermute | solution.py:480
  13.1 0.0 copy-done
  13.1 0.8 %shard_map.51 = (bf16[64,192]{1,0:T(8,128)(2,1)S(1)}, bf16[64,192]{1,0:T(8,128)(2,1)S(1)}, f32[64,128]{1,0:T(8,128)S(1)}, f32[64,128]{1,0:T(8,128)S(1)}) custom-call(f32[64]{0:T(128)S(1)} %copy-done), custom_call_target="tpu_custom_call" | custom-call | tf_op jit(solution)/shard_map/pallas_call | solution.py:484
  13.9 0.0 collective-permute-done.x_first_ref
  13.9 2.3 %collective-permute-done.1.x_second_ref = f32[2,72,256]{2,1,0:T(8,128)S(1)} collective-permute-done((f32[2,72,256]{2,1,0:T(8,128)S(1)}, f32[2,72,256]{2,1,0:T(8,128)S(1)}, u32[]{:S(2)}, u32[]{:S(2)}) %collective-permute-start.1) | collective-permute-done | bytes 147488 | tf_op jit(solution)/shard_map/ppermute | solution.py:480
  16.2 0.3 shard_map.52
  16.5 0.7 collective-permute-start.2
  17.2 3.5 %collective-permute-start.3 = (f32[72,128]{1,0:T(8,128)S(1)}, f32[72,128]{1,0:T(8,128)S(1)}, u32[]{:S(2)}, u32[]{:S(2)}) collective-permute-start(f32[72,128]{1,0:T(8,128)S(1)} %get-tuple-element.30), channel_id=1, source_target_pairs={{0,1},{1,0},{2,3},{3,2},{4,5},{5,4},{6,7},{7,6},{8,9},{9,8},{10,11... | collective-permute-start | bytes 110600 | tf_op jit(solution)/shard_map/ppermute | solution.py:481
  20.6 0.3 shard_map.53.u1_ref
  21.0 0.0 collective-permute-done.2.second_ref.y_second_ref
  21.0 0.5 collective-permute-done.3.first_ref.y_first_ref
  21.5 2.6 %shard_map.54 = (f32[64,384]{1,0:T(8,128)S(1)}, f32[10,64,384]{2,1,0:T(8,128)S(1)}, f32[2,64,384]{2,1,0:T(8,128)S(1)}) custom-call(f32[8,72,256]{2,1,0:T(8,128)S(1)} %get-tuple-element.23.own_ref, f32[2,72,256]{2,1,0:T(8,128)S(1)} %get-tuple-element.27.left_ref, f32[2,72,256]{2,1,0:T(8,128)S(1)} %get-tuple-element.28.right_ref, ...), custom_call_target="tpu_custom_call" | custom-call | tf_op jit(solution)/shard_map/pallas_call | solution.py:495
  24.1 10.5 %all_to_all.15.blocks_ref = f32[8,8,384]{2,1,0:T(8,128)S(1)} all-to-all(f32[8,8,384]{2,1,0:T(8,128)S(1)} %bitcast.18), channel_id=1, replica_groups={{16,20,24,28,0,4,8,12},{48,52,56,60,32,36,40,44},{80,84,88,92,64,68,72,..., dimensions={0} | all-to-all | bytes 196608 | tf_op jit(solution)/shard_map/all_to_all | solution.py:505
  34.6 0.8 %shard_map.55 = f32[16,8,256]{2,1,0:T(8,128)} custom-call(f32[8,8,384]{2,1,0:T(8,128)S(1)} %all_to_all.15.blocks_ref, f32[64,128]{1,0:T(8,128)S(1)} %get-tuple-element.26._.retain_ref), custom_call_target="tpu_custom_call" | custom-call | tf_op jit(solution)/shard_map/pallas_call | solution.py:511
  35.4 16.8 %all-to-all-start.1 = ((f32[16,8,256]{2,1,0:T(8,128)}), f32[16,8,256]{2,1,0:T(8,128)S(1)}, u32[]{:S(2)}, u32[]{:S(2)}) async-start(f32[16,8,256]{2,1,0:T(8,128)} %shard_map.55), calls=%async_computation.1 | async-start | bytes 262144 | tf_op jit(solution)/shard_map/all_to_all | solution.py:505
  52.1 0.1 shard_map.57
  52.3 2.3 %collective-permute-start.4 = (f32[7,64,128]{2,1,0:T(8,128)S(1)}, f32[7,64,128]{2,1,0:T(8,128)S(1)}, u32[]{:S(2)}, u32[]{:S(2)}) collective-permute-start(f32[7,64,128]{2,1,0:T(8,128)S(1)} %get-tuple-element.39), channel_id=1, source_target_pairs={{0,4},{4,0},{8,12},{12,8},{16,20},{20,16},{24,28},{28,24},{32,36},... | collective-permute-start | bytes 688136 | tf_op jit(solution)/shard_map/ppermute | solution.py:481
  54.6 3.5 %collective-permute-start.5 = (f32[7,64,128]{2,1,0:T(8,128)S(1)}, f32[7,64,128]{2,1,0:T(8,128)S(1)}, u32[]{:S(2)}, u32[]{:S(2)}) collective-permute-start(f32[7,64,128]{2,1,0:T(8,128)S(1)} %get-tuple-element.40), channel_id=1, source_target_pairs={{4,8},{8,4},{12,16},{16,12},{20,24},{24,20},{28,32},{32,28},{36,40... | collective-permute-start | bytes 688136 | tf_op jit(solution)/shard_map/ppermute | solution.py:480
  58.1 1.6 %all-to-all-done.1.others_ref = f32[16,8,256]{2,1,0:T(8,128)S(1)} async-done(((f32[16,8,256]{2,1,0:T(8,128)}), f32[16,8,256]{2,1,0:T(8,128)S(1)}, u32[]{:S(2)}, u32[]{:S(2)}) %all-to-all-start.1) | async-done | bytes 131104 | tf_op jit(solution)/shard_map/all_to_all | solution.py:505
  59.7 0.8 %shard_map.56 = f32[8,8,384]{2,1,0:T(8,128)} custom-call(f32[8,8,384]{2,1,0:T(8,128)S(1)} %all_to_all.15.blocks_ref, f32[16,8,256]{2,1,0:T(8,128)S(1)} %all-to-all-done.1.others_ref, f32[64,128]{1,0:T(8,128)S(1)} %get-tuple-element.26._.retain_ref), custom_call_target="tpu_custom_call" | custom-call | tf_op jit(solution)/shard_map/pallas_call | solution.py:513
  60.5 4.2 %all-to-all-start.2 = ((f32[8,8,384]{2,1,0:T(8,128)}), f32[8,8,384]{2,1,0:T(8,128)S(1)}, u32[]{:S(2)}, u32[]{:S(2)}) async-start(f32[8,8,384]{2,1,0:T(8,128)} %shard_map.56), calls=%async_computation.2 | async-start | bytes 196608 | tf_op jit(solution)/shard_map/all_to_all | solution.py:505
  64.7 0.9 %collective-permute-done.4.deep_first_ref = f32[7,64,128]{2,1,0:T(8,128)S(1)} collective-permute-done((f32[7,64,128]{2,1,0:T(8,128)S(1)}, f32[7,64,128]{2,1,0:T(8,128)S(1)}, u32[]{:S(2)}, u32[]{:S(2)}) %collective-permute-start.4) | collective-permute-done | bytes 229408 | tf_op jit(solution)/shard_map/ppermute | solution.py:481
  65.6 0.0 collective-permute-done.5.deep_second_ref
  65.6 4.2 %all-to-all-done.2 = f32[8,8,384]{2,1,0:T(8,128)S(1)} async-done(((f32[8,8,384]{2,1,0:T(8,128)}), f32[8,8,384]{2,1,0:T(8,128)S(1)}, u32[]{:S(2)}, u32[]{:S(2)}) %all-to-all-start.2) | async-done | bytes 98336 | tf_op jit(solution)/shard_map/all_to_all | solution.py:505
  69.8 4.8 %shard_map.58 = (f32[1024,128]{1,0:T(8,128)}, f32[1024,128]{1,0:T(8,128)}) custom-call(f32[64,384]{1,0:T(8,128)S(1)} %bitcast.17, f32[8,72,256]{2,1,0:T(8,128)S(1)} %get-tuple-element.23.own_ref, f32[2,72,256]{2,1,0:T(8,128)S(1)} %get-tuple-element.27.left_ref, f32[2,72,256]{2,1,0:T(8,128)S(1)} %get-tuple-element.28.right_ref, ...), custom_call_target="tpu_custom_call" | custom-call | tf_op jit(solution)/shard_map/pallas_call | solution.py:517
Async XLA Ops:
  1.9 11.2 %copy-start = (f32[64]{0:T(128)S(1)}, f32[64]{0:T(128)}, u32[]{:S(2)}) copy-start(f32[64]{0:T(128)} %stiff_ref.1) | copy-start | bytes 772
  1.9 12.0 %collective-permute-start = (f32[2,72,256]{2,1,0:T(8,128)S(1)}, f32[2,72,256]{2,1,0:T(8,128)S(1)}, u32[]{:S(2)}, u32[]{:S(2)}) collective-permute-start(f32[2,72,256]{2,1,0:T(8,128)S(1)} %get-tuple-element.24), channel_id=1, source_target_pairs={{0,4},{4,0},{8,12},{12,8},{16,20},{20,16},{24,28},{28,24},{32,36},... | collective-permute-start | bytes 442376 | tf_op jit(solution)/shard_map/ppermute | solution.py:481
  5.4 10.8 %collective-permute-start.1 = (f32[2,72,256]{2,1,0:T(8,128)S(1)}, f32[2,72,256]{2,1,0:T(8,128)S(1)}, u32[]{:S(2)}, u32[]{:S(2)}) collective-permute-start(f32[2,72,256]{2,1,0:T(8,128)S(1)} %get-tuple-element.25), channel_id=1, source_target_pairs={{4,8},{8,4},{12,16},{16,12},{20,24},{24,20},{28,32},{32,28},{36,40... | collective-permute-start | bytes 442376 | tf_op jit(solution)/shard_map/ppermute | solution.py:480
  16.5 4.5 %collective-permute-start.2 = (f32[72,128]{1,0:T(8,128)S(1)}, f32[72,128]{1,0:T(8,128)S(1)}, u32[]{:S(2)}, u32[]{:S(2)}) collective-permute-start(f32[72,128]{1,0:T(8,128)S(1)} %get-tuple-element.29), channel_id=1, source_target_pairs={{1,2},{2,1},{5,6},{6,5},{9,10},{10,9},{13,14},{14,13},{17,18},{18,... | collective-permute-start | bytes 110600 | tf_op jit(solution)/shard_map/ppermute | solution.py:480
  17.2 4.3 %collective-permute-start.3 = (f32[72,128]{1,0:T(8,128)S(1)}, f32[72,128]{1,0:T(8,128)S(1)}, u32[]{:S(2)}, u32[]{:S(2)}) collective-permute-start(f32[72,128]{1,0:T(8,128)S(1)} %get-tuple-element.30), channel_id=1, source_target_pairs={{0,1},{1,0},{2,3},{3,2},{4,5},{5,4},{6,7},{7,6},{8,9},{9,8},{10,11... | collective-permute-start | bytes 110600 | tf_op jit(solution)/shard_map/ppermute | solution.py:481
  35.4 24.4 %all-to-all-start.1 = ((f32[16,8,256]{2,1,0:T(8,128)}), f32[16,8,256]{2,1,0:T(8,128)S(1)}, u32[]{:S(2)}, u32[]{:S(2)}) async-start(f32[16,8,256]{2,1,0:T(8,128)} %shard_map.55), calls=%async_computation.1 | async-start | bytes 262144 | tf_op jit(solution)/shard_map/all_to_all | solution.py:505
  52.3 13.4 %collective-permute-start.4 = (f32[7,64,128]{2,1,0:T(8,128)S(1)}, f32[7,64,128]{2,1,0:T(8,128)S(1)}, u32[]{:S(2)}, u32[]{:S(2)}) collective-permute-start(f32[7,64,128]{2,1,0:T(8,128)S(1)} %get-tuple-element.39), channel_id=1, source_target_pairs={{0,4},{4,0},{8,12},{12,8},{16,20},{20,16},{24,28},{28,24},{32,36},... | collective-permute-start | bytes 688136 | tf_op jit(solution)/shard_map/ppermute | solution.py:481
  54.6 11.0 %collective-permute-start.5 = (f32[7,64,128]{2,1,0:T(8,128)S(1)}, f32[7,64,128]{2,1,0:T(8,128)S(1)}, u32[]{:S(2)}, u32[]{:S(2)}) collective-permute-start(f32[7,64,128]{2,1,0:T(8,128)S(1)} %get-tuple-element.40), channel_id=1, source_target_pairs={{4,8},{8,4},{12,16},{16,12},{20,24},{24,20},{28,32},{32,28},{36,40... | collective-permute-start | bytes 688136 | tf_op jit(solution)/shard_map/ppermute | solution.py:480
  60.5 9.3 %all-to-all-start.2 = ((f32[8,8,384]{2,1,0:T(8,128)}), f32[8,8,384]{2,1,0:T(8,128)S(1)}, u32[]{:S(2)}, u32[]{:S(2)}) async-start(f32[8,8,384]{2,1,0:T(8,128)} %shard_map.56), calls=%async_computation.2 | async-start | bytes 196608 | tf_op jit(solution)/shard_map/all_to_all | solution.py:505

commit v8 on v7

--- a/solution.py
+++ b/solution.py
@@ -238,7 +238,7 @@
 
 
 def before_scan(
-    own_ref, left_ref, right_ref, second_ref, first_ref, u1_ref, smooth_ref, vert_ref, retain_ref,
+    own_ref, left_ref, right_ref, first_ref, second_ref, u1_ref, smooth_ref, vert_ref, retain_ref,
     sent_ref, u2_ref, both_ref, tails_ref, fine, coarse_ref, u1,
 ):
     smooth = smooth_ref[...]
@@ -497,7 +497,7 @@
         K2_OUTS,
         K2_SCRATCH,
         on_vmem(9),
-    )(own, left, right, second, first, u1, smooth, vert, retain)
+    )(own, left, right, first, second, u1, smooth, vert, retain)
     in_plane = [[p * PLANE + (s + FIRST_M) % PLANE for s in range(PLANE)] for p in range(planes)]
     over_planes = [[(s + FIRST_Z) % planes * PLANE + m for s in range(planes)] for m in range(PLANE)]
 

time: 75.1 us -> 75.8 us (level)
  the two profiles are of different devices: /device:TPU:2 before, /device:TPU:18 now
where the time goes in v8:
time: 75.8 us; the launch traced here: 75.3 us
  starting transfers between devices  39.8 us (53%)
  waiting for transfers between devices  11.9 us (16%)
  Pallas kernels  11.7 us (15%)
  blocking collectives  11.2 us (15%)
    all_to_all x2, starting transfers between devices, exchange(): lax.all_to_all(array, 'wide', 0, 0, tiled=True, axis_index_groups=groups)  20.9 us
    ppermute x3, starting transfers between devices, in_pairs(): lax.ppermute(second, axis, [(i, (i + 1 ^ 1) - 1) for i in range(1, count...  11.5 us
    all_to_all x1, blocking collectives, exchange(): lax.all_to_all(array, 'wide', 0, 0, tiled=True, axis_index_groups=groups)  11.2 us
    ppermute x3, starting transfers between devices, in_pairs(): lax.ppermute(first, axis, [(i, i ^ 1) for i in range(count)])  7.45 us
    all_to_all x2, waiting for transfers between devices, exchange(): lax.all_to_all(array, 'wide', 0, 0, tiled=True, axis_index_groups=groups)  5.94 us
    ppermute x3, waiting for transfers between devices, in_pairs(): lax.ppermute(second, axis, [(i, (i + 1 ^ 1) - 1) for i in range(1, count...  5.1 us
    pallas_call x1, Pallas kernels, local(): call(after_scan, [((K * 16, 128), f32)] * 2, K4_SCRATCH, on_vmem(14))  4.77 us
    pallas_call x1, Pallas kernels, local(): call(before_scan, K2_OUTS, K2_SCRATCH, on_vmem(9))  2.57 us
  transfers between devices with their start and end apart: 8, of which 5 were waited for; matrix products, arithmetic and copies ran while one was open for 0% of the time, Pallas kernels for 3%

profile of v8, /device:TPU:18, one launch (start us, length us, event | category | flops | bytes accessed | tf_op | source)
XLA Modules:
  0.0 75.3 jit_solution(1947337564158634386)
XLA Ops:
  0.6 1.2 %shard_map.50 = (f32[2,72,256]{2,1,0:T(8,128)S(1)}, f32[2,72,256]{2,1,0:T(8,128)S(1)}, f32[8,72,256]{2,1,0:T(8,128)S(1)}) custom-call(f32[1024,128]{1,0:T(8,128)} %bitcast.19, f32[8,256]{1,0:T(8,128)} %areas_hbm.1), custom_call_target="tpu_custom_call" | custom-call | tf_op jit(solution)/shard_map/pallas_call | solution.py:472
  1.9 0.0 copy-start
  1.9 3.2 %collective-permute-start = (f32[2,72,256]{2,1,0:T(8,128)S(1)}, f32[2,72,256]{2,1,0:T(8,128)S(1)}, u32[]{:S(2)}, u32[]{:S(2)}) collective-permute-start(f32[2,72,256]{2,1,0:T(8,128)S(1)} %get-tuple-element.24), channel_id=1, source_target_pairs={{0,4},{4,0},{8,12},{12,8},{16,20},{20,16},{24,28},{28,24},{32,36},... | collective-permute-start | bytes 442376 | tf_op jit(solution)/shard_map/ppermute | solution.py:481
  5.1 2.6 %collective-permute-start.1 = (f32[2,72,256]{2,1,0:T(8,128)S(1)}, f32[2,72,256]{2,1,0:T(8,128)S(1)}, u32[]{:S(2)}, u32[]{:S(2)}) collective-permute-start(f32[2,72,256]{2,1,0:T(8,128)S(1)} %get-tuple-element.25), channel_id=1, source_target_pairs={{4,8},{8,4},{12,16},{16,12},{20,24},{24,20},{28,32},{32,28},{36,40... | collective-permute-start | bytes 442376 | tf_op jit(solution)/shard_map/ppermute | solution.py:480
  7.7 0.0 copy-done
  7.7 0.8 %shard_map.51 = (bf16[64,192]{1,0:T(8,128)(2,1)S(1)}, bf16[64,192]{1,0:T(8,128)(2,1)S(1)}, f32[64,128]{1,0:T(8,128)S(1)}, f32[64,128]{1,0:T(8,128)S(1)}) custom-call(f32[64]{0:T(128)S(1)} %copy-done), custom_call_target="tpu_custom_call" | custom-call | tf_op jit(solution)/shard_map/pallas_call | solution.py:484
  8.6 0.8 %collective-permute-done.x_first_ref = f32[2,72,256]{2,1,0:T(8,128)S(1)} collective-permute-done((f32[2,72,256]{2,1,0:T(8,128)S(1)}, f32[2,72,256]{2,1,0:T(8,128)S(1)}, u32[]{:S(2)}, u32[]{:S(2)}) %collective-permute-start) | collective-permute-done | bytes 147488 | tf_op jit(solution)/shard_map/ppermute | solution.py:481
  9.4 3.8 %collective-permute-done.1.x_second_ref = f32[2,72,256]{2,1,0:T(8,128)S(1)} collective-permute-done((f32[2,72,256]{2,1,0:T(8,128)S(1)}, f32[2,72,256]{2,1,0:T(8,128)S(1)}, u32[]{:S(2)}, u32[]{:S(2)}) %collective-permute-start.1) | collective-permute-done | bytes 147488 | tf_op jit(solution)/shard_map/ppermute | solution.py:480
  13.2 0.3 shard_map.52
  13.5 1.9 %collective-permute-start.2 = (f32[72,128]{1,0:T(8,128)S(1)}, f32[72,128]{1,0:T(8,128)S(1)}, u32[]{:S(2)}, u32[]{:S(2)}) collective-permute-start(f32[72,128]{1,0:T(8,128)S(1)} %get-tuple-element.29), channel_id=1, source_target_pairs={{0,1},{1,0},{2,3},{3,2},{4,5},{5,4},{6,7},{7,6},{8,9},{9,8},{10,11... | collective-permute-start | bytes 110600 | tf_op jit(solution)/shard_map/ppermute | solution.py:481
  15.4 5.4 %collective-permute-start.3 = (f32[72,128]{1,0:T(8,128)S(1)}, f32[72,128]{1,0:T(8,128)S(1)}, u32[]{:S(2)}, u32[]{:S(2)}) collective-permute-start(f32[72,128]{1,0:T(8,128)S(1)} %get-tuple-element.30), channel_id=1, source_target_pairs={{1,2},{2,1},{5,6},{6,5},{9,10},{10,9},{13,14},{14,13},{17,18},{18,... | collective-permute-start | bytes 110600 | tf_op jit(solution)/shard_map/ppermute | solution.py:480
  20.8 0.3 shard_map.53.u1_ref
  21.1 0.0 collective-permute-done.2.first_ref.y_first_ref
  21.1 1.3 %collective-permute-done.3.second_ref.y_second_ref = f32[72,128]{1,0:T(8,128)S(1)} collective-permute-done((f32[72,128]{1,0:T(8,128)S(1)}, f32[72,128]{1,0:T(8,128)S(1)}, u32[]{:S(2)}, u32[]{:S(2)}) %collective-permute-start.3) | collective-permute-done | bytes 36896 | tf_op jit(solution)/shard_map/ppermute | solution.py:480
  22.4 2.6 %shard_map.54 = (f32[64,384]{1,0:T(8,128)S(1)}, f32[10,64,384]{2,1,0:T(8,128)S(1)}, f32[2,64,384]{2,1,0:T(8,128)S(1)}) custom-call(f32[8,72,256]{2,1,0:T(8,128)S(1)} %get-tuple-element.23.own_ref, f32[2,72,256]{2,1,0:T(8,128)S(1)} %get-tuple-element.27.left_ref, f32[2,72,256]{2,1,0:T(8,128)S(1)} %get-tuple-element.28.right_ref, ...), custom_call_target="tpu_custom_call" | custom-call | tf_op jit(solution)/shard_map/pallas_call | solution.py:495
  25.0 11.2 %all_to_all.15.blocks_ref = f32[8,8,384]{2,1,0:T(8,128)S(1)} all-to-all(f32[8,8,384]{2,1,0:T(8,128)S(1)} %bitcast.18), channel_id=1, replica_groups={{16,20,24,28,0,4,8,12},{48,52,56,60,32,36,40,44},{80,84,88,92,64,68,72,..., dimensions={0} | all-to-all | bytes 196608 | tf_op jit(solution)/shard_map/all_to_all | solution.py:505
  36.1 0.8 shard_map.55
  36.9 16.4 %all-to-all-start.1 = ((f32[16,8,256]{2,1,0:T(8,128)}), f32[16,8,256]{2,1,0:T(8,128)S(1)}, u32[]{:S(2)}, u32[]{:S(2)}) async-start(f32[16,8,256]{2,1,0:T(8,128)} %shard_map.55), calls=%async_computation.1 | async-start | bytes 262144 | tf_op jit(solution)/shard_map/all_to_all | solution.py:505
  53.3 0.1 shard_map.57
  53.4 2.3 %collective-permute-start.4 = (f32[7,64,128]{2,1,0:T(8,128)S(1)}, f32[7,64,128]{2,1,0:T(8,128)S(1)}, u32[]{:S(2)}, u32[]{:S(2)}) collective-permute-start(f32[7,64,128]{2,1,0:T(8,128)S(1)} %get-tuple-element.39), channel_id=1, source_target_pairs={{0,4},{4,0},{8,12},{12,8},{16,20},{20,16},{24,28},{28,24},{32,36},... | collective-permute-start | bytes 688136 | tf_op jit(solution)/shard_map/ppermute | solution.py:481
  55.8 3.5 %collective-permute-start.5 = (f32[7,64,128]{2,1,0:T(8,128)S(1)}, f32[7,64,128]{2,1,0:T(8,128)S(1)}, u32[]{:S(2)}, u32[]{:S(2)}) collective-permute-start(f32[7,64,128]{2,1,0:T(8,128)S(1)} %get-tuple-element.40), channel_id=1, source_target_pairs={{4,8},{8,4},{12,16},{16,12},{20,24},{24,20},{28,32},{32,28},{36,40... | collective-permute-start | bytes 688136 | tf_op jit(solution)/shard_map/ppermute | solution.py:480
  59.3 0.9 %all-to-all-done.1.others_ref = f32[16,8,256]{2,1,0:T(8,128)S(1)} async-done(((f32[16,8,256]{2,1,0:T(8,128)}), f32[16,8,256]{2,1,0:T(8,128)S(1)}, u32[]{:S(2)}, u32[]{:S(2)}) %all-to-all-start.1) | async-done | bytes 131104 | tf_op jit(solution)/shard_map/all_to_all | solution.py:505
  60.1 0.8 %shard_map.56 = f32[8,8,384]{2,1,0:T(8,128)} custom-call(f32[8,8,384]{2,1,0:T(8,128)S(1)} %all_to_all.15.blocks_ref, f32[16,8,256]{2,1,0:T(8,128)S(1)} %all-to-all-done.1.others_ref, f32[64,128]{1,0:T(8,128)S(1)} %get-tuple-element.26._.retain_ref), custom_call_target="tpu_custom_call" | custom-call | tf_op jit(solution)/shard_map/pallas_call | solution.py:513
  60.9 4.5 %all-to-all-start.2 = ((f32[8,8,384]{2,1,0:T(8,128)}), f32[8,8,384]{2,1,0:T(8,128)S(1)}, u32[]{:S(2)}, u32[]{:S(2)}) async-start(f32[8,8,384]{2,1,0:T(8,128)} %shard_map.56), calls=%async_computation.2 | async-start | bytes 196608 | tf_op jit(solution)/shard_map/all_to_all | solution.py:505
  65.4 0.0 collective-permute-done.4.deep_first_ref
  65.4 0.0 collective-permute-done.5.deep_second_ref
  65.4 5.1 %all-to-all-done.2 = f32[8,8,384]{2,1,0:T(8,128)S(1)} async-done(((f32[8,8,384]{2,1,0:T(8,128)}), f32[8,8,384]{2,1,0:T(8,128)S(1)}, u32[]{:S(2)}, u32[]{:S(2)}) %all-to-all-start.2) | async-done | bytes 98336 | tf_op jit(solution)/shard_map/all_to_all | solution.py:505
  70.5 4.8 %shard_map.58 = (f32[1024,128]{1,0:T(8,128)}, f32[1024,128]{1,0:T(8,128)}) custom-call(f32[64,384]{1,0:T(8,128)S(1)} %bitcast.17, f32[8,72,256]{2,1,0:T(8,128)S(1)} %get-tuple-element.23.own_ref, f32[2,72,256]{2,1,0:T(8,128)S(1)} %get-tuple-element.27.left_ref, f32[2,72,256]{2,1,0:T(8,128)S(1)} %get-tuple-element.28.right_ref, ...), custom_call_target="tpu_custom_call" | custom-call | tf_op jit(solution)/shard_map/pallas_call | solution.py:517
Async XLA Ops:
  1.9 5.8 %copy-start = (f32[64]{0:T(128)S(1)}, f32[64]{0:T(128)}, u32[]{:S(2)}) copy-start(f32[64]{0:T(128)} %stiff_ref.1) | copy-start | bytes 772
  1.9 7.5 %collective-permute-start = (f32[2,72,256]{2,1,0:T(8,128)S(1)}, f32[2,72,256]{2,1,0:T(8,128)S(1)}, u32[]{:S(2)}, u32[]{:S(2)}) collective-permute-start(f32[2,72,256]{2,1,0:T(8,128)S(1)} %get-tuple-element.24), channel_id=1, source_target_pairs={{0,4},{4,0},{8,12},{12,8},{16,20},{20,16},{24,28},{28,24},{32,36},... | collective-permute-start | bytes 442376 | tf_op jit(solution)/shard_map/ppermute | solution.py:481
  5.1 8.1 %collective-permute-start.1 = (f32[2,72,256]{2,1,0:T(8,128)S(1)}, f32[2,72,256]{2,1,0:T(8,128)S(1)}, u32[]{:S(2)}, u32[]{:S(2)}) collective-permute-start(f32[2,72,256]{2,1,0:T(8,128)S(1)} %get-tuple-element.25), channel_id=1, source_target_pairs={{4,8},{8,4},{12,16},{16,12},{20,24},{24,20},{28,32},{32,28},{36,40... | collective-permute-start | bytes 442376 | tf_op jit(solution)/shard_map/ppermute | solution.py:480
  13.5 7.6 %collective-permute-start.2 = (f32[72,128]{1,0:T(8,128)S(1)}, f32[72,128]{1,0:T(8,128)S(1)}, u32[]{:S(2)}, u32[]{:S(2)}) collective-permute-start(f32[72,128]{1,0:T(8,128)S(1)} %get-tuple-element.29), channel_id=1, source_target_pairs={{0,1},{1,0},{2,3},{3,2},{4,5},{5,4},{6,7},{7,6},{8,9},{9,8},{10,11... | collective-permute-start | bytes 110600 | tf_op jit(solution)/shard_map/ppermute | solution.py:481
  15.4 7.0 %collective-permute-start.3 = (f32[72,128]{1,0:T(8,128)S(1)}, f32[72,128]{1,0:T(8,128)S(1)}, u32[]{:S(2)}, u32[]{:S(2)}) collective-permute-start(f32[72,128]{1,0:T(8,128)S(1)} %get-tuple-element.30), channel_id=1, source_target_pairs={{1,2},{2,1},{5,6},{6,5},{9,10},{10,9},{13,14},{14,13},{17,18},{18,... | collective-permute-start | bytes 110600 | tf_op jit(solution)/shard_map/ppermute | solution.py:480
  36.9 23.2 %all-to-all-start.1 = ((f32[16,8,256]{2,1,0:T(8,128)}), f32[16,8,256]{2,1,0:T(8,128)S(1)}, u32[]{:S(2)}, u32[]{:S(2)}) async-start(f32[16,8,256]{2,1,0:T(8,128)} %shard_map.55), calls=%async_computation.1 | async-start | bytes 262144 | tf_op jit(solution)/shard_map/all_to_all | solution.py:505
  53.4 12.0 %collective-permute-start.4 = (f32[7,64,128]{2,1,0:T(8,128)S(1)}, f32[7,64,128]{2,1,0:T(8,128)S(1)}, u32[]{:S(2)}, u32[]{:S(2)}) collective-permute-start(f32[7,64,128]{2,1,0:T(8,128)S(1)} %get-tuple-element.39), channel_id=1, source_target_pairs={{0,4},{4,0},{8,12},{12,8},{16,20},{20,16},{24,28},{28,24},{32,36},... | collective-permute-start | bytes 688136 | tf_op jit(solution)/shard_map/ppermute | solution.py:481
  55.8 9.6 %collective-permute-start.5 = (f32[7,64,128]{2,1,0:T(8,128)S(1)}, f32[7,64,128]{2,1,0:T(8,128)S(1)}, u32[]{:S(2)}, u32[]{:S(2)}) collective-permute-start(f32[7,64,128]{2,1,0:T(8,128)S(1)} %get-tuple-element.40), channel_id=1, source_target_pairs={{4,8},{8,4},{12,16},{16,12},{20,24},{24,20},{28,32},{32,28},{36,40... | collective-permute-start | bytes 688136 | tf_op jit(solution)/shard_map/ppermute | solution.py:480
  60.9 9.6 %all-to-all-start.2 = ((f32[8,8,384]{2,1,0:T(8,128)}), f32[8,8,384]{2,1,0:T(8,128)S(1)}, u32[]{:S(2)}, u32[]{:S(2)}) async-start(f32[8,8,384]{2,1,0:T(8,128)} %shard_map.56), calls=%async_computation.2 | async-start | bytes 196608 | tf_op jit(solution)/shard_map/all_to_all | solution.py:505
